TPU v7x, 32 devices: a whole 2x2x4 slice. The times are simulated.
32 devices in a mesh: sess: 2 (over x), ctx: 16 (over z, y, core).
Axes of the slice: x: 2, y: 2, z: 4, core: 2. Of those that a mesh axis runs over, the one named last changes fastest.
Arguments:
- mamba_input: bfloat16 [2, 2048, 8192], P('sess', 'ctx'), may hold values from -6 to 6
- step_size: bfloat16 [2, 2048, 64], P('sess', 'ctx'), may hold values from 0.19921875 to 1.5
- decay_log: bfloat16 [2, 2048, 64], P('sess', 'ctx'), may hold values from -0.8 to 0
- state_write: bfloat16 [2, 2048, 512], P('sess', 'ctx'), may hold values from -0.375 to 0.375
- state_read: bfloat16 [2, 2048, 512], P('sess', 'ctx'), may hold values from -0.75 to 0.75
- skip_gain: float32 [64], replicated, may hold values from 0.1 to 1.9
- saved_states: float32 [2, 3, 64, 8192], P('sess', None, 'ctx'), may hold values from -6 to 6
- home_slot: int32 [6], replicated, may hold values from 0 to 5, each once
- turn_lengths: int32 [2, 3], P('sess'), may hold values from 1 to 1024, 2048 in all within a row
- history_lengths: int32 [2, 3], P('sess'), may hold values from 4 to 1023
- queries: bfloat16 [2, 2048, 4096], P('sess', 'ctx'), may hold values from -150 to 150
- turn_keys: bfloat16 [2, 2048, 512], P('sess', 'ctx'), may hold values from -6 to 6
- turn_values: bfloat16 [2, 2048, 512], P('sess', 'ctx'), may hold values from -6 to 6
- cache_keys: bfloat16 [2, 3, 512, 512], P('sess', None, 'ctx'), may hold values from -6 to 6
- cache_values: bfloat16 [2, 3, 512, 512], P('sess', None, 'ctx'), may hold values from -6 to 6
- sink_keys: bfloat16 [2, 3, 4, 512], P('sess'), may hold values from -12 to 12
- sink_values: bfloat16 [2, 3, 4, 512], P('sess'), may hold values from -6 to 6
Outputs:
- mixed: bfloat16 [2, 2048, 8192], P('sess', 'ctx')
- attended: bfloat16 [2, 2048, 4096], P('sess', 'ctx')
Inputs may be any that keep to these rules, and one draw needn't show every extreme that they name: `home_slot`: entry g * 3 + s names the stored state, in the group-major list of saved_states, from which session s of group g resumes.
All inputs are finite; a program needn't handle non-finite values.
Results may differ from a plain program's by a relative error of at most 0.004.
Values may be sent and summed in bfloat16 or wider, within the bound.
No kernel may reach another device: no remote copies, remote signals or barrier semaphores. Data moves between devices by JAX's collectives and lax.ppermute only.
A program may use at most 256 MiB of HBM per device.

v0:
```python
import math

import jax
import jax.numpy as jnp
from jax import lax
from jax.experimental import pallas as pl
from jax.experimental.pallas import tpu as pltpu
from jax.sharding import PartitionSpec as P

REACH = 4
SEQS = 3
SINKS = 4
H = 64
P_SIZE = 128
N = 64
G = 8
QH = 32
KVH = 4
HD = 128
WINDOW = 512
TOK = 128

HEADS_PER = H // G
PAIR = 2 * HEADS_PER
STEPS = H // PAIR
EXTRA = 16
BLOCK = 64
SPAN = WINDOW + BLOCK
COLUMNS = SPAN + 64
NEG = -1e30
TOKEN = jax.ShapeDtypeStruct((8, 128), jnp.float32)
SHORT = pl.CostEstimate(flops=1024, bytes_accessed=1024, transcendentals=0)
LONG = pl.CostEstimate(flops=1 << 35, bytes_accessed=1 << 20, transcendentals=0)


class Scalars:
    def __init__(self, ids):
        self.place, self.group = ids[0], ids[1]
        self.one = ids[2]
        self.two = ids[2] + ids[3]
        self.ids = ids
        self.even = self.place % 2 == 0

    def history(self, session):
        return self.ids[2 + SEQS + session]

    def home(self, number):
        return self.ids[2 + 2 * SEQS + number]

    def session_at(self, position):
        return (position >= self.one).astype(jnp.int32) + (position >= self.two).astype(jnp.int32)

    def start_of(self, session):
        return jnp.where(session == 0, 0, jnp.where(session == 1, self.one, self.two))

    def last_start(self):
        first = self.place * TOK
        return jnp.maximum(self.start_of(self.session_at(first + TOK - 1)) - first, 0)


def scalars(kernel, *options):
    def body(ids, *refs):
        kernel(*options, Scalars(ids), *refs)

    return body


def params(mib=60):
    return pltpu.CompilerParams(vmem_limit_bytes=mib * 1024 * 1024)


def running_rows(dl_ref):
    k = lax.broadcasted_iota(jnp.int32, (TOK, TOK), 0)
    u = lax.broadcasted_iota(jnp.int32, (TOK, TOK), 1)
    upto = (k <= u).astype(jnp.bfloat16)
    running = jnp.dot(dl_ref[...], upto, preferred_element_type=jnp.float32)
    return dl_ref[...].astype(jnp.float32), running


def summary_kernel(
    local, meta, x_ref, dl_ref, step_ref, write_ref, keep_ref, send_ref, coef_s, factor_s, write_s
):
    step = pl.program_id(0)

    @pl.when(step == 0)
    def _():
        rates, running = running_rows(dl_ref)
        steps = step_ref[...].astype(jnp.float32)
        r = meta.last_start()
        lane = lax.broadcasted_iota(jnp.int32, (H, TOK), 1)
        last = running[:, TOK - 1 :]
        base = jnp.sum(jnp.where(lane < r, rates, 0.0), axis=1, keepdims=True)
        coef_s[...] = jnp.where(lane >= r, jnp.exp(last - running) * steps, 0.0)
        factor_s[...] = jnp.broadcast_to(jnp.exp(last - base), (H, TOK))
        write_s[...] = write_ref[...].astype(jnp.float32).T

    even = meta.even
    coef = coef_s[pl.ds(pl.multiple_of(step * PAIR, PAIR), PAIR), :]
    factor = factor_s[pl.ds(pl.multiple_of(step * PAIR, PAIR), PAIR), :]
    writes = write_s[pl.ds(pl.multiple_of(step * 2 * N, 2 * N), 2 * N), :]

    def summary(k):
        group = k // HEADS_PER
        loading = (writes[group * N : (group + 1) * N] * coef[k : k + 1]).astype(jnp.bfloat16)
        return jnp.dot(
            loading, x_ref[:, k * P_SIZE : (k + 1) * P_SIZE], preferred_element_type=jnp.float32
        )

    for chip in range(PAIR // (2 * local)):
        low, high = 2 * local * chip, 2 * local * chip + local
        for k in range(local):
            first, second = summary(low + k), summary(high + k)
            rows = slice(k * N, (k + 1) * N)
            keep_ref[chip, rows, :] = jnp.where(even, first, second).astype(jnp.bfloat16)
            send_ref[chip, rows, :] = jnp.where(even, second, first).astype(jnp.bfloat16)
        first, second = factor[low : low + local], factor[high : high + local]
        keep_ref[chip, local * N :, :] = factor_rows(jnp.where(even, first, second))
        send_ref[chip, local * N :, :] = factor_rows(jnp.where(even, second, first))


def factor_rows(rows):
    high = rows.astype(jnp.bfloat16).astype(jnp.float32)
    parts = [high, rows - high]
    if EXTRA > 2 * rows.shape[0]:
        parts.append(jnp.zeros((EXTRA - 2 * rows.shape[0], TOK), jnp.float32))
    return jnp.concatenate(parts, axis=0).astype(jnp.bfloat16)


def factors_of(block, local):
    block = block.astype(jnp.float32)
    return block[:local] + block[local : 2 * local]


def summaries(meta, x, rates, steps, writes, local):
    chips = H // (2 * local)
    rows = local * N + EXTRA
    shape = jax.ShapeDtypeStruct((chips, rows, P_SIZE), jnp.bfloat16)
    spec = pl.BlockSpec((PAIR // (2 * local), rows, P_SIZE), lambda i, *m: (i, 0, 0))
    return pl.pallas_call(
        scalars(summary_kernel, local),
        out_shape=[shape, shape],
        grid_spec=pltpu.PrefetchScalarGridSpec(
            num_scalar_prefetch=1,
            grid=(STEPS,),
            in_specs=[
                pl.BlockSpec((TOK, PAIR * P_SIZE), lambda i, *m: (0, i)),
                pl.BlockSpec((H, TOK), lambda i, *m: (0, 0)),
                pl.BlockSpec((H, TOK), lambda i, *m: (0, 0)),
                pl.BlockSpec((TOK, G * N), lambda i, *m: (0, 0)),
            ],
            out_specs=[spec, spec],
            scratch_shapes=[
                pltpu.VMEM((H, TOK), jnp.float32),
                pltpu.VMEM((H, TOK), jnp.float32),
                pltpu.VMEM((G * N, TOK), jnp.float32),
            ],
        ),
        compiler_params=params(),
        cost_estimate=LONG,
        name="summaries",
    )(meta, x, rates, steps, writes)


def idle_spec(array):
    return pl.BlockSpec(memory_space=pl.ANY)


def whole(kernel, name, meta, arrays, shapes, idle=(), mib=16, scratch=()):
    def spec(shape):
        return pl.BlockSpec(shape, lambda i, *m: (0,) * len(shape))

    return pl.pallas_call(
        kernel,
        out_shape=[jax.ShapeDtypeStruct(s, t) for s, t in shapes],
        grid_spec=pltpu.PrefetchScalarGridSpec(
            num_scalar_prefetch=1,
            grid=(1,),
            in_specs=[spec(a.shape) for a in arrays] + [idle_spec(a) for a in idle],
            out_specs=[spec(s) for s, _ in shapes],
            scratch_shapes=scratch,
        ),
        compiler_params=params(mib),
        cost_estimate=LONG,
        name=name,
    )(meta, *arrays, *idle)


def restore_kernel(local, half, groups, meta, *refs):
    stored, (keys_ref, values_ref, turn_keys_ref, turn_values_ref) = refs[:groups], refs[groups : groups + 4]
    home_ref, away_ref, band_ref, restored_ref = refs[-4:]
    band_ref[0] = turn_keys_ref[...]
    band_ref[1] = turn_values_ref[...]
    for s in range(SEQS):
        slot = meta.home(meta.group * SEQS + s)
        source = (slot // SEQS - meta.group + groups) % groups
        for k in range(local):
            state = stored[0][slot % SEQS, k]
            for j in range(1, groups):
                state = jnp.where(source == j, stored[j][slot % SEQS, k], state)
            restored_ref[s, k * N : (k + 1) * N, :] = state.T
    rows = keys_ref.shape[1]
    upper = (meta.place >= half).astype(jnp.int32)
    for out_ref, first in ((home_ref, upper), (away_ref, 1 - upper)):
        for which, ref in enumerate((keys_ref, values_ref)):
            for s in range(2):
                for j in range(KVH):
                    place = ((which * 2 + s) * KVH + j) * rows
                    out_ref[0, place : place + rows, :] = ref[first + s, :, j * HD : (j + 1) * HD]
        out_ref[0, 4 * KVH * rows :, :] = restored_ref[first + 1].astype(jnp.bfloat16)


def copy_kernel(meta, array_ref, *refs):
    refs[-1][...] = array_ref[...]


def join_kernel(meta, first_ref, second_ref, *refs):
    out_ref = refs[-1]
    count = first_ref.shape[0]
    out_ref[:count] = first_ref[...]
    out_ref[count:] = second_ref[...]


def join_two_kernel(meta, first_ref, second_ref, key_value_ref, four_ref, *refs):
    out_ref, two_ref = refs[-2:]
    count = first_ref.shape[0]
    out_ref[:count] = first_ref[...]
    out_ref[count:] = second_ref[...]
    two_ref[...] = jnp.where(meta.place // 2 % 2 == 0, key_value_ref[...], four_ref[...])


def far_place(distance, bits):
    place = distance * 0
    for k in range(bits):
        place = place + ((distance // (1 << k)) % 2) * (1 << (bits - 1 - k))
    return place


def combine_kernel(local, meta, keep_ref, got_ref, *refs):
    out_ref = refs[-1]
    even = meta.even
    second = (meta.place // 2 * 2 + 1) * TOK
    closes = meta.start_of(meta.session_at(second + TOK - 1)) >= second
    width = local * N
    for chip in range(keep_ref.shape[0]):
        keep = factors_of(keep_ref[chip, width:, :], local)
        got = factors_of(got_ref[chip, width:, :], local)
        f0, f1 = jnp.where(even, keep, got), jnp.where(even, got, keep)
        out_ref[chip, width:, :] = factor_rows(jnp.where(closes, f1, f0 * f1))
        carry = jnp.where(closes, 0.0, f1)
        for k in range(local):
            rows = slice(k * N, (k + 1) * N)
            keep = keep_ref[chip, rows, :].astype(jnp.float32)
            got = got_ref[chip, rows, :].astype(jnp.float32)
            s0, s1 = jnp.where(even, keep, got), jnp.where(even, got, keep)
            out_ref[chip, rows, :] = (carry[k : k + 1] * s0 + s1).astype(jnp.bfloat16)


def recurrence_kernel(local, meta, got_ref, restored_ref, *refs):
    out_ref, token_ref = refs[-2:]
    token_ref[...] = jnp.zeros_like(token_ref)
    width = local * N
    span = 2 * TOK
    state = [jnp.zeros((N, P_SIZE), jnp.float32) for _ in range(local)]
    for c in range(got_ref.shape[0]):
        first = c * span
        opening = meta.session_at(first)
        closing = meta.session_at(first + span - 1)
        opens = meta.start_of(opening) >= first
        closes = meta.start_of(closing) >= first
        factor = factors_of(got_ref[c, width:, :], local)
        for k in range(local):
            rows = slice(k * N, (k + 1) * N)
            entering = jnp.where(opens, restored_ref[opening, rows, :], state[k])
            out_ref[c, rows, :] = entering.astype(jnp.bfloat16)
            source = jnp.where(closes, restored_ref[closing, rows, :], state[k])
            state[k] = factor[k : k + 1] * source + got_ref[c, rows, :].astype(jnp.float32)


def intra_kernel(meta, skip, x_ref, dl_ref, step_ref, write_ref, read_ref, _, out_ref, token_ref, run_s, step_s):
    step = pl.program_id(0)

    @pl.when(step == 0)
    def _():
        _, running = running_rows(dl_ref)
        run_s[...] = running
        step_s[...] = step_ref[...].astype(jnp.float32)

    token_ref[...] = jnp.zeros_like(token_ref)
    heads = pl.ds(pl.multiple_of(step * PAIR, PAIR), PAIR)
    running = run_s[heads, :]
    sizes = step_s[heads, :]
    columns = running.T
    r = meta.last_start()
    t = lax.broadcasted_iota(jnp.int32, (TOK, TOK), 0)
    u = lax.broadcasted_iota(jnp.int32, (TOK, TOK), 1)
    causal = (u <= t) & ((u >= r) | (t < r))
    for group in range(2):
        part = slice(group * N, (group + 1) * N)
        products = lax.dot_general(
            read_ref[:, part], write_ref[:, part], (((1,), (1,)), ((), ())),
            preferred_element_type=jnp.float32,
        )
        products = jnp.where(causal, products, 0.0)
        for k in range(group * HEADS_PER, (group + 1) * HEADS_PER):
            difference = columns[:, k : k + 1] - running[k : k + 1]
            decay = jnp.exp(jnp.minimum(difference, 0.0))
            mixing = (products * decay * sizes[k : k + 1]).astype(jnp.bfloat16)
            place = slice(k * P_SIZE, (k + 1) * P_SIZE)
            x = x_ref[:, place]
            mixed = jnp.dot(mixing, x, preferred_element_type=jnp.float32)
            out_ref[:, place] = mixed + skip[step * PAIR + k] * x.astype(jnp.float32)


def intra(meta, skip, x, rates, steps, writes, reads, idle):
    return pl.pallas_call(
        scalars(intra_kernel),
        out_shape=[jax.ShapeDtypeStruct((TOK, H * P_SIZE), jnp.float32), TOKEN],
        grid_spec=pltpu.PrefetchScalarGridSpec(
            num_scalar_prefetch=2,
            grid=(STEPS,),
            in_specs=[
                pl.BlockSpec((TOK, PAIR * P_SIZE), lambda i, *m: (0, i)),
                pl.BlockSpec((H, TOK), lambda i, *m: (0, 0)),
                pl.BlockSpec((H, TOK), lambda i, *m: (0, 0)),
                pl.BlockSpec((TOK, 2 * N), lambda i, *m: (0, i)),
                pl.BlockSpec((TOK, 2 * N), lambda i, *m: (0, i)),
                pl.BlockSpec(memory_space=pl.ANY),
            ],
            out_specs=[
                pl.BlockSpec((TOK, PAIR * P_SIZE), lambda i, *m: (0, i)),
                pl.BlockSpec(TOKEN.shape, lambda i, *m: (0, 0)),
            ],
            scratch_shapes=[
                pltpu.VMEM((H, TOK), jnp.float32),
                pltpu.VMEM((H, TOK), jnp.float32),
            ],
        ),
        compiler_params=params(),
        cost_estimate=LONG,
        name="intra",
    )(meta, skip, x, rates, steps, writes, reads, idle)


def finish_kernel(
    local, meta, part_ref, dl_ref, read_ref, own_ref, other_ref, low_ref, high_ref, *refs,
):
    pieces, (out_ref, factor_s) = refs[:8], refs[-2:]
    bits = pieces[0].shape[0].bit_length() - 1
    step = pl.program_id(0)
    even = meta.even
    r = meta.last_start()
    first = meta.place // 2 * 2 * TOK
    second = first + TOK
    start = meta.start_of(meta.session_at(second + TOK - 1))
    closes = (start > first) & (start < second)
    opens = start == second
    width = local * N

    @pl.when(step == 0)
    def _():
        rates, running = running_rows(dl_ref)
        lane = lax.broadcasted_iota(jnp.int32, (H, TOK), 1)
        base = jnp.sum(jnp.where(lane < r, rates, 0.0), axis=1, keepdims=True)
        factor_s[...] = jnp.exp(jnp.minimum(running - jnp.where(lane >= r, base, 0.0), 0.0))

    factor = factor_s[pl.ds(pl.multiple_of(step * PAIR, PAIR), PAIR), :].T
    token = lax.broadcasted_iota(jnp.int32, (TOK, N), 0)
    resumed = (token >= r) & (r > 0)
    decays = [[factors_of(ref[chip, width:, :], local) for ref in (low_ref, high_ref)] for chip in range(own_ref.shape[0])]
    for group in range(2):
        reads = read_ref[:, group * N : (group + 1) * N].astype(jnp.float32)
        left = jnp.where(resumed, 0.0, reads)
        right = jnp.where(resumed, reads, 0.0)
        reads = jnp.concatenate([left, right], axis=1).astype(jnp.bfloat16)
        for k in range(group * HEADS_PER, (group + 1) * HEADS_PER):
            chip, half, head = k // (2 * local), k // local % 2, k % local
            rows = slice(head * N, (head + 1) * N)
            own = even if half == 0 else jnp.logical_not(even)
            entering = jnp.where(own, own_ref[chip, rows, :], other_ref[chip, rows, :]).astype(jnp.float32)
            distance = (step * own_ref.shape[0] + chip) ^ (meta.place // 2)
            far = far_place(distance // 4, bits)
            near, low_bit = distance % 2 == 0, distance // 2 % 2 == 0
            found = [piece[far, rows, :] for piece in pieces]
            found = [jnp.where(low_bit, found[i], found[i + 1]) for i in range(0, 8, 2)]
            restored = jnp.where(own, jnp.where(near, found[0], found[1]), jnp.where(near, found[2], found[3]))
            whole_state = restored.astype(jnp.float32)
            summary = (low_ref, high_ref)[half][chip, rows, :].astype(jnp.float32)
            middle = decays[chip][half][head : head + 1] * jnp.where(closes, whole_state, entering) + summary
            middle = jnp.where(opens, whole_state, middle)
            entering = jnp.where(even, entering, middle).astype(jnp.bfloat16)
            states = jnp.concatenate([entering, restored], axis=0)
            carried = jnp.dot(reads, states, preferred_element_type=jnp.float32)
            place = slice(k * P_SIZE, (k + 1) * P_SIZE)
            out_ref[:, place] = (part_ref[:, place] + factor[:, k : k + 1] * carried).astype(jnp.bfloat16)


def finish(meta, part, rates, reads, own, other, low, high, pieces, local):
    chips = PAIR // (2 * local)
    count, length, _ = pieces[0].shape
    resumed = pl.BlockSpec((count, local * N, P_SIZE), lambda i, *m: (0, length // (local * N) - 1, 0))
    states = pl.BlockSpec((chips, local * N, P_SIZE), lambda i, *m: (i, 0, 0))
    stretch = pl.BlockSpec((chips, local * N + EXTRA, P_SIZE), lambda i, *m: (i, 0, 0))
    return pl.pallas_call(
        scalars(finish_kernel, local),
        out_shape=jax.ShapeDtypeStruct((TOK, H * P_SIZE), jnp.bfloat16),
        grid_spec=pltpu.PrefetchScalarGridSpec(
            num_scalar_prefetch=1,
            grid=(STEPS,),
            in_specs=[
                pl.BlockSpec((TOK, PAIR * P_SIZE), lambda i, *m: (0, i)),
                pl.BlockSpec((H, TOK), lambda i, *m: (0, 0)),
                pl.BlockSpec((TOK, 2 * N), lambda i, *m: (0, i)),
                states,
                states,
                stretch,
                stretch,
            ]
            + [resumed] * 8,
            out_specs=pl.BlockSpec((TOK, PAIR * P_SIZE), lambda i, *m: (0, i)),
            scratch_shapes=[pltpu.VMEM((H, TOK), jnp.float32)],
        ),
        compiler_params=params(),
        cost_estimate=LONG,
        name="finish",
    )(meta, part, rates, reads, own, other, low, high, *pieces)


def attend_kernel(
    meta, q_ref, four, two, now, four_across, two_across, now_across, *refs,
):
    history_refs, (sk_ref, sv_ref), (out_ref, token_ref, key_s, value_s) = refs[:32], refs[32:34], refs[-4:]
    factor = 1.0 / math.sqrt(HD)
    first = meta.place * TOK
    r = meta.last_start()
    opening = meta.session_at(first)
    closing = meta.session_at(first + TOK - 1)
    even = meta.even

    def band(number, part):
        if number == 0:
            return four[part]
        if number == 1:
            return jnp.where(even, four_across[part], two_across[part])
        if number == 2:
            return two[part]
        if number == 3:
            return jnp.where(even, two_across[part], now_across[part])
        return now[part]

    token_ref[...] = jnp.zeros_like(token_ref)

    def sinks(ref, session):
        rows = ref[session].astype(jnp.float32)
        spare = jnp.zeros((COLUMNS - SPAN - SINKS, HD), jnp.float32)
        return jnp.concatenate([rows, spare], axis=0).astype(jnp.bfloat16)

    length = (REACH + 1) * TOK

    def one_session(session, key_refs, value_refs, resuming, needed):
        start = meta.start_of(session) - first + WINDOW
        oldest = start - WINDOW + jnp.maximum(SINKS + WINDOW - meta.history(session), 0)

        @pl.when(needed & (start > 0))
        def _():
            row = lax.broadcasted_iota(jnp.int32, (length, WINDOW), 0)
            chips, share, _ = key_refs[0].shape
            index = lax.broadcasted_iota(jnp.int32, (1, WINDOW), 1)
            piece, index = index // (WINDOW // 8), index % (WINDOW // 8)
            near, row_in = index // share, index % share
            far = far_place(near, chips.bit_length() - 1)
            device = meta.place ^ (piece // 4 + piece // 2 % 2 * 2 + piece % 2 * 4 + far * 8)
            place = device * share + row_in
            moved = (row == place + start - WINDOW).astype(jnp.bfloat16)
            part = (WINDOW // 8, HD)
            keys = jnp.concatenate([ref[...].reshape(part) for ref in key_refs], axis=0)
            values = jnp.concatenate([ref[...].reshape(part) for ref in value_refs], axis=0)
            history = jnp.dot(
                moved, jnp.concatenate([keys, values], axis=1), preferred_element_type=jnp.float32
            )
            for i in range(REACH + 1):
                rows = slice(i * TOK, (i + 1) * TOK)
                index = lax.broadcasted_iota(jnp.int32, (TOK, HD), 0) + i * TOK
                turn = index >= start
                key_s[rows, :] = jnp.where(
                    turn, band(i, 0).astype(jnp.float32), history[rows, :HD]
                ).astype(jnp.bfloat16)
                value_s[rows, :] = jnp.where(
                    turn, band(i, 1).astype(jnp.float32), history[rows, HD:]
                ).astype(jnp.bfloat16)

        @pl.when(needed & (start <= 0))
        def _():
            for i in range(REACH + 1):
                rows = slice(i * TOK, (i + 1) * TOK)
                key_s[rows, :] = band(i, 0)
                value_s[rows, :] = band(i, 1)

        for b in range(TOK // BLOCK):
            inside = (b * BLOCK + BLOCK > r) if resuming else (b * BLOCK < r)

            @pl.when(needed & inside)
            def _():
                rows = slice(b * BLOCK, b * BLOCK + SPAN)
                keys = jnp.concatenate([key_s[rows, :], sinks(sk_ref, session)], axis=0)
                values = jnp.concatenate([value_s[rows, :], sinks(sv_ref, session)], axis=0)
                tokens = slice(b * BLOCK, (b + 1) * BLOCK)
                queries = jnp.concatenate(
                    [q_ref[tokens, g * HD : (g + 1) * HD] for g in range(QH // KVH)], axis=0
                )
                scores = lax.dot_general(
                    queries, keys, (((1,), (1,)), ((), ())), preferred_element_type=jnp.float32
                )
                token = lax.broadcasted_iota(jnp.int32, (BLOCK, COLUMNS), 0)
                column = lax.broadcasted_iota(jnp.int32, (BLOCK, COLUMNS), 1)
                seen = (column > token) & (column <= token + WINDOW) & (column >= oldest - b * BLOCK)
                seen = (seen & (column < SPAN)) | ((column >= SPAN) & (column < SPAN + SINKS))
                bias = jnp.where(seen, 0.0, NEG)
                weights, sums = [], []
                for g in range(QH // KVH):
                    score = scores[g * BLOCK : (g + 1) * BLOCK] * factor + bias
                    weight = jnp.exp(score - jnp.max(score, axis=1, keepdims=True))
                    sums.append(jnp.sum(weight, axis=1, keepdims=True))
                    weights.append(weight.astype(jnp.bfloat16))
                mixed = jnp.dot(
                    jnp.concatenate(weights, axis=0), values, preferred_element_type=jnp.float32
                )
                for g in range(QH // KVH):
                    result = mixed[g * BLOCK : (g + 1) * BLOCK] / sums[g]
                    lanes = slice(g * HD, (g + 1) * HD)
                    if resuming:
                        index = lax.broadcasted_iota(jnp.int32, (BLOCK, HD), 0) + b * BLOCK
                        before = out_ref[tokens, lanes].astype(jnp.float32)
                        result = jnp.where(index >= r, result, before)
                    out_ref[tokens, lanes] = result.astype(jnp.bfloat16)

    one_session(opening, history_refs[0:8], history_refs[8:16], False, r > 0)
    one_session(closing, history_refs[16:24], history_refs[24:], True, r >= 0)


def attend(meta, queries, bands, pieces, half, sink_keys, sink_values, idle):
    chips = pieces[0].shape[0]
    share = WINDOW // (8 * chips)
    lanes = QH // KVH * HD

    def history_spec(which, last):
        def index(j, *m):
            known = Scalars(*m)
            session = known.session_at(known.place * TOK + (TOK - 1 if last else 0))
            session = session - (known.place >= half).astype(jnp.int32)
            return (0, (which * 2 + session) * KVH + j, 0)

        return pl.BlockSpec((chips, share, HD), index)

    pad = SEQS, SINKS, HD
    return pl.pallas_call(
        scalars(attend_kernel),
        out_shape=[jax.ShapeDtypeStruct((TOK, QH * HD), jnp.bfloat16), TOKEN],
        grid_spec=pltpu.PrefetchScalarGridSpec(
            num_scalar_prefetch=1,
            grid=(KVH,),
            in_specs=[pl.BlockSpec((TOK, lanes), lambda j, *m: (0, j))]
            + [pl.BlockSpec((2, TOK, HD), lambda j, *m: (0, 0, j))] * len(bands)
            + [history_spec(0, False)] * 8
            + [history_spec(1, False)] * 8
            + [history_spec(0, True)] * 8
            + [history_spec(1, True)] * 8
            + [pl.BlockSpec(pad, lambda j, *m: (0, 0, j))] * 2
            + [idle_spec(a) for a in idle],
            out_specs=[
                pl.BlockSpec((TOK, lanes), lambda j, *m: (0, j)),
                pl.BlockSpec(TOKEN.shape, lambda j, *m: (0, 0)),
            ],
            scratch_shapes=[
                pltpu.VMEM(((REACH + 1) * TOK, HD), jnp.bfloat16),
                pltpu.VMEM(((REACH + 1) * TOK, HD), jnp.bfloat16),
            ],
        ),
        compiler_params=params(),
        cost_estimate=SHORT,
        name="attend",
    )(
        meta, queries, *bands, *pieces, *pieces, *pieces, *pieces, sink_keys, sink_values, *idle
    )


def shifted(block, axis, distance):
    devices = range(lax.axis_size(axis))
    return lax.ppermute(block, axis, [(i - distance, i) for i in devices if i - distance in devices])


def shards(
    mamba_input,
    step_size,
    decay_log,
    state_write,
    state_read,
    skip_gain,
    saved_states,
    home_slot,
    turn_lengths,
    history_lengths,
    queries,
    turn_keys,
    turn_values,
    cache_keys,
    cache_values,
    sink_keys,
    sink_values,
):
    place = lax.axis_index("ctx")
    group = lax.axis_index("sess")
    groups = lax.axis_size("sess")
    devices = lax.axis_size("ctx")
    local = saved_states.shape[2]
    width = local * N
    chips = devices // 2
    same_core = [list(range(core, devices, 2)) for core in range(2)]
    meta = jnp.concatenate(
        [jnp.stack([place, group]).astype(jnp.int32), turn_lengths[0], history_lengths[0], home_slot]
    )
    x, rates, steps = mamba_input[0], decay_log[0].T, step_size[0].T
    writes, reads = state_write[0], state_read[0]
    def apart(block, distance):
        return lax.ppermute(block, "ctx", [(i, i ^ distance) for i in range(devices)])

    def exchanged(block):
        return lax.all_to_all(block, "ctx", 0, 0, axis_index_groups=same_core, tiled=True)

    stored = [saved_states[0]]
    for j in range(1, groups):
        route = [((i + j) % groups, i) for i in range(groups)]
        stored.append(lax.ppermute(saved_states[0], "sess", route))
    stored = [block.reshape(SEQS, local, P_SIZE, N) for block in stored]

    keep, send = summaries(meta, x, rates, steps, writes, local)
    got = apart(send, 1)

    parcel = (1, 4 * KVH * cache_keys.shape[2] + width, HD)
    band = (2, TOK, KVH * HD)
    near, away, key_value, restored = whole(
        scalars(restore_kernel, local, devices // 2, groups),
        "restore",
        meta,
        [*stored, cache_keys[0], cache_values[0], turn_keys[0], turn_values[0]],
        [
            (parcel, jnp.bfloat16),
            (parcel, jnp.bfloat16),
            (band, jnp.bfloat16),
            ((SEQS, width, P_SIZE), jnp.float32),
        ],
        idle=[send],
        mib=60,
    )
    distance = devices // 2
    moved = apart(away, distance)
    four = shifted(key_value, "ctx", 4)

    def joined(array):
        return ((2 * array.shape[0], *array.shape[1:]), jnp.bfloat16)

    after = got
    while distance > 8:
        [near] = whole(scalars(join_kernel), "join", meta, [near, moved], [joined(near)], idle=[after])
        after = near
        distance //= 2
        moved = apart(near, distance)
    near, two = whole(
        scalars(join_two_kernel),
        "join_two",
        meta,
        [near, moved, key_value, four],
        [joined(near), (band, jnp.bfloat16)],
        idle=[after],
    )
    moved = apart(near, 4)
    two = apart(two, 2)
    beside = apart(near, 2)
    [chip] = whole(
        scalars(combine_kernel, local),
        "combine",
        meta,
        [keep, got],
        [(keep.shape, jnp.bfloat16)],
        idle=[near],
    )
    total = exchanged(chip)
    part, token = intra(meta, skip_gain, x, rates, steps, writes, reads, chip)
    pieces = [near, moved, beside, apart(moved, 2)]
    bands = [four, two, key_value]
    across = [apart(block, 1) for block in bands]
    low = apart(keep, 1)

    entering, after = whole(
        scalars(recurrence_kernel, local),
        "recurrence",
        meta,
        [total, restored],
        [((chips, width, P_SIZE), jnp.bfloat16), (TOKEN.shape, TOKEN.dtype)],
        idle=[token, low, *across, *pieces],
    )
    entering = exchanged(entering)
    pieces += [apart(piece, 1) for piece in pieces]
    attended, token = attend(
        meta, queries[0], bands + across, pieces, devices // 2, sink_keys[0], sink_values[0], [after]
    )
    [entering] = whole(
        scalars(copy_kernel), "copy", meta, [entering], [((chips, width, P_SIZE), jnp.bfloat16)], idle=[token]
    )
    other = apart(entering, 1)
    mixed = finish(meta, part, rates, reads, entering, other, low, got, pieces, local)
    return mixed[None], attended[None]


def solution(mesh):
    token = P("sess", "ctx", None)
    return jax.shard_map(
        shards,
        mesh=mesh,
        in_specs=(
            token,
            token,
            token,
            token,
            token,
            P(),
            P("sess", None, "ctx", None),
            P(),
            P("sess", None),
            P("sess", None),
            token,
            token,
            token,
            P("sess", None, "ctx", None),
            P("sess", None, "ctx", None),
            P("sess", None, None, None),
            P("sess", None, None, None),
        ),
        out_specs=(token, token),
        check_vma=False,
    )
```

profile of v0, /device:TPU:19, one launch (start us, length us, event | category | flops | bytes accessed | tf_op | source)
XLA Modules:
  0.0 113.3 jit_solution(9131151439268174748)
XLA Ops:
  0.6 0.3 collective-permute-start.1
  1.0 1.3 %concatenate.3.ids = s32[14]{0:T(128)} concatenate(s32[1]{0:T(128)} %bitcast, s32[1]{0:T(128)} %bitcast.1, s32[3]{0:T(128)} %bitcast.27, s32[3]{0:T(128)} %bitcast.28, s32[6]{0:T(128)} %param.24), dimensions={0} | concatenate | bytes 112 | tf_op jit(solution)/shard_map/concatenate | solution.py:618
  2.3 5.3 %summaries.1 = (bf16[8,272,128]{2,1,0:T(8,128)(2,1)}, bf16[8,272,128]{2,1,0:T(8,128)(2,1)}) custom-call(s32[14]{0:T(128)} %concatenate.3.ids, bf16[128,8192]{1,0:T(8,128)(2,1)} %bitcast.29, bf16[64,128]{1,0:T(8,128)(2,1)} %bitcast.42, bf16[64,128]{1,0:T(8,128)(2,1)} %bitcast.40, bf16[128,512]{1,0:T(8,128)(2,1)} %bitcast.34), custom_call_target="tpu_custom_call" | custom-call | flops 34359738368 | bytes 1048576 | tf_op jit(solution)/shard_map/summaries/pallas_call | solution.py:139
  7.6 1.0 collective-permute-start
  8.5 0.0 copy-done.23
  8.5 1.3 %reshape_squeeze.3.refs_0_ = f32[3,4,128,64]{3,2,1,0:T(8,128)} reshape(f32[1,3,4,8192]{3,2,1,0:T(4,128)S(1)} %copy-done.23) | data formatting | bytes 786432 | tf_op jit(solution)/shard_map/reshape;squeeze | solution.py:633
  9.8 1.1 collective-permute-done.1
  10.9 1.3 %reshape.7.refs_1_ = f32[3,4,128,64]{3,2,1,0:T(8,128)} reshape(f32[3,4,8192]{2,1,0:T(4,128)S(1)} %collective-permute-done.1) | data formatting | bytes 786432 | tf_op jit(solution)/shard_map/reshape | solution.py:633
  12.2 3.5 %restore.1 = (bf16[1,768,128]{2,1,0:T(8,128)(2,1)}, bf16[1,768,128]{2,1,0:T(8,128)(2,1)}, bf16[2,128,512]{2,1,0:T(8,128)(2,1)}, f32[3,256,128]{2,1,0:T(8,128)}) custom-call(s32[14]{0:T(128)} %concatenate.3.ids, f32[3,4,128,64]{3,2,1,0:T(8,128)} %reshape_squeeze.3.refs_0_, f32[3,4,128,64]{3,2,1,0:T(8,128)} %reshape.7.refs_1_, bf16[3,32,512]{2,1,0:T(8,128)(2,1)} %bitcast.38, ...), custom_call_target="tpu_custom_call" | custom-call | flops 34359738368 | bytes 1048576 | tf_op jit(solution)/shard_map/restore/pallas_call | solution.py:172
  15.7 3.2 %collective-permute-start.3 = (bf16[2,128,512]{2,1,0:T(8,128)(2,1)}, bf16[2,128,512]{2,1,0:T(8,128)(2,1)S(1)}, u32[]{:S(2)}, u32[]{:S(2)}) collective-permute-start(bf16[2,128,512]{2,1,0:T(8,128)(2,1)} %get-tuple-element.20.refs_2_.refs_3_), channel_id=1, source_target_pairs={{0,4},{1,5},{2,6},{3,7},{4,8},{5,9},{6,10},{7,11},{8,12},{9,13},{1... | collective-permute-start | bytes 786440 | tf_op jit(solution)/shard_map/ppermute | solution.py:588
  18.9 0.1 collective-permute-start.2
  19.1 2.1 %collective-permute-start.4 = (bf16[8,272,128]{2,1,0:T(8,128)(2,1)}, bf16[8,272,128]{2,1,0:T(8,128)(2,1)}, u32[]{:S(2)}, u32[]{:S(2)}) collective-permute-start(bf16[8,272,128]{2,1,0:T(8,128)(2,1)} %get-tuple-element.16.refs_0_), channel_id=1, source_target_pairs={{0,1},{1,0},{2,3},{3,2},{4,5},{5,4},{6,7},{7,6},{8,9},{9,8},{10,11... | collective-permute-start | bytes 1671176 | tf_op jit(solution)/shard_map/ppermute | solution.py:624
  21.2 0.0 collective-permute-start.8
  21.2 0.0 collective-permute-done.refs_4_.refs_1_.refs_6_
  21.2 7.0 %collective-permute-done.2.refs_1_ = bf16[1,768,128]{2,1,0:T(8,128)(2,1)S(1)} collective-permute-done((bf16[1,768,128]{2,1,0:T(8,128)(2,1)}, bf16[1,768,128]{2,1,0:T(8,128)(2,1)S(1)}, u32[]{:S(2)}, u32[]{:S(2)}) %collective-permute-start.2) | collective-permute-done | bytes 196640 | tf_op jit(solution)/shard_map/ppermute | solution.py:624
  28.2 0.0 collective-permute-done.3.refs_3_.refs_1_
  28.2 1.0 copy-done.4
  29.2 0.9 copy-done.17
  30.2 0.6 join_two.1
  30.8 1.3 %collective-permute-start.10 = (bf16[2,768,128]{2,1,0:T(8,128)(2,1)S(1)}, bf16[2,768,128]{2,1,0:T(8,128)(2,1)S(1)}, u32[]{:S(2)}, u32[]{:S(2)}) collective-permute-start(bf16[2,768,128]{2,1,0:T(8,128)(2,1)S(1)} %get-tuple-element.21.refs_2_.refs_7_.refs_15_.refs_23_.refs_31_), channel_id=1, source_target_pairs={{0,2},{1,3},{2,0},{3,1},{4,6},{5,7},{6,4},{7,5},{8,10},{9,11},{10,... | collective-permute-start | bytes 1179656 | tf_op jit(solution)/shard_map/ppermute | solution.py:624
  32.1 5.5 %collective-permute-start.9 = (bf16[2,768,128]{2,1,0:T(8,128)(2,1)S(1)}, bf16[2,768,128]{2,1,0:T(8,128)(2,1)S(1)}, u32[]{:S(2)}, u32[]{:S(2)}) collective-permute-start(bf16[2,768,128]{2,1,0:T(8,128)(2,1)S(1)} %get-tuple-element.21.refs_2_.refs_7_.refs_15_.refs_23_.refs_31_), channel_id=1, source_target_pairs={{0,4},{1,5},{2,6},{3,7},{4,0},{5,1},{6,2},{7,3},{8,12},{9,13},{10,... | collective-permute-start | bytes 1179656 | tf_op jit(solution)/shard_map/ppermute | solution.py:624
  37.6 0.2 collective-permute-start.6
  37.8 2.6 %combine.1.refs_6_ = bf16[8,272,128]{2,1,0:T(8,128)(2,1)} custom-call(s32[14]{0:T(128)S(1)} %copy-done.10, bf16[8,272,128]{2,1,0:T(8,128)(2,1)} %get-tuple-element.16.refs_0_, bf16[8,272,128]{2,1,0:T(8,128)(2,1)S(1)} %collective-permute-done.refs_4_.refs_1_.refs_6_, bf16[2,768,128]{2,1,0:T(8,128)(2,1)S(1)} %get-tuple-element.21.refs_2_.refs_7_.refs_15_.refs_23_.refs_31_), custom_call_target="tpu_custom_call" | custom-call | flops 34359738368 | bytes 1048576 | tf_op jit(solution)/shard_map/combine/pallas_call | solution.py:172
  40.5 4.6 %all-to-all-start = ((bf16[8,272,128]{2,1,0:T(8,128)(2,1)}), bf16[8,272,128]{2,1,0:T(8,128)(2,1)S(1)}, u32[]{:S(2)}, u32[]{:S(2)}) async-start(bf16[8,272,128]{2,1,0:T(8,128)(2,1)} %combine.1.refs_6_), calls=%async_computation | async-start | bytes 1114112 | tf_op jit(solution)/shard_map/all_to_all | solution.py:627
  45.1 0.0 collective-permute-done.4.refs_3_.refs_5_
  45.1 3.9 %collective-permute-start.5 = (bf16[2,128,512]{2,1,0:T(8,128)(2,1)S(1)}, bf16[2,128,512]{2,1,0:T(8,128)(2,1)S(1)}, u32[]{:S(2)}, u32[]{:S(2)}) collective-permute-start(bf16[2,128,512]{2,1,0:T(8,128)(2,1)S(1)} %collective-permute-done.3.refs_3_.refs_1_), channel_id=1, source_target_pairs={{0,1},{1,0},{2,3},{3,2},{4,5},{5,4},{6,7},{7,6},{8,9},{9,8},{10,11... | collective-permute-start | bytes 786440 | tf_op jit(solution)/shard_map/ppermute | solution.py:624
  49.0 0.0 collective-permute-done.6.refs_2_
  49.0 1.9 %collective-permute-start.7 = (bf16[2,128,512]{2,1,0:T(8,128)(2,1)S(1)}, bf16[2,128,512]{2,1,0:T(8,128)(2,1)S(1)}, u32[]{:S(2)}, u32[]{:S(2)}) collective-permute-start(bf16[2,128,512]{2,1,0:T(8,128)(2,1)S(1)} %collective-permute-done.6.refs_2_), channel_id=1, source_target_pairs={{0,1},{1,0},{2,3},{3,2},{4,5},{5,4},{6,7},{7,6},{8,9},{9,8},{10,11... | collective-permute-start | bytes 786440 | tf_op jit(solution)/shard_map/ppermute | solution.py:624
  50.9 0.0 collective-permute-done.9.refs_8_.refs_16_.refs_24_.refs_32_
  50.9 2.2 %collective-permute-start.11 = (bf16[2,768,128]{2,1,0:T(8,128)(2,1)S(1)}, bf16[2,768,128]{2,1,0:T(8,128)(2,1)S(1)}, u32[]{:S(2)}, u32[]{:S(2)}) collective-permute-start(bf16[2,768,128]{2,1,0:T(8,128)(2,1)S(1)} %collective-permute-done.9.refs_8_.refs_16_.refs_24_.refs_32_), channel_id=1, source_target_pairs={{0,2},{1,3},{2,0},{3,1},{4,6},{5,7},{6,4},{7,5},{8,10},{9,11},{10,... | collective-permute-start | bytes 1179656 | tf_op jit(solution)/shard_map/ppermute | solution.py:624
  53.1 6.7 %intra.1 = (f32[128,8192]{1,0:T(8,128)}, f32[8,128]{1,0:T(8,128)}) custom-call(s32[14]{0:T(128)} %concatenate.3.ids, f32[64]{0:T(128)} %refs_0_.1, bf16[128,8192]{1,0:T(8,128)(2,1)} %bitcast.30, bf16[64,128]{1,0:T(8,128)(2,1)} %bitcast.43, bf16[64,128]{1,0:T(8,128)(2,1)} %bitcast.41, bf16[128,512]{1,0:T(8,128)(2,1)} %bitcast.35, bf16[128,512]{1,0:T(8,128)(2,1)} %bitcast.36, ...), custom_call_target="tpu_custom_call" | custom-call | flops 34359738368 | bytes 1048576 | tf_op jit(solution)/shard_map/intra/pallas_call | solution.py:315
  59.9 0.0 collective-permute-done.8.refs_6_
  59.9 0.0 collective-permute-done.5.refs_4_
  59.9 0.0 collective-permute-done.10.refs_9_.refs_17_.refs_25_.refs_33_
  59.9 0.0 collective-permute-done.7.refs_5_
  59.9 4.5 %collective-permute-done.11.refs_10_.refs_18_.refs_26_.refs_34_ = bf16[2,768,128]{2,1,0:T(8,128)(2,1)S(1)} collective-permute-done((bf16[2,768,128]{2,1,0:T(8,128)(2,1)S(1)}, bf16[2,768,128]{2,1,0:T(8,128)(2,1)S(1)}, u32[]{:S(2)}, u32[]{:S(2)}) %collective-permute-start.11) | collective-permute-done | bytes 393248 | tf_op jit(solution)/shard_map/ppermute | solution.py:624
  64.5 0.0 all-to-all-done.refs_0_
  64.5 1.1 copy-done.16
  65.6 0.7 copy-done.18
  66.3 1.6 %recurrence.1 = (bf16[8,256,128]{2,1,0:T(8,128)(2,1)}, f32[8,128]{1,0:T(8,128)S(1)}) custom-call(s32[14]{0:T(128)S(1)} %copy-done.11, bf16[8,272,128]{2,1,0:T(8,128)(2,1)S(1)} %all-to-all-done.refs_0_, f32[3,256,128]{2,1,0:T(8,128)S(1)} %copy-done.16, f32[8,128]{1,0:T(8,128)S(1)} %copy-done.18, bf16[8,272,128]{2,1,0:T(8,128)(2,1)} %collective-permute-done.4.refs_3_.refs_5_, ...), custom_call_target="tpu_custom_call" | custom-call | flops 34359738368 | bytes 1048576 | tf_op jit(solution)/shard_map/recurrence/pallas_call | solution.py:172
  67.9 0.0 copy-done.6
  67.9 8.5 %all-to-all-start.1 = ((bf16[8,256,128]{2,1,0:T(8,128)(2,1)}), bf16[8,256,128]{2,1,0:T(8,128)(2,1)S(1)}, u32[]{:S(2)}, u32[]{:S(2)}) async-start(bf16[8,256,128]{2,1,0:T(8,128)(2,1)} %get-tuple-element.26), calls=%async_computation.1 | async-start | bytes 1048576 | tf_op jit(solution)/shard_map/all_to_all | solution.py:627
  76.4 0.0 copy-done
  76.4 1.4 %collective-permute-start.12 = (bf16[2,768,128]{2,1,0:T(8,128)(2,1)S(1)}, bf16[2,768,128]{2,1,0:T(8,128)(2,1)S(1)}, u32[]{:S(2)}, u32[]{:S(2)}) collective-permute-start(bf16[2,768,128]{2,1,0:T(8,128)(2,1)S(1)} %get-tuple-element.21.refs_2_.refs_7_.refs_15_.refs_23_.refs_31_), channel_id=1, source_target_pairs={{0,1},{1,0},{2,3},{3,2},{4,5},{5,4},{6,7},{7,6},{8,9},{9,8},{10,11... | collective-permute-start | bytes 1179656 | tf_op jit(solution)/shard_map/ppermute | solution.py:624
  77.8 0.0 copy-done.1
  77.8 0.1 collective-permute-start.14
  77.9 0.4 collective-permute-start.13
  78.3 0.1 collective-permute-start.15
  78.4 0.8 collective-permute-done.12.refs_11_.refs_19_.refs_27_.refs_35_
  79.2 0.6 collective-permute-done.14.refs_13_.refs_21_.refs_29_.refs_37_
  79.7 0.6 collective-permute-done.13.refs_12_.refs_20_.refs_28_.refs_36_
  80.3 0.6 collective-permute-done.15.refs_14_.refs_22_.refs_30_.refs_38_
  80.9 0.2 copy-done.21
  81.1 0.5 copy-done.22
  81.6 20.2 %attend.1 = (bf16[128,4096]{1,0:T(8,128)(2,1)}, f32[8,128]{1,0:T(8,128)}) custom-call(s32[14]{0:T(128)} %concatenate.3.ids, bf16[128,4096]{1,0:T(8,128)(2,1)} %bitcast.23, bf16[2,128,512]{2,1,0:T(8,128)(2,1)} %copy-done.5, bf16[2,128,512]{2,1,0:T(8,128)(2,1)} %copy-done.24, bf16[2,128,512]{2,1,0:T(8,128)(2,1)} %get-tuple-element.20.refs_2_.refs_3_, ...), custom_call_target="tpu_custom_call" | custom-call | flops 1024 | bytes 1024 | tf_op jit(solution)/shard_map/attend/pallas_call | solution.py:555
  101.9 0.0 all-to-all-done.1.refs_0_
  101.9 0.0 copy-done.12
  101.9 0.0 copy-start.15
  101.9 0.7 copy-done.15
  102.6 0.6 copy.20.refs_3_
  103.2 0.1 collective-permute-start.16
  103.2 1.9 %collective-permute-done.16.refs_4_ = bf16[8,256,128]{2,1,0:T(8,128)(2,1)S(1)} collective-permute-done((bf16[8,256,128]{2,1,0:T(8,128)(2,1)S(1)}, bf16[8,256,128]{2,1,0:T(8,128)(2,1)S(1)}, u32[]{:S(2)}, u32[]{:S(2)}) %collective-permute-start.16) | collective-permute-done | bytes 524320 | tf_op jit(solution)/shard_map/ppermute | solution.py:624
  105.1 0.8 copy-done.25
  105.9 7.4 %finish.1 = bf16[128,8192]{1,0:T(8,128)(2,1)} custom-call(s32[14]{0:T(128)} %concatenate.3.ids, f32[128,8192]{1,0:T(8,128)} %get-tuple-element.22.refs_0_, bf16[64,128]{1,0:T(8,128)(2,1)} %bitcast.44, bf16[128,512]{1,0:T(8,128)(2,1)} %bitcast.37, bf16[8,256,128]{2,1,0:T(8,128)(2,1)} %copy-done.14, bf16[8,256,128]{2,1,0:T(8,128)(2,1)} %copy-done.25, ...), custom_call_target="tpu_custom_call" | custom-call | flops 34359738368 | bytes 1048576 | tf_op jit(solution)/shard_map/finish/pallas_call | solution.py:403
  (38 shorter events, 0.1 us)
Async XLA Ops:
  0.6 10.3 %collective-permute-start.1 = (f32[3,4,8192]{2,1,0:T(4,128)}, f32[3,4,8192]{2,1,0:T(4,128)S(1)}, u32[]{:S(2)}, u32[]{:S(2)}) collective-permute-start(f32[3,4,8192]{2,1,0:T(4,128)} %bitcast.24), channel_id=1, source_target_pairs={{16,0},{0,16},{17,1},{1,17},{18,2},{2,18},{19,3},{3,19},{20,4},{4,... | collective-permute-start | bytes 1179656 | tf_op jit(solution)/shard_map/ppermute | solution.py:632
  2.3 6.2 %copy-start.23 = (f32[1,3,4,8192]{3,2,1,0:T(4,128)S(1)}, f32[1,3,4,8192]{3,2,1,0:T(4,128)}, u32[]{:S(2)}) copy-start(f32[1,3,4,8192]{3,2,1,0:T(4,128)} %param.23) | copy-start | bytes 1179652
  7.6 13.6 %collective-permute-start = (bf16[8,272,128]{2,1,0:T(8,128)(2,1)}, bf16[8,272,128]{2,1,0:T(8,128)(2,1)S(1)}, u32[]{:S(2)}, u32[]{:S(2)}) collective-permute-start(bf16[8,272,128]{2,1,0:T(8,128)(2,1)} %get-tuple-element.17.refs_6_), channel_id=1, source_target_pairs={{0,1},{1,0},{2,3},{3,2},{4,5},{5,4},{6,7},{7,6},{8,9},{9,8},{10,11... | collective-permute-start | bytes 1671176 | tf_op jit(solution)/shard_map/ppermute | solution.py:624
  12.2 16.0 %copy-start.10 = (s32[14]{0:T(128)S(1)}, s32[14]{0:T(128)}, u32[]{:S(2)}) copy-start(s32[14]{0:T(128)} %concatenate.3.ids) | copy-start | bytes 172
  15.7 12.4 %collective-permute-start.3 = (bf16[2,128,512]{2,1,0:T(8,128)(2,1)}, bf16[2,128,512]{2,1,0:T(8,128)(2,1)S(1)}, u32[]{:S(2)}, u32[]{:S(2)}) collective-permute-start(bf16[2,128,512]{2,1,0:T(8,128)(2,1)} %get-tuple-element.20.refs_2_.refs_3_), channel_id=1, source_target_pairs={{0,4},{1,5},{2,6},{3,7},{4,8},{5,9},{6,10},{7,11},{8,12},{9,13},{1... | collective-permute-start | bytes 786440 | tf_op jit(solution)/shard_map/ppermute | solution.py:588
  18.9 9.2 %collective-permute-start.2 = (bf16[1,768,128]{2,1,0:T(8,128)(2,1)}, bf16[1,768,128]{2,1,0:T(8,128)(2,1)S(1)}, u32[]{:S(2)}, u32[]{:S(2)}) collective-permute-start(bf16[1,768,128]{2,1,0:T(8,128)(2,1)} %get-tuple-element.19), channel_id=1, source_target_pairs={{0,8},{1,9},{2,10},{3,11},{4,12},{5,13},{6,14},{7,15},{8,0},{9,1},... | collective-permute-start | bytes 589832 | tf_op jit(solution)/shard_map/ppermute | solution.py:624
  19.1 26.0 %collective-permute-start.4 = (bf16[8,272,128]{2,1,0:T(8,128)(2,1)}, bf16[8,272,128]{2,1,0:T(8,128)(2,1)}, u32[]{:S(2)}, u32[]{:S(2)}) collective-permute-start(bf16[8,272,128]{2,1,0:T(8,128)(2,1)} %get-tuple-element.16.refs_0_), channel_id=1, source_target_pairs={{0,1},{1,0},{2,3},{3,2},{4,5},{5,4},{6,7},{7,6},{8,9},{9,8},{10,11... | collective-permute-start | bytes 1671176 | tf_op jit(solution)/shard_map/ppermute | solution.py:624
  21.2 38.7 %collective-permute-start.8 = (bf16[2,128,512]{2,1,0:T(8,128)(2,1)}, bf16[2,128,512]{2,1,0:T(8,128)(2,1)S(1)}, u32[]{:S(2)}, u32[]{:S(2)}) collective-permute-start(bf16[2,128,512]{2,1,0:T(8,128)(2,1)} %get-tuple-element.20.refs_2_.refs_3_), channel_id=1, source_target_pairs={{0,1},{1,0},{2,3},{3,2},{4,5},{5,4},{6,7},{7,6},{8,9},{9,8},{10,11... | collective-permute-start | bytes 786440 | tf_op jit(solution)/shard_map/ppermute | solution.py:624
  21.2 16.6 %copy-start.13 = (bf16[8,272,128]{2,1,0:T(8,128)(2,1)}, bf16[8,272,128]{2,1,0:T(8,128)(2,1)S(1)}, u32[]{:S(2)}) copy-start(bf16[8,272,128]{2,1,0:T(8,128)(2,1)S(1)} %collective-permute-done.refs_4_.refs_1_.refs_6_) | copy-start | bytes 1671172
  28.2 16.9 %copy-start.5 = (bf16[2,128,512]{2,1,0:T(8,128)(2,1)}, bf16[2,128,512]{2,1,0:T(8,128)(2,1)S(1)}, u32[]{:S(2)}) copy-start(bf16[2,128,512]{2,1,0:T(8,128)(2,1)S(1)} %collective-permute-done.3.refs_3_.refs_1_) | copy-start | bytes 786436
  28.2 1.0 copy-start.4
  29.2 0.9 copy-start.17
  30.8 45.7 %copy-start = (bf16[2,768,128]{2,1,0:T(8,128)(2,1)}, bf16[2,768,128]{2,1,0:T(8,128)(2,1)S(1)}, u32[]{:S(2)}) copy-start(bf16[2,768,128]{2,1,0:T(8,128)(2,1)S(1)} %get-tuple-element.21.refs_2_.refs_7_.refs_15_.refs_23_.refs_31_) | copy-start | bytes 1179652
  30.8 29.1 %collective-permute-start.10 = (bf16[2,768,128]{2,1,0:T(8,128)(2,1)S(1)}, bf16[2,768,128]{2,1,0:T(8,128)(2,1)S(1)}, u32[]{:S(2)}, u32[]{:S(2)}) collective-permute-start(bf16[2,768,128]{2,1,0:T(8,128)(2,1)S(1)} %get-tuple-element.21.refs_2_.refs_7_.refs_15_.refs_23_.refs_31_), channel_id=1, source_target_pairs={{0,2},{1,3},{2,0},{3,1},{4,6},{5,7},{6,4},{7,5},{8,10},{9,11},{10,... | collective-permute-start | bytes 1179656 | tf_op jit(solution)/shard_map/ppermute | solution.py:624
  32.1 18.8 %collective-permute-start.9 = (bf16[2,768,128]{2,1,0:T(8,128)(2,1)S(1)}, bf16[2,768,128]{2,1,0:T(8,128)(2,1)S(1)}, u32[]{:S(2)}, u32[]{:S(2)}) collective-permute-start(bf16[2,768,128]{2,1,0:T(8,128)(2,1)S(1)} %get-tuple-element.21.refs_2_.refs_7_.refs_15_.refs_23_.refs_31_), channel_id=1, source_target_pairs={{0,4},{1,5},{2,6},{3,7},{4,0},{5,1},{6,2},{7,3},{8,12},{9,13},{10,... | collective-permute-start | bytes 1179656 | tf_op jit(solution)/shard_map/ppermute | solution.py:624
  37.6 11.4 %collective-permute-start.6 = (bf16[2,128,512]{2,1,0:T(8,128)(2,1)S(1)}, bf16[2,128,512]{2,1,0:T(8,128)(2,1)S(1)}, u32[]{:S(2)}, u32[]{:S(2)}) collective-permute-start(bf16[2,128,512]{2,1,0:T(8,128)(2,1)S(1)} %get-tuple-element.25), channel_id=1, source_target_pairs={{0,2},{1,3},{2,0},{3,1},{4,6},{5,7},{6,4},{7,5},{8,10},{9,11},{10,... | collective-permute-start | bytes 786440 | tf_op jit(solution)/shard_map/ppermute | solution.py:624
  40.5 24.0 %all-to-all-start = ((bf16[8,272,128]{2,1,0:T(8,128)(2,1)}), bf16[8,272,128]{2,1,0:T(8,128)(2,1)S(1)}, u32[]{:S(2)}, u32[]{:S(2)}) async-start(bf16[8,272,128]{2,1,0:T(8,128)(2,1)} %combine.1.refs_6_), calls=%async_computation | async-start | bytes 1114112 | tf_op jit(solution)/shard_map/all_to_all | solution.py:627
  45.1 14.8 %collective-permute-start.5 = (bf16[2,128,512]{2,1,0:T(8,128)(2,1)S(1)}, bf16[2,128,512]{2,1,0:T(8,128)(2,1)S(1)}, u32[]{:S(2)}, u32[]{:S(2)}) collective-permute-start(bf16[2,128,512]{2,1,0:T(8,128)(2,1)S(1)} %collective-permute-done.3.refs_3_.refs_1_), channel_id=1, source_target_pairs={{0,1},{1,0},{2,3},{3,2},{4,5},{5,4},{6,7},{7,6},{8,9},{9,8},{10,11... | collective-permute-start | bytes 786440 | tf_op jit(solution)/shard_map/ppermute | solution.py:624
  49.0 10.9 %copy-start.24 = (bf16[2,128,512]{2,1,0:T(8,128)(2,1)}, bf16[2,128,512]{2,1,0:T(8,128)(2,1)S(1)}, u32[]{:S(2)}) copy-start(bf16[2,128,512]{2,1,0:T(8,128)(2,1)S(1)} %collective-permute-done.6.refs_2_) | copy-start | bytes 786436
  49.0 10.9 %collective-permute-start.7 = (bf16[2,128,512]{2,1,0:T(8,128)(2,1)S(1)}, bf16[2,128,512]{2,1,0:T(8,128)(2,1)S(1)}, u32[]{:S(2)}, u32[]{:S(2)}) collective-permute-start(bf16[2,128,512]{2,1,0:T(8,128)(2,1)S(1)} %collective-permute-done.6.refs_2_), channel_id=1, source_target_pairs={{0,1},{1,0},{2,3},{3,2},{4,5},{5,4},{6,7},{7,6},{8,9},{9,8},{10,11... | collective-permute-start | bytes 786440 | tf_op jit(solution)/shard_map/ppermute | solution.py:624
  50.9 27.0 %copy-start.2 = (bf16[2,768,128]{2,1,0:T(8,128)(2,1)}, bf16[2,768,128]{2,1,0:T(8,128)(2,1)S(1)}, u32[]{:S(2)}) copy-start(bf16[2,768,128]{2,1,0:T(8,128)(2,1)S(1)} %collective-permute-done.9.refs_8_.refs_16_.refs_24_.refs_32_) | copy-start | bytes 1179652
  50.9 13.6 %collective-permute-start.11 = (bf16[2,768,128]{2,1,0:T(8,128)(2,1)S(1)}, bf16[2,768,128]{2,1,0:T(8,128)(2,1)S(1)}, u32[]{:S(2)}, u32[]{:S(2)}) collective-permute-start(bf16[2,768,128]{2,1,0:T(8,128)(2,1)S(1)} %collective-permute-done.9.refs_8_.refs_16_.refs_24_.refs_32_), channel_id=1, source_target_pairs={{0,2},{1,3},{2,0},{3,1},{4,6},{5,7},{6,4},{7,5},{8,10},{9,11},{10,... | collective-permute-start | bytes 1179656 | tf_op jit(solution)/shard_map/ppermute | solution.py:624
  53.1 11.4 %copy-start.11 = (s32[14]{0:T(128)S(1)}, s32[14]{0:T(128)}, u32[]{:S(2)}) copy-start(s32[14]{0:T(128)} %concatenate.3.ids) | copy-start | bytes 172
  59.9 8.0 %copy-start.6 = (bf16[2,128,512]{2,1,0:T(8,128)(2,1)}, bf16[2,128,512]{2,1,0:T(8,128)(2,1)S(1)}, u32[]{:S(2)}) copy-start(bf16[2,128,512]{2,1,0:T(8,128)(2,1)S(1)} %collective-permute-done.8.refs_6_) | copy-start | bytes 786436
  59.9 8.0 %copy-start.7 = (bf16[2,128,512]{2,1,0:T(8,128)(2,1)}, bf16[2,128,512]{2,1,0:T(8,128)(2,1)S(1)}, u32[]{:S(2)}) copy-start(bf16[2,128,512]{2,1,0:T(8,128)(2,1)S(1)} %collective-permute-done.5.refs_4_) | copy-start | bytes 786436
  59.9 17.9 %copy-start.1 = (bf16[2,768,128]{2,1,0:T(8,128)(2,1)}, bf16[2,768,128]{2,1,0:T(8,128)(2,1)S(1)}, u32[]{:S(2)}) copy-start(bf16[2,768,128]{2,1,0:T(8,128)(2,1)S(1)} %collective-permute-done.10.refs_9_.refs_17_.refs_25_.refs_33_) | copy-start | bytes 1179652
  59.9 7.9 %copy-start.8 = (bf16[2,128,512]{2,1,0:T(8,128)(2,1)}, bf16[2,128,512]{2,1,0:T(8,128)(2,1)S(1)}, u32[]{:S(2)}) copy-start(bf16[2,128,512]{2,1,0:T(8,128)(2,1)S(1)} %collective-permute-done.7.refs_5_) | copy-start | bytes 786436
  64.5 13.9 %copy-start.3 = (bf16[2,768,128]{2,1,0:T(8,128)(2,1)}, bf16[2,768,128]{2,1,0:T(8,128)(2,1)S(1)}, u32[]{:S(2)}) copy-start(bf16[2,768,128]{2,1,0:T(8,128)(2,1)S(1)} %collective-permute-done.11.refs_10_.refs_18_.refs_26_.refs_34_) | copy-start | bytes 1179652
  64.5 1.1 %copy-start.16 = (f32[3,256,128]{2,1,0:T(8,128)S(1)}, f32[3,256,128]{2,1,0:T(8,128)}, u32[]{:S(2)}) copy-start(f32[3,256,128]{2,1,0:T(8,128)} %get-tuple-element.23.refs_1_) | copy-start | bytes 1179652
  65.6 0.7 copy-start.18
  67.9 13.0 %copy-start.9 = (f32[8,128]{1,0:T(8,128)}, f32[8,128]{1,0:T(8,128)S(1)}, u32[]{:S(2)}) copy-start(f32[8,128]{1,0:T(8,128)S(1)} %get-tuple-element.27.refs_41_) | copy-start | bytes 12292
  67.9 34.0 %all-to-all-start.1 = ((bf16[8,256,128]{2,1,0:T(8,128)(2,1)}), bf16[8,256,128]{2,1,0:T(8,128)(2,1)S(1)}, u32[]{:S(2)}, u32[]{:S(2)}) async-start(bf16[8,256,128]{2,1,0:T(8,128)(2,1)} %get-tuple-element.26), calls=%async_computation.1 | async-start | bytes 1048576 | tf_op jit(solution)/shard_map/all_to_all | solution.py:627
  76.4 2.8 %collective-permute-start.12 = (bf16[2,768,128]{2,1,0:T(8,128)(2,1)S(1)}, bf16[2,768,128]{2,1,0:T(8,128)(2,1)S(1)}, u32[]{:S(2)}, u32[]{:S(2)}) collective-permute-start(bf16[2,768,128]{2,1,0:T(8,128)(2,1)S(1)} %get-tuple-element.21.refs_2_.refs_7_.refs_15_.refs_23_.refs_31_), channel_id=1, source_target_pairs={{0,1},{1,0},{2,3},{3,2},{4,5},{5,4},{6,7},{7,6},{8,9},{9,8},{10,11... | collective-permute-start | bytes 1179656 | tf_op jit(solution)/shard_map/ppermute | solution.py:624
  77.8 1.9 %collective-permute-start.14 = (bf16[2,768,128]{2,1,0:T(8,128)(2,1)S(1)}, bf16[2,768,128]{2,1,0:T(8,128)(2,1)S(1)}, u32[]{:S(2)}, u32[]{:S(2)}) collective-permute-start(bf16[2,768,128]{2,1,0:T(8,128)(2,1)S(1)} %collective-permute-done.10.refs_9_.refs_17_.refs_25_.refs_33_), channel_id=1, source_target_pairs={{0,1},{1,0},{2,3},{3,2},{4,5},{5,4},{6,7},{7,6},{8,9},{9,8},{10,11... | collective-permute-start | bytes 1179656 | tf_op jit(solution)/shard_map/ppermute | solution.py:624
  77.9 2.4 %collective-permute-start.13 = (bf16[2,768,128]{2,1,0:T(8,128)(2,1)S(1)}, bf16[2,768,128]{2,1,0:T(8,128)(2,1)S(1)}, u32[]{:S(2)}, u32[]{:S(2)}) collective-permute-start(bf16[2,768,128]{2,1,0:T(8,128)(2,1)S(1)} %collective-permute-done.9.refs_8_.refs_16_.refs_24_.refs_32_), channel_id=1, source_target_pairs={{0,1},{1,0},{2,3},{3,2},{4,5},{5,4},{6,7},{7,6},{8,9},{9,8},{10,11... | collective-permute-start | bytes 1179656 | tf_op jit(solution)/shard_map/ppermute | solution.py:624
  78.3 2.5 %collective-permute-start.15 = (bf16[2,768,128]{2,1,0:T(8,128)(2,1)S(1)}, bf16[2,768,128]{2,1,0:T(8,128)(2,1)S(1)}, u32[]{:S(2)}, u32[]{:S(2)}) collective-permute-start(bf16[2,768,128]{2,1,0:T(8,128)(2,1)S(1)} %collective-permute-done.11.refs_10_.refs_18_.refs_26_.refs_34_), channel_id=1, source_target_pairs={{0,1},{1,0},{2,3},{3,2},{4,5},{5,4},{6,7},{7,6},{8,9},{9,8},{10,11... | collective-permute-start | bytes 1179656 | tf_op jit(solution)/shard_map/ppermute | solution.py:624
  79.2 1.7 %copy-start.19 = (bf16[2,768,128]{2,1,0:T(8,128)(2,1)}, bf16[2,768,128]{2,1,0:T(8,128)(2,1)S(1)}, u32[]{:S(2)}) copy-start(bf16[2,768,128]{2,1,0:T(8,128)(2,1)S(1)} %collective-permute-done.12.refs_11_.refs_19_.refs_27_.refs_35_) | copy-start | bytes 1179652
  79.7 1.1 %copy-start.20 = (bf16[2,768,128]{2,1,0:T(8,128)(2,1)}, bf16[2,768,128]{2,1,0:T(8,128)(2,1)S(1)}, u32[]{:S(2)}) copy-start(bf16[2,768,128]{2,1,0:T(8,128)(2,1)S(1)} %collective-permute-done.14.refs_13_.refs_21_.refs_29_.refs_37_) | copy-start | bytes 1179652
  80.3 0.8 copy-start.21
  80.9 0.8 copy-start.22
  81.6 20.3 %copy-start.12 = (s32[14]{0:T(128)S(1)}, s32[14]{0:T(128)}, u32[]{:S(2)}) copy-start(s32[14]{0:T(128)} %concatenate.3.ids) | copy-start | bytes 172
  101.9 0.7 copy-start.15
  103.1 2.0 %copy-start.14 = (bf16[8,256,128]{2,1,0:T(8,128)(2,1)}, bf16[8,256,128]{2,1,0:T(8,128)(2,1)S(1)}, u32[]{:S(2)}) copy-start(bf16[8,256,128]{2,1,0:T(8,128)(2,1)S(1)} %copy.20.refs_3_) | copy-start | bytes 1572868
  103.2 2.0 %collective-permute-start.16 = (bf16[8,256,128]{2,1,0:T(8,128)(2,1)S(1)}, bf16[8,256,128]{2,1,0:T(8,128)(2,1)S(1)}, u32[]{:S(2)}, u32[]{:S(2)}) collective-permute-start(bf16[8,256,128]{2,1,0:T(8,128)(2,1)S(1)} %copy.20.refs_3_), channel_id=1, source_target_pairs={{0,1},{1,0},{2,3},{3,2},{4,5},{5,4},{6,7},{7,6},{8,9},{9,8},{10,11... | collective-permute-start | bytes 1572872 | tf_op jit(solution)/shard_map/ppermute | solution.py:624
  105.1 0.8 copy-start.25
where the time goes:
time: 114 us; the launch traced here: 113 us
  Pallas kernels  48.6 us (43%)
  starting transfers between devices  37 us (32%)
  waiting for transfers between devices  17 us (15%)
  local copies, waits for them, and re-layouts  9.97 us (9%)
    ppermute x15, starting transfers between devices, apart(): lax.ppermute(block, 'ctx', [(i, i ^ distance) for i in range(devices)])  20.4 us
    pallas_call x1, Pallas kernels, attend(): pl.pallas_call(scalars(attend_kernel), out_shape=[jax.ShapeDtypeStruct((T...  20.2 us
    ppermute x15, waiting for transfers between devices, apart(): lax.ppermute(block, 'ctx', [(i, i ^ distance) for i in range(devices)])  15.9 us
    all_to_all x2, starting transfers between devices, exchanged(): lax.all_to_all(block, 'ctx', 0, 0, axis_index_groups=same_core, tiled=True)  13.1 us
    pallas_call x5, Pallas kernels, whole(): pl.pallas_call(kernel, out_shape=[jax.ShapeDtypeStruct(s, t) for s, t in...  8.92 us
    pallas_call x1, Pallas kernels, finish(): pl.pallas_call(scalars(finish_kernel, local), out_shape=jax.ShapeDtypeStr...  7.41 us
    pallas_call x1, Pallas kernels, intra(): pl.pallas_call(scalars(intra_kernel), out_shape=[jax.ShapeDtypeStruct((TO...  6.74 us
    unnamed x52, local copies, waits for them, and re-layouts  6.06 us
  transfers between devices with their start and end apart: 19, of which 8 were waited for; matrix products, arithmetic and copies ran while one was open for 3% of the time, Pallas kernels for 34%

commit v1 on v0

--- a/solution.py
+++ b/solution.py
@@ -78,7 +78,7 @@
 
 
 def summary_kernel(
-    local, meta, x_ref, dl_ref, step_ref, write_ref, keep_ref, send_ref, coef_s, factor_s, write_s
+    local, meta, x_ref, dl_ref, step_ref, write_ref, _, keep_ref, send_ref, coef_s, factor_s, write_s
 ):
     step = pl.program_id(0)
 
@@ -131,7 +131,7 @@
     return block[:local] + block[local : 2 * local]
 
 
-def summaries(meta, x, rates, steps, writes, local):
+def summaries(meta, x, rates, steps, writes, local, idle):
     chips = H // (2 * local)
     rows = local * N + EXTRA
     shape = jax.ShapeDtypeStruct((chips, rows, P_SIZE), jnp.bfloat16)
@@ -147,6 +147,7 @@
                 pl.BlockSpec((H, TOK), lambda i, *m: (0, 0)),
                 pl.BlockSpec((H, TOK), lambda i, *m: (0, 0)),
                 pl.BlockSpec((TOK, G * N), lambda i, *m: (0, 0)),
+                pl.BlockSpec(memory_space=pl.ANY),
             ],
             out_specs=[spec, spec],
             scratch_shapes=[
@@ -158,7 +159,7 @@
         compiler_params=params(),
         cost_estimate=LONG,
         name="summaries",
-    )(meta, x, rates, steps, writes)
+    )(meta, x, rates, steps, writes, idle)
 
 
 def idle_spec(array):
@@ -185,11 +186,21 @@
     )(meta, *arrays, *idle)
 
 
-def restore_kernel(local, half, groups, meta, *refs):
-    stored, (keys_ref, values_ref, turn_keys_ref, turn_values_ref) = refs[:groups], refs[groups : groups + 4]
-    home_ref, away_ref, band_ref, restored_ref = refs[-4:]
+def pack_kernel(half, meta, keys_ref, values_ref, turn_keys_ref, turn_values_ref, home_ref, away_ref, band_ref):
     band_ref[0] = turn_keys_ref[...]
     band_ref[1] = turn_values_ref[...]
+    rows = keys_ref.shape[1]
+    upper = (meta.place >= half).astype(jnp.int32)
+    for out_ref, first in ((home_ref, upper), (away_ref, 1 - upper)):
+        for which, ref in enumerate((keys_ref, values_ref)):
+            for s in range(2):
+                for j in range(KVH):
+                    place = ((which * 2 + s) * KVH + j) * rows
+                    out_ref[0, place : place + rows, :] = ref[first + s, :, j * HD : (j + 1) * HD]
+
+
+def restore_kernel(local, half, groups, meta, *refs):
+    stored, (home_ref, away_ref, restored_ref) = refs[:groups], refs[-3:]
     for s in range(SEQS):
         slot = meta.home(meta.group * SEQS + s)
         source = (slot // SEQS - meta.group + groups) % groups
@@ -198,15 +209,9 @@
             for j in range(1, groups):
                 state = jnp.where(source == j, stored[j][slot % SEQS, k], state)
             restored_ref[s, k * N : (k + 1) * N, :] = state.T
-    rows = keys_ref.shape[1]
     upper = (meta.place >= half).astype(jnp.int32)
-    for out_ref, first in ((home_ref, upper), (away_ref, 1 - upper)):
-        for which, ref in enumerate((keys_ref, values_ref)):
-            for s in range(2):
-                for j in range(KVH):
-                    place = ((which * 2 + s) * KVH + j) * rows
-                    out_ref[0, place : place + rows, :] = ref[first + s, :, j * HD : (j + 1) * HD]
-        out_ref[0, 4 * KVH * rows :, :] = restored_ref[first + 1].astype(jnp.bfloat16)
+    home_ref[0] = restored_ref[upper + 1].astype(jnp.bfloat16)
+    away_ref[0] = restored_ref[2 - upper].astype(jnp.bfloat16)
 
 
 def copy_kernel(meta, array_ref, *refs):
@@ -220,11 +225,14 @@
     out_ref[count:] = second_ref[...]
 
 
-def join_two_kernel(meta, first_ref, second_ref, key_value_ref, four_ref, *refs):
+def join_two_kernel(
+    meta, first_ref, second_ref, first_state_ref, second_state_ref, key_value_ref, four_ref, *refs
+):
     out_ref, two_ref = refs[-2:]
-    count = first_ref.shape[0]
-    out_ref[:count] = first_ref[...]
-    out_ref[count:] = second_ref[...]
+    rows = first_ref.shape[1]
+    for i, (parcel, state) in enumerate(((first_ref, first_state_ref), (second_ref, second_state_ref))):
+        out_ref[i, :rows, :] = parcel[0]
+        out_ref[i, rows:, :] = state[0]
     two_ref[...] = jnp.where(meta.place // 2 % 2 == 0, key_value_ref[...], four_ref[...])
 
 
@@ -632,46 +640,45 @@
         stored.append(lax.ppermute(saved_states[0], "sess", route))
     stored = [block.reshape(SEQS, local, P_SIZE, N) for block in stored]
 
-    keep, send = summaries(meta, x, rates, steps, writes, local)
+    parcel = (1, 4 * KVH * cache_keys.shape[2], HD)
+    band = (2, TOK, KVH * HD)
+    near, away, key_value = whole(
+        scalars(pack_kernel, devices // 2),
+        "pack",
+        meta,
+        [cache_keys[0], cache_values[0], turn_keys[0], turn_values[0]],
+        [(parcel, jnp.bfloat16), (parcel, jnp.bfloat16), (band, jnp.bfloat16)],
+        mib=60,
+    )
+    moved = apart(away, devices // 2)
+    four = shifted(key_value, "ctx", 4)
+
+    keep, send = summaries(meta, x, rates, steps, writes, local, away)
     got = apart(send, 1)
 
-    parcel = (1, 4 * KVH * cache_keys.shape[2] + width, HD)
-    band = (2, TOK, KVH * HD)
-    near, away, key_value, restored = whole(
+    one = (1, width, P_SIZE)
+    home, away, restored = whole(
         scalars(restore_kernel, local, devices // 2, groups),
         "restore",
         meta,
-        [*stored, cache_keys[0], cache_values[0], turn_keys[0], turn_values[0]],
-        [
-            (parcel, jnp.bfloat16),
-            (parcel, jnp.bfloat16),
-            (band, jnp.bfloat16),
-            ((SEQS, width, P_SIZE), jnp.float32),
-        ],
+        stored,
+        [(one, jnp.bfloat16), (one, jnp.bfloat16), ((SEQS, width, P_SIZE), jnp.float32)],
         idle=[send],
-        mib=60,
-    )
-    distance = devices // 2
-    moved = apart(away, distance)
-    four = shifted(key_value, "ctx", 4)
-
-    def joined(array):
-        return ((2 * array.shape[0], *array.shape[1:]), jnp.bfloat16)
-
-    after = got
-    while distance > 8:
-        [near] = whole(scalars(join_kernel), "join", meta, [near, moved], [joined(near)], idle=[after])
-        after = near
-        distance //= 2
-        moved = apart(near, distance)
+    )
+    away = apart(away, devices // 2)
     near, two = whole(
         scalars(join_two_kernel),
         "join_two",
         meta,
-        [near, moved, key_value, four],
-        [joined(near), (band, jnp.bfloat16)],
-        idle=[after],
-    )
+        [near, moved, home, away, key_value, four],
+        [((2, parcel[1] + width, HD), jnp.bfloat16), (band, jnp.bfloat16)],
+        idle=[got],
+    )
+    distance = devices // 4
+    while distance > 4:
+        joined = (2 * near.shape[0], *near.shape[1:])
+        [near] = whole(scalars(join_kernel), "join", meta, [near, apart(near, distance)], [(joined, jnp.bfloat16)])
+        distance //= 2
     moved = apart(near, 4)
     two = apart(two, 2)
     beside = apart(near, 2)

time: 114 us -> 107 us (0.939)
  the two profiles are of different devices: /device:TPU:19 before, /device:TPU:3 now
where the time goes in v1:
time: 107 us; the launch traced here: 105 us
  Pallas kernels  48.3 us (45%)
  waiting for transfers between devices  24 us (22%)
  starting transfers between devices  22.8 us (21%)
  local copies, waits for them, and re-layouts  9.15 us (9%)
    ppermute x16, waiting for transfers between devices, apart(): lax.ppermute(block, 'ctx', [(i, i ^ distance) for i in range(devices)])  24 us
    pallas_call x1, Pallas kernels, attend(): pl.pallas_call(scalars(attend_kernel), out_shape=[jax.ShapeDtypeStruct((T...  20.2 us
    ppermute x16, starting transfers between devices, apart(): lax.ppermute(block, 'ctx', [(i, i ^ distance) for i in range(devices)])  10.9 us
    pallas_call x6, Pallas kernels, whole(): pl.pallas_call(kernel, out_shape=[jax.ShapeDtypeStruct(s, t) for s, t in...  8.76 us
    all_to_all x2, starting transfers between devices, exchanged(): lax.all_to_all(block, 'ctx', 0, 0, axis_index_groups=same_core, tiled=True)  8.69 us
    pallas_call x1, Pallas kernels, finish(): pl.pallas_call(scalars(finish_kernel, local), out_shape=jax.ShapeDtypeStr...  7.42 us
    pallas_call x1, Pallas kernels, intra(): pl.pallas_call(scalars(intra_kernel), out_shape=[jax.ShapeDtypeStruct((TO...  6.73 us
    unnamed x56, local copies, waits for them, and re-layouts  6 us
  transfers between devices with their start and end apart: 20, of which 9 were waited for; matrix products, arithmetic and copies ran while one was open for 3% of the time, Pallas kernels for 37%

profile of v1, /device:TPU:3, one launch (start us, length us, event | category | flops | bytes accessed | tf_op | source)
XLA Modules:
  0.0 105.2 jit_solution(7023652685042656620)
XLA Ops:
  0.6 0.1 collective-permute-start.2
  0.7 1.3 %concatenate.3.ids = s32[14]{0:T(128)} concatenate(s32[1]{0:T(128)} %bitcast, s32[1]{0:T(128)} %bitcast.1, s32[3]{0:T(128)} %bitcast.27, s32[3]{0:T(128)} %bitcast.28, s32[6]{0:T(128)} %param.24), dimensions={0} | concatenate | bytes 112 | tf_op jit(solution)/shard_map/concatenate | solution.py:626
  2.1 2.5 %pack.1 = (bf16[1,512,128]{2,1,0:T(8,128)(2,1)}, bf16[1,512,128]{2,1,0:T(8,128)(2,1)}, bf16[2,128,512]{2,1,0:T(8,128)(2,1)}) custom-call(s32[14]{0:T(128)} %concatenate.3.ids, bf16[3,32,512]{2,1,0:T(8,128)(2,1)} %bitcast.38, bf16[3,32,512]{2,1,0:T(8,128)(2,1)} %bitcast.39, bf16[128,512]{1,0:T(8,128)(2,1)} %bitcast.32, bf16[128,512]{1,0:T(8,128)(2,1)} %bitcast.33), custom_call_target="tpu_custom_call" | custom-call | flops 34359738368 | bytes 1048576 | tf_op jit(solution)/shard_map/pack/pallas_call | solution.py:173
  4.6 2.5 %collective-permute-start.1 = (bf16[1,512,128]{2,1,0:T(8,128)(2,1)}, bf16[1,512,128]{2,1,0:T(8,128)(2,1)S(1)}, u32[]{:S(2)}, u32[]{:S(2)}) collective-permute-start(bf16[1,512,128]{2,1,0:T(8,128)(2,1)} %get-tuple-element.18.refs_4_), channel_id=1, source_target_pairs={{0,8},{1,9},{2,10},{3,11},{4,12},{5,13},{6,14},{7,15},{8,0},{9,1},... | collective-permute-start | bytes 393224 | tf_op jit(solution)/shard_map/ppermute | solution.py:632
  7.1 3.2 %collective-permute-start.4 = (bf16[2,128,512]{2,1,0:T(8,128)(2,1)}, bf16[2,128,512]{2,1,0:T(8,128)(2,1)S(1)}, u32[]{:S(2)}, u32[]{:S(2)}) collective-permute-start(bf16[2,128,512]{2,1,0:T(8,128)(2,1)} %get-tuple-element.24.refs_4_.refs_3_), channel_id=1, source_target_pairs={{0,4},{1,5},{2,6},{3,7},{4,8},{5,9},{6,10},{7,11},{8,12},{9,13},{1... | collective-permute-start | bytes 786440 | tf_op jit(solution)/shard_map/ppermute | solution.py:596
  10.4 0.0 copy-start.25
  10.4 5.2 %summaries.1 = (bf16[8,272,128]{2,1,0:T(8,128)(2,1)}, bf16[8,272,128]{2,1,0:T(8,128)(2,1)}) custom-call(s32[14]{0:T(128)} %concatenate.3.ids, bf16[128,8192]{1,0:T(8,128)(2,1)} %bitcast.29, bf16[64,128]{1,0:T(8,128)(2,1)} %bitcast.42, bf16[64,128]{1,0:T(8,128)(2,1)} %bitcast.40, bf16[128,512]{1,0:T(8,128)(2,1)} %bitcast.34, ...), custom_call_target="tpu_custom_call" | custom-call | flops 34359738368 | bytes 1048576 | tf_op jit(solution)/shard_map/summaries/pallas_call | solution.py:139
  15.6 1.5 %collective-permute-start = (bf16[8,272,128]{2,1,0:T(8,128)(2,1)}, bf16[8,272,128]{2,1,0:T(8,128)(2,1)S(1)}, u32[]{:S(2)}, u32[]{:S(2)}) collective-permute-start(bf16[8,272,128]{2,1,0:T(8,128)(2,1)} %get-tuple-element.20.refs_2_), channel_id=1, source_target_pairs={{0,1},{1,0},{2,3},{3,2},{4,5},{5,4},{6,7},{7,6},{8,9},{9,8},{10,11... | collective-permute-start | bytes 1671176 | tf_op jit(solution)/shard_map/ppermute | solution.py:632
  17.1 0.4 reshape_squeeze.3.refs_0_
  17.5 0.0 collective-permute-done.2
  17.6 1.4 %reshape.7.refs_1_ = f32[3,4,128,64]{3,2,1,0:T(8,128)S(1)} reshape(f32[3,4,8192]{2,1,0:T(4,128)} %collective-permute-done.2) | data formatting | bytes 786432 | tf_op jit(solution)/shard_map/reshape | solution.py:641
  19.0 0.0 copy-start.14
  19.0 1.0 copy-done.14
  20.0 0.8 restore.1
  20.9 0.0 copy-start.17
  20.9 0.8 copy-done.17
  21.7 0.0 collective-permute-start.3
  21.7 0.3 collective-permute-start.9
  22.0 0.0 collective-permute-done.1.refs_1_
  22.0 0.2 collective-permute-start.5
  22.2 0.0 collective-permute-done.4.refs_5_.refs_1_
  22.2 0.3 collective-permute-start.6
  22.5 4.9 %collective-permute-done.3.refs_3_ = bf16[1,256,128]{2,1,0:T(8,128)(2,1)S(1)} collective-permute-done((bf16[1,256,128]{2,1,0:T(8,128)(2,1)S(1)}, bf16[1,256,128]{2,1,0:T(8,128)(2,1)S(1)}, u32[]{:S(2)}, u32[]{:S(2)}) %collective-permute-start.3) | collective-permute-done | bytes 65568 | tf_op jit(solution)/shard_map/ppermute | solution.py:632
  27.5 0.0 collective-permute-done.refs_6_.refs_1_
  27.5 0.6 join_two.1
  28.1 1.3 %collective-permute-start.7 = (bf16[2,128,512]{2,1,0:T(8,128)(2,1)S(1)}, bf16[2,128,512]{2,1,0:T(8,128)(2,1)S(1)}, u32[]{:S(2)}, u32[]{:S(2)}) collective-permute-start(bf16[2,128,512]{2,1,0:T(8,128)(2,1)S(1)} %get-tuple-element.29), channel_id=1, source_target_pairs={{0,2},{1,3},{2,0},{3,1},{4,6},{5,7},{6,4},{7,5},{8,10},{9,11},{10,... | collective-permute-start | bytes 786440 | tf_op jit(solution)/shard_map/ppermute | solution.py:632
  29.4 0.0 collective-permute-start.10
  29.4 0.0 copy-done.13
  29.4 2.6 %combine.1.refs_6_ = bf16[8,272,128]{2,1,0:T(8,128)(2,1)} custom-call(s32[14]{0:T(128)S(1)} %copy-done.10, bf16[8,272,128]{2,1,0:T(8,128)(2,1)} %get-tuple-element.19.refs_0_, bf16[8,272,128]{2,1,0:T(8,128)(2,1)S(1)} %collective-permute-done.refs_6_.refs_1_, bf16[2,768,128]{2,1,0:T(8,128)(2,1)S(1)} %get-tuple-element.25.refs_2_.refs_7_.refs_15_.refs_23_.refs_31_), custom_call_target="tpu_custom_call" | custom-call | flops 34359738368 | bytes 1048576 | tf_op jit(solution)/shard_map/combine/pallas_call | solution.py:173
  32.1 3.5 %all-to-all-start = ((bf16[8,272,128]{2,1,0:T(8,128)(2,1)}), bf16[8,272,128]{2,1,0:T(8,128)(2,1)S(1)}, u32[]{:S(2)}, u32[]{:S(2)}) async-start(bf16[8,272,128]{2,1,0:T(8,128)(2,1)} %combine.1.refs_6_), calls=%async_computation | async-start | bytes 1114112 | tf_op jit(solution)/shard_map/all_to_all | solution.py:635
  35.6 0.0 collective-permute-done.9.refs_6_
  35.6 1.4 %collective-permute-start.11 = (bf16[2,768,128]{2,1,0:T(8,128)(2,1)S(1)}, bf16[2,768,128]{2,1,0:T(8,128)(2,1)S(1)}, u32[]{:S(2)}, u32[]{:S(2)}) collective-permute-start(bf16[2,768,128]{2,1,0:T(8,128)(2,1)S(1)} %get-tuple-element.25.refs_2_.refs_7_.refs_15_.refs_23_.refs_31_), channel_id=1, source_target_pairs={{0,2},{1,3},{2,0},{3,1},{4,6},{5,7},{6,4},{7,5},{8,10},{9,11},{10,... | collective-permute-start | bytes 1179656 | tf_op jit(solution)/shard_map/ppermute | solution.py:632
  37.0 0.0 collective-permute-done.7.refs_2_
  37.1 1.3 %collective-permute-start.8 = (bf16[2,128,512]{2,1,0:T(8,128)(2,1)S(1)}, bf16[2,128,512]{2,1,0:T(8,128)(2,1)S(1)}, u32[]{:S(2)}, u32[]{:S(2)}) collective-permute-start(bf16[2,128,512]{2,1,0:T(8,128)(2,1)S(1)} %collective-permute-done.7.refs_2_), channel_id=1, source_target_pairs={{0,1},{1,0},{2,3},{3,2},{4,5},{5,4},{6,7},{7,6},{8,9},{9,8},{10,11... | collective-permute-start | bytes 786440 | tf_op jit(solution)/shard_map/ppermute | solution.py:632
  38.3 1.0 collective-permute-done.10.refs_8_.refs_16_.refs_24_.refs_32_
  39.4 0.2 collective-permute-start.12
  39.6 6.7 %intra.1 = (f32[128,8192]{1,0:T(8,128)}, f32[8,128]{1,0:T(8,128)}) custom-call(s32[14]{0:T(128)} %concatenate.3.ids, f32[64]{0:T(128)} %refs_0_.1, bf16[128,8192]{1,0:T(8,128)(2,1)} %bitcast.30, bf16[64,128]{1,0:T(8,128)(2,1)} %bitcast.43, bf16[64,128]{1,0:T(8,128)(2,1)} %bitcast.41, bf16[128,512]{1,0:T(8,128)(2,1)} %bitcast.35, bf16[128,512]{1,0:T(8,128)(2,1)} %bitcast.36, ...), custom_call_target="tpu_custom_call" | custom-call | flops 34359738368 | bytes 1048576 | tf_op jit(solution)/shard_map/intra/pallas_call | solution.py:323
  46.3 0.0 collective-permute-done.6.refs_4_
  46.3 0.0 collective-permute-done.5.refs_3_.refs_5_
  46.3 5.3 %collective-permute-done.11.refs_9_.refs_17_.refs_25_.refs_33_ = bf16[2,768,128]{2,1,0:T(8,128)(2,1)S(1)} collective-permute-done((bf16[2,768,128]{2,1,0:T(8,128)(2,1)S(1)}, bf16[2,768,128]{2,1,0:T(8,128)(2,1)S(1)}, u32[]{:S(2)}, u32[]{:S(2)}) %collective-permute-start.11) | collective-permute-done | bytes 393248 | tf_op jit(solution)/shard_map/ppermute | solution.py:632
  51.6 0.0 collective-permute-done.8.refs_5_
  51.6 8.4 %collective-permute-done.12.refs_10_.refs_18_.refs_26_.refs_34_ = bf16[2,768,128]{2,1,0:T(8,128)(2,1)S(1)} collective-permute-done((bf16[2,768,128]{2,1,0:T(8,128)(2,1)S(1)}, bf16[2,768,128]{2,1,0:T(8,128)(2,1)S(1)}, u32[]{:S(2)}, u32[]{:S(2)}) %collective-permute-start.12) | collective-permute-done | bytes 393248 | tf_op jit(solution)/shard_map/ppermute | solution.py:632
  60.0 0.0 all-to-all-done.refs_0_
  60.1 1.1 %copy-done.18 = f32[3,256,128]{2,1,0:T(8,128)S(1)} copy-done((f32[3,256,128]{2,1,0:T(8,128)S(1)}, f32[3,256,128]{2,1,0:T(8,128)}, u32[]{:S(2)}) %copy-start.18) | copy-done | bytes 393240
  61.2 0.7 copy-done.20
  61.9 1.6 %recurrence.1 = (bf16[8,256,128]{2,1,0:T(8,128)(2,1)}, f32[8,128]{1,0:T(8,128)S(1)}) custom-call(s32[14]{0:T(128)S(1)} %copy-done.11, bf16[8,272,128]{2,1,0:T(8,128)(2,1)S(1)} %all-to-all-done.refs_0_, f32[3,256,128]{2,1,0:T(8,128)S(1)} %copy-done.18, f32[8,128]{1,0:T(8,128)S(1)} %copy-done.20, bf16[8,272,128]{2,1,0:T(8,128)(2,1)} %collective-permute-done.5.refs_3_.refs_5_, ...), custom_call_target="tpu_custom_call" | custom-call | flops 34359738368 | bytes 1048576 | tf_op jit(solution)/shard_map/recurrence/pallas_call | solution.py:173
  63.5 5.2 %all-to-all-start.1 = ((bf16[8,256,128]{2,1,0:T(8,128)(2,1)}), bf16[8,256,128]{2,1,0:T(8,128)(2,1)S(1)}, u32[]{:S(2)}, u32[]{:S(2)}) async-start(bf16[8,256,128]{2,1,0:T(8,128)(2,1)} %get-tuple-element.30), calls=%async_computation.1 | async-start | bytes 1048576 | tf_op jit(solution)/shard_map/all_to_all | solution.py:635
  68.6 1.1 %collective-permute-start.13 = (bf16[2,768,128]{2,1,0:T(8,128)(2,1)S(1)}, bf16[2,768,128]{2,1,0:T(8,128)(2,1)S(1)}, u32[]{:S(2)}, u32[]{:S(2)}) collective-permute-start(bf16[2,768,128]{2,1,0:T(8,128)(2,1)S(1)} %get-tuple-element.25.refs_2_.refs_7_.refs_15_.refs_23_.refs_31_), channel_id=1, source_target_pairs={{0,1},{1,0},{2,3},{3,2},{4,5},{5,4},{6,7},{7,6},{8,9},{9,8},{10,11... | collective-permute-start | bytes 1179656 | tf_op jit(solution)/shard_map/ppermute | solution.py:632
  69.7 0.1 collective-permute-start.15
  69.8 0.4 collective-permute-start.14
  70.2 0.1 collective-permute-start.16
  70.3 0.7 collective-permute-done.13.refs_11_.refs_19_.refs_27_.refs_35_
  71.0 0.6 collective-permute-done.15.refs_13_.refs_21_.refs_29_.refs_37_
  71.6 0.6 collective-permute-done.14.refs_12_.refs_20_.refs_28_.refs_36_
  72.2 0.6 collective-permute-done.16.refs_14_.refs_22_.refs_30_.refs_38_
  72.7 0.8 copy-done.24
  73.5 20.2 %attend.1 = (bf16[128,4096]{1,0:T(8,128)(2,1)}, f32[8,128]{1,0:T(8,128)}) custom-call(s32[14]{0:T(128)} %concatenate.3.ids, bf16[128,4096]{1,0:T(8,128)(2,1)} %bitcast.23, bf16[2,128,512]{2,1,0:T(8,128)(2,1)} %copy-done.5, bf16[2,128,512]{2,1,0:T(8,128)(2,1)} %copy-done.26, bf16[2,128,512]{2,1,0:T(8,128)(2,1)} %get-tuple-element.24.refs_4_.refs_3_, ...), custom_call_target="tpu_custom_call" | custom-call | flops 1024 | bytes 1024 | tf_op jit(solution)/shard_map/attend/pallas_call | solution.py:563
  93.7 0.0 all-to-all-done.1.refs_0_
  93.7 0.7 copy-done.16
  94.4 0.6 copy.20.refs_3_
  95.0 0.1 collective-permute-start.17
  95.1 1.9 %collective-permute-done.17.refs_4_ = bf16[8,256,128]{2,1,0:T(8,128)(2,1)S(1)} collective-permute-done((bf16[8,256,128]{2,1,0:T(8,128)(2,1)S(1)}, bf16[8,256,128]{2,1,0:T(8,128)(2,1)S(1)}, u32[]{:S(2)}, u32[]{:S(2)}) %collective-permute-start.17) | collective-permute-done | bytes 524320 | tf_op jit(solution)/shard_map/ppermute | solution.py:632
  97.0 0.8 copy-done.27
  97.8 7.4 %finish.1 = bf16[128,8192]{1,0:T(8,128)(2,1)} custom-call(s32[14]{0:T(128)} %concatenate.3.ids, f32[128,8192]{1,0:T(8,128)} %get-tuple-element.26.refs_0_, bf16[64,128]{1,0:T(8,128)(2,1)} %bitcast.44, bf16[128,512]{1,0:T(8,128)(2,1)} %bitcast.37, bf16[8,256,128]{2,1,0:T(8,128)(2,1)} %copy-done.15, bf16[8,256,128]{2,1,0:T(8,128)(2,1)} %copy-done.27, ...), custom_call_target="tpu_custom_call" | custom-call | flops 34359738368 | bytes 1048576 | tf_op jit(solution)/shard_map/finish/pallas_call | solution.py:411
  (45 shorter events, 0.1 us)
Async XLA Ops:
  0.6 16.9 %collective-permute-start.2 = (f32[3,4,8192]{2,1,0:T(4,128)}, f32[3,4,8192]{2,1,0:T(4,128)}, u32[]{:S(2)}, u32[]{:S(2)}) collective-permute-start(f32[3,4,8192]{2,1,0:T(4,128)} %bitcast.24), channel_id=1, source_target_pairs={{16,0},{0,16},{17,1},{1,17},{18,2},{2,18},{19,3},{3,19},{20,4},{4,... | collective-permute-start | bytes 1179656 | tf_op jit(solution)/shard_map/ppermute | solution.py:640
  4.6 17.4 %collective-permute-start.1 = (bf16[1,512,128]{2,1,0:T(8,128)(2,1)}, bf16[1,512,128]{2,1,0:T(8,128)(2,1)S(1)}, u32[]{:S(2)}, u32[]{:S(2)}) collective-permute-start(bf16[1,512,128]{2,1,0:T(8,128)(2,1)} %get-tuple-element.18.refs_4_), channel_id=1, source_target_pairs={{0,8},{1,9},{2,10},{3,11},{4,12},{5,13},{6,14},{7,15},{8,0},{9,1},... | collective-permute-start | bytes 393224 | tf_op jit(solution)/shard_map/ppermute | solution.py:632
  7.1 15.1 %collective-permute-start.4 = (bf16[2,128,512]{2,1,0:T(8,128)(2,1)}, bf16[2,128,512]{2,1,0:T(8,128)(2,1)S(1)}, u32[]{:S(2)}, u32[]{:S(2)}) collective-permute-start(bf16[2,128,512]{2,1,0:T(8,128)(2,1)} %get-tuple-element.24.refs_4_.refs_3_), channel_id=1, source_target_pairs={{0,4},{1,5},{2,6},{3,7},{4,8},{5,9},{6,10},{7,11},{8,12},{9,13},{1... | collective-permute-start | bytes 786440 | tf_op jit(solution)/shard_map/ppermute | solution.py:596
  10.4 6.8 %copy-start.25 = (f32[1,3,4,8192]{3,2,1,0:T(4,128)S(1)}, f32[1,3,4,8192]{3,2,1,0:T(4,128)}, u32[]{:S(2)}) copy-start(f32[1,3,4,8192]{3,2,1,0:T(4,128)} %param.23) | copy-start | bytes 1179652
  15.6 3.3 %copy-start.10 = (s32[14]{0:T(128)S(1)}, s32[14]{0:T(128)}, u32[]{:S(2)}) copy-start(s32[14]{0:T(128)} %concatenate.3.ids) | copy-start | bytes 172
  15.6 11.9 %collective-permute-start = (bf16[8,272,128]{2,1,0:T(8,128)(2,1)}, bf16[8,272,128]{2,1,0:T(8,128)(2,1)S(1)}, u32[]{:S(2)}, u32[]{:S(2)}) collective-permute-start(bf16[8,272,128]{2,1,0:T(8,128)(2,1)} %get-tuple-element.20.refs_2_), channel_id=1, source_target_pairs={{0,1},{1,0},{2,3},{3,2},{4,5},{5,4},{6,7},{7,6},{8,9},{9,8},{10,11... | collective-permute-start | bytes 1671176 | tf_op jit(solution)/shard_map/ppermute | solution.py:632
  19.0 1.1 %copy-start.14 = (bf16[8,272,128]{2,1,0:T(8,128)(2,1)S(1)}, bf16[8,272,128]{2,1,0:T(8,128)(2,1)}, u32[]{:S(2)}) copy-start(bf16[8,272,128]{2,1,0:T(8,128)(2,1)} %get-tuple-element.20.refs_2_) | copy-start | bytes 1671172
  20.0 1.7 %copy-start.4 = (bf16[2,128,512]{2,1,0:T(8,128)(2,1)S(1)}, bf16[2,128,512]{2,1,0:T(8,128)(2,1)}, u32[]{:S(2)}) copy-start(bf16[2,128,512]{2,1,0:T(8,128)(2,1)} %get-tuple-element.24.refs_4_.refs_3_) | copy-start | bytes 786436
  20.0 7.5 %copy-start.19 = (bf16[1,512,128]{2,1,0:T(8,128)(2,1)S(1)}, bf16[1,512,128]{2,1,0:T(8,128)(2,1)}, u32[]{:S(2)}) copy-start(bf16[1,512,128]{2,1,0:T(8,128)(2,1)} %get-tuple-element.21.refs_0_) | copy-start | bytes 393220
  20.9 0.8 copy-start.17
  21.7 5.8 %collective-permute-start.3 = (bf16[1,256,128]{2,1,0:T(8,128)(2,1)S(1)}, bf16[1,256,128]{2,1,0:T(8,128)(2,1)S(1)}, u32[]{:S(2)}, u32[]{:S(2)}) collective-permute-start(bf16[1,256,128]{2,1,0:T(8,128)(2,1)S(1)} %get-tuple-element.23), channel_id=1, source_target_pairs={{0,8},{1,9},{2,10},{3,11},{4,12},{5,13},{6,14},{7,15},{8,0},{9,1},... | collective-permute-start | bytes 196616 | tf_op jit(solution)/shard_map/ppermute | solution.py:632
  21.7 13.9 %collective-permute-start.9 = (bf16[2,128,512]{2,1,0:T(8,128)(2,1)S(1)}, bf16[2,128,512]{2,1,0:T(8,128)(2,1)S(1)}, u32[]{:S(2)}, u32[]{:S(2)}) collective-permute-start(bf16[2,128,512]{2,1,0:T(8,128)(2,1)S(1)} %copy-done.4), channel_id=1, source_target_pairs={{0,1},{1,0},{2,3},{3,2},{4,5},{5,4},{6,7},{7,6},{8,9},{9,8},{10,11... | collective-permute-start | bytes 786440 | tf_op jit(solution)/shard_map/ppermute | solution.py:632
  22.0 24.3 %collective-permute-start.5 = (bf16[8,272,128]{2,1,0:T(8,128)(2,1)}, bf16[8,272,128]{2,1,0:T(8,128)(2,1)}, u32[]{:S(2)}, u32[]{:S(2)}) collective-permute-start(bf16[8,272,128]{2,1,0:T(8,128)(2,1)} %get-tuple-element.19.refs_0_), channel_id=1, source_target_pairs={{0,1},{1,0},{2,3},{3,2},{4,5},{5,4},{6,7},{7,6},{8,9},{9,8},{10,11... | collective-permute-start | bytes 1671176 | tf_op jit(solution)/shard_map/ppermute | solution.py:632
  22.2 5.9 %copy-start.5 = (bf16[2,128,512]{2,1,0:T(8,128)(2,1)}, bf16[2,128,512]{2,1,0:T(8,128)(2,1)S(1)}, u32[]{:S(2)}) copy-start(bf16[2,128,512]{2,1,0:T(8,128)(2,1)S(1)} %collective-permute-done.4.refs_5_.refs_1_) | copy-start | bytes 786436
  22.2 24.1 %collective-permute-start.6 = (bf16[2,128,512]{2,1,0:T(8,128)(2,1)S(1)}, bf16[2,128,512]{2,1,0:T(8,128)(2,1)S(1)}, u32[]{:S(2)}, u32[]{:S(2)}) collective-permute-start(bf16[2,128,512]{2,1,0:T(8,128)(2,1)S(1)} %collective-permute-done.4.refs_5_.refs_1_), channel_id=1, source_target_pairs={{0,1},{1,0},{2,3},{3,2},{4,5},{5,4},{6,7},{7,6},{8,9},{9,8},{10,11... | collective-permute-start | bytes 786440 | tf_op jit(solution)/shard_map/ppermute | solution.py:632
  27.5 1.9 %copy-start.13 = (bf16[8,272,128]{2,1,0:T(8,128)(2,1)}, bf16[8,272,128]{2,1,0:T(8,128)(2,1)S(1)}, u32[]{:S(2)}) copy-start(bf16[8,272,128]{2,1,0:T(8,128)(2,1)S(1)} %collective-permute-done.refs_6_.refs_1_) | copy-start | bytes 1671172
  28.1 40.5 %copy-start = (bf16[2,768,128]{2,1,0:T(8,128)(2,1)}, bf16[2,768,128]{2,1,0:T(8,128)(2,1)S(1)}, u32[]{:S(2)}) copy-start(bf16[2,768,128]{2,1,0:T(8,128)(2,1)S(1)} %get-tuple-element.25.refs_2_.refs_7_.refs_15_.refs_23_.refs_31_) | copy-start | bytes 1179652
  28.1 8.9 %collective-permute-start.7 = (bf16[2,128,512]{2,1,0:T(8,128)(2,1)S(1)}, bf16[2,128,512]{2,1,0:T(8,128)(2,1)S(1)}, u32[]{:S(2)}, u32[]{:S(2)}) collective-permute-start(bf16[2,128,512]{2,1,0:T(8,128)(2,1)S(1)} %get-tuple-element.29), channel_id=1, source_target_pairs={{0,2},{1,3},{2,0},{3,1},{4,6},{5,7},{6,4},{7,5},{8,10},{9,11},{10,... | collective-permute-start | bytes 786440 | tf_op jit(solution)/shard_map/ppermute | solution.py:632
  29.4 9.9 %collective-permute-start.10 = (bf16[2,768,128]{2,1,0:T(8,128)(2,1)S(1)}, bf16[2,768,128]{2,1,0:T(8,128)(2,1)S(1)}, u32[]{:S(2)}, u32[]{:S(2)}) collective-permute-start(bf16[2,768,128]{2,1,0:T(8,128)(2,1)S(1)} %get-tuple-element.25.refs_2_.refs_7_.refs_15_.refs_23_.refs_31_), channel_id=1, source_target_pairs={{0,4},{1,5},{2,6},{3,7},{4,0},{5,1},{6,2},{7,3},{8,12},{9,13},{10,... | collective-permute-start | bytes 1179656 | tf_op jit(solution)/shard_map/ppermute | solution.py:632
  32.1 28.0 %all-to-all-start = ((bf16[8,272,128]{2,1,0:T(8,128)(2,1)}), bf16[8,272,128]{2,1,0:T(8,128)(2,1)S(1)}, u32[]{:S(2)}, u32[]{:S(2)}) async-start(bf16[8,272,128]{2,1,0:T(8,128)(2,1)} %combine.1.refs_6_), calls=%async_computation | async-start | bytes 1114112 | tf_op jit(solution)/shard_map/all_to_all | solution.py:635
  35.6 24.4 %copy-start.6 = (bf16[2,128,512]{2,1,0:T(8,128)(2,1)}, bf16[2,128,512]{2,1,0:T(8,128)(2,1)S(1)}, u32[]{:S(2)}) copy-start(bf16[2,128,512]{2,1,0:T(8,128)(2,1)S(1)} %collective-permute-done.9.refs_6_) | copy-start | bytes 786436
  35.6 16.0 %collective-permute-start.11 = (bf16[2,768,128]{2,1,0:T(8,128)(2,1)S(1)}, bf16[2,768,128]{2,1,0:T(8,128)(2,1)S(1)}, u32[]{:S(2)}, u32[]{:S(2)}) collective-permute-start(bf16[2,768,128]{2,1,0:T(8,128)(2,1)S(1)} %get-tuple-element.25.refs_2_.refs_7_.refs_15_.refs_23_.refs_31_), channel_id=1, source_target_pairs={{0,2},{1,3},{2,0},{3,1},{4,6},{5,7},{6,4},{7,5},{8,10},{9,11},{10,... | collective-permute-start | bytes 1179656 | tf_op jit(solution)/shard_map/ppermute | solution.py:632
  37.0 9.3 %copy-start.26 = (bf16[2,128,512]{2,1,0:T(8,128)(2,1)}, bf16[2,128,512]{2,1,0:T(8,128)(2,1)S(1)}, u32[]{:S(2)}) copy-start(bf16[2,128,512]{2,1,0:T(8,128)(2,1)S(1)} %collective-permute-done.7.refs_2_) | copy-start | bytes 786436
  37.1 14.6 %collective-permute-start.8 = (bf16[2,128,512]{2,1,0:T(8,128)(2,1)S(1)}, bf16[2,128,512]{2,1,0:T(8,128)(2,1)S(1)}, u32[]{:S(2)}, u32[]{:S(2)}) collective-permute-start(bf16[2,128,512]{2,1,0:T(8,128)(2,1)S(1)} %collective-permute-done.7.refs_2_), channel_id=1, source_target_pairs={{0,1},{1,0},{2,3},{3,2},{4,5},{5,4},{6,7},{7,6},{8,9},{9,8},{10,11... | collective-permute-start | bytes 786440 | tf_op jit(solution)/shard_map/ppermute | solution.py:632
  39.3 30.4 %copy-start.1 = (bf16[2,768,128]{2,1,0:T(8,128)(2,1)}, bf16[2,768,128]{2,1,0:T(8,128)(2,1)S(1)}, u32[]{:S(2)}) copy-start(bf16[2,768,128]{2,1,0:T(8,128)(2,1)S(1)} %collective-permute-done.10.refs_8_.refs_16_.refs_24_.refs_32_) | copy-start | bytes 1179652
  39.4 20.7 %collective-permute-start.12 = (bf16[2,768,128]{2,1,0:T(8,128)(2,1)S(1)}, bf16[2,768,128]{2,1,0:T(8,128)(2,1)S(1)}, u32[]{:S(2)}, u32[]{:S(2)}) collective-permute-start(bf16[2,768,128]{2,1,0:T(8,128)(2,1)S(1)} %collective-permute-done.10.refs_8_.refs_16_.refs_24_.refs_32_), channel_id=1, source_target_pairs={{0,2},{1,3},{2,0},{3,1},{4,6},{5,7},{6,4},{7,5},{8,10},{9,11},{10,... | collective-permute-start | bytes 1179656 | tf_op jit(solution)/shard_map/ppermute | solution.py:632
  39.6 20.5 %copy-start.11 = (s32[14]{0:T(128)S(1)}, s32[14]{0:T(128)}, u32[]{:S(2)}) copy-start(s32[14]{0:T(128)} %concatenate.3.ids) | copy-start | bytes 172
  46.3 17.1 %copy-start.7 = (bf16[2,128,512]{2,1,0:T(8,128)(2,1)}, bf16[2,128,512]{2,1,0:T(8,128)(2,1)S(1)}, u32[]{:S(2)}) copy-start(bf16[2,128,512]{2,1,0:T(8,128)(2,1)S(1)} %collective-permute-done.6.refs_4_) | copy-start | bytes 786436
  51.6 18.1 %copy-start.2 = (bf16[2,768,128]{2,1,0:T(8,128)(2,1)}, bf16[2,768,128]{2,1,0:T(8,128)(2,1)S(1)}, u32[]{:S(2)}) copy-start(bf16[2,768,128]{2,1,0:T(8,128)(2,1)S(1)} %collective-permute-done.11.refs_9_.refs_17_.refs_25_.refs_33_) | copy-start | bytes 1179652
  51.6 11.8 %copy-start.8 = (bf16[2,128,512]{2,1,0:T(8,128)(2,1)}, bf16[2,128,512]{2,1,0:T(8,128)(2,1)S(1)}, u32[]{:S(2)}) copy-start(bf16[2,128,512]{2,1,0:T(8,128)(2,1)S(1)} %collective-permute-done.8.refs_5_) | copy-start | bytes 786436
  60.0 10.2 %copy-start.3 = (bf16[2,768,128]{2,1,0:T(8,128)(2,1)}, bf16[2,768,128]{2,1,0:T(8,128)(2,1)S(1)}, u32[]{:S(2)}) copy-start(bf16[2,768,128]{2,1,0:T(8,128)(2,1)S(1)} %collective-permute-done.12.refs_10_.refs_18_.refs_26_.refs_34_) | copy-start | bytes 1179652
  60.1 1.1 %copy-start.18 = (f32[3,256,128]{2,1,0:T(8,128)S(1)}, f32[3,256,128]{2,1,0:T(8,128)}, u32[]{:S(2)}) copy-start(f32[3,256,128]{2,1,0:T(8,128)} %copy-done.17) | copy-start | bytes 1179652
  61.2 0.7 copy-start.20
  63.5 10.1 %copy-start.9 = (f32[8,128]{1,0:T(8,128)}, f32[8,128]{1,0:T(8,128)S(1)}, u32[]{:S(2)}) copy-start(f32[8,128]{1,0:T(8,128)S(1)} %get-tuple-element.31.refs_41_) | copy-start | bytes 12292
  63.5 30.3 %all-to-all-start.1 = ((bf16[8,256,128]{2,1,0:T(8,128)(2,1)}), bf16[8,256,128]{2,1,0:T(8,128)(2,1)S(1)}, u32[]{:S(2)}, u32[]{:S(2)}) async-start(bf16[8,256,128]{2,1,0:T(8,128)(2,1)} %get-tuple-element.30), calls=%async_computation.1 | async-start | bytes 1048576 | tf_op jit(solution)/shard_map/all_to_all | solution.py:635
  68.6 2.4 %collective-permute-start.13 = (bf16[2,768,128]{2,1,0:T(8,128)(2,1)S(1)}, bf16[2,768,128]{2,1,0:T(8,128)(2,1)S(1)}, u32[]{:S(2)}, u32[]{:S(2)}) collective-permute-start(bf16[2,768,128]{2,1,0:T(8,128)(2,1)S(1)} %get-tuple-element.25.refs_2_.refs_7_.refs_15_.refs_23_.refs_31_), channel_id=1, source_target_pairs={{0,1},{1,0},{2,3},{3,2},{4,5},{5,4},{6,7},{7,6},{8,9},{9,8},{10,11... | collective-permute-start | bytes 1179656 | tf_op jit(solution)/shard_map/ppermute | solution.py:632
  69.7 1.9 %collective-permute-start.15 = (bf16[2,768,128]{2,1,0:T(8,128)(2,1)S(1)}, bf16[2,768,128]{2,1,0:T(8,128)(2,1)S(1)}, u32[]{:S(2)}, u32[]{:S(2)}) collective-permute-start(bf16[2,768,128]{2,1,0:T(8,128)(2,1)S(1)} %collective-permute-done.11.refs_9_.refs_17_.refs_25_.refs_33_), channel_id=1, source_target_pairs={{0,1},{1,0},{2,3},{3,2},{4,5},{5,4},{6,7},{7,6},{8,9},{9,8},{10,11... | collective-permute-start | bytes 1179656 | tf_op jit(solution)/shard_map/ppermute | solution.py:632
  69.8 2.4 %collective-permute-start.14 = (bf16[2,768,128]{2,1,0:T(8,128)(2,1)S(1)}, bf16[2,768,128]{2,1,0:T(8,128)(2,1)S(1)}, u32[]{:S(2)}, u32[]{:S(2)}) collective-permute-start(bf16[2,768,128]{2,1,0:T(8,128)(2,1)S(1)} %collective-permute-done.10.refs_8_.refs_16_.refs_24_.refs_32_), channel_id=1, source_target_pairs={{0,1},{1,0},{2,3},{3,2},{4,5},{5,4},{6,7},{7,6},{8,9},{9,8},{10,11... | collective-permute-start | bytes 1179656 | tf_op jit(solution)/shard_map/ppermute | solution.py:632
  70.2 2.5 %collective-permute-start.16 = (bf16[2,768,128]{2,1,0:T(8,128)(2,1)S(1)}, bf16[2,768,128]{2,1,0:T(8,128)(2,1)S(1)}, u32[]{:S(2)}, u32[]{:S(2)}) collective-permute-start(bf16[2,768,128]{2,1,0:T(8,128)(2,1)S(1)} %collective-permute-done.12.refs_10_.refs_18_.refs_26_.refs_34_), channel_id=1, source_target_pairs={{0,1},{1,0},{2,3},{3,2},{4,5},{5,4},{6,7},{7,6},{8,9},{9,8},{10,11... | collective-permute-start | bytes 1179656 | tf_op jit(solution)/shard_map/ppermute | solution.py:632
  71.0 2.5 %copy-start.21 = (bf16[2,768,128]{2,1,0:T(8,128)(2,1)}, bf16[2,768,128]{2,1,0:T(8,128)(2,1)S(1)}, u32[]{:S(2)}) copy-start(bf16[2,768,128]{2,1,0:T(8,128)(2,1)S(1)} %collective-permute-done.13.refs_11_.refs_19_.refs_27_.refs_35_) | copy-start | bytes 1179652
  71.6 1.9 %copy-start.22 = (bf16[2,768,128]{2,1,0:T(8,128)(2,1)}, bf16[2,768,128]{2,1,0:T(8,128)(2,1)S(1)}, u32[]{:S(2)}) copy-start(bf16[2,768,128]{2,1,0:T(8,128)(2,1)S(1)} %collective-permute-done.15.refs_13_.refs_21_.refs_29_.refs_37_) | copy-start | bytes 1179652
  72.2 1.4 %copy-start.23 = (bf16[2,768,128]{2,1,0:T(8,128)(2,1)}, bf16[2,768,128]{2,1,0:T(8,128)(2,1)S(1)}, u32[]{:S(2)}) copy-start(bf16[2,768,128]{2,1,0:T(8,128)(2,1)S(1)} %collective-permute-done.14.refs_12_.refs_20_.refs_28_.refs_36_) | copy-start | bytes 1179652
  72.7 0.8 copy-start.24
  73.5 20.2 %copy-start.12 = (s32[14]{0:T(128)S(1)}, s32[14]{0:T(128)}, u32[]{:S(2)}) copy-start(s32[14]{0:T(128)} %concatenate.3.ids) | copy-start | bytes 172
  93.7 0.7 copy-start.16
  95.0 2.0 %copy-start.15 = (bf16[8,256,128]{2,1,0:T(8,128)(2,1)}, bf16[8,256,128]{2,1,0:T(8,128)(2,1)S(1)}, u32[]{:S(2)}) copy-start(bf16[8,256,128]{2,1,0:T(8,128)(2,1)S(1)} %copy.20.refs_3_) | copy-start | bytes 1572868
  95.0 2.0 %collective-permute-start.17 = (bf16[8,256,128]{2,1,0:T(8,128)(2,1)S(1)}, bf16[8,256,128]{2,1,0:T(8,128)(2,1)S(1)}, u32[]{:S(2)}, u32[]{:S(2)}) collective-permute-start(bf16[8,256,128]{2,1,0:T(8,128)(2,1)S(1)} %copy.20.refs_3_), channel_id=1, source_target_pairs={{0,1},{1,0},{2,3},{3,2},{4,5},{5,4},{6,7},{7,6},{8,9},{9,8},{10,11... | collective-permute-start | bytes 1572872 | tf_op jit(solution)/shard_map/ppermute | solution.py:632
  97.0 0.8 copy-start.27

commit v2 on v1

--- a/solution.py
+++ b/solution.py
@@ -653,9 +653,6 @@
     moved = apart(away, devices // 2)
     four = shifted(key_value, "ctx", 4)
 
-    keep, send = summaries(meta, x, rates, steps, writes, local, away)
-    got = apart(send, 1)
-
     one = (1, width, P_SIZE)
     home, away, restored = whole(
         scalars(restore_kernel, local, devices // 2, groups),
@@ -663,16 +660,19 @@
         meta,
         stored,
         [(one, jnp.bfloat16), (one, jnp.bfloat16), ((SEQS, width, P_SIZE), jnp.float32)],
-        idle=[send],
+        idle=[key_value],
     )
     away = apart(away, devices // 2)
+    keep, send = summaries(meta, x, rates, steps, writes, local, home)
+    got = apart(send, 1)
+
     near, two = whole(
         scalars(join_two_kernel),
         "join_two",
         meta,
         [near, moved, home, away, key_value, four],
         [((2, parcel[1] + width, HD), jnp.bfloat16), (band, jnp.bfloat16)],
-        idle=[got],
+        idle=[send],
     )
     distance = devices // 4
     while distance > 4:

time: 107 us -> 112 us (1.047)
  starting transfers between devices: 22.8 us -> 37.7 us
  Pallas kernels: 48.3 us -> 43.2 us
  waiting for transfers between devices: 24 us -> 19.2 us
    ppermute x16, starting transfers between devices: 10.9 us -> 24.8 us  [apart(): lax.ppermute(block, 'ctx', [(i, i ^ distance) for i in range(devices)])]
    ppermute x16, waiting for transfers between devices: 24 us -> 18.3 us  [apart(): lax.ppermute(block, 'ctx', [(i, i ^ distance) for i in range(devices)])]
    pallas_call x1, Pallas kernels: 20.2 us -> 15 us  [attend(): pl.pallas_call(scalars(attend_kernel), out_shape=[jax.ShapeDtypeStruct((T...]
    unnamed x56 -> x60, local copies, waits for them, and re-layouts: 6 us -> 7.13 us
  transfers between devices with their start and end apart: 20 -> 20, of which waited for: 9 -> 9; matrix products, arithmetic and copies ran while one was open for 3% -> 2% of each run, Pallas kernels for 37% -> 31%
where the time goes in v2:
time: 112 us; the launch traced here: 110 us
  Pallas kernels  43.2 us (39%)
  starting transfers between devices  37.7 us (34%)
  waiting for transfers between devices  19.2 us (17%)
  local copies, waits for them, and re-layouts  9.26 us (8%)
    ppermute x16, starting transfers between devices, apart(): lax.ppermute(block, 'ctx', [(i, i ^ distance) for i in range(devices)])  24.8 us
    ppermute x16, waiting for transfers between devices, apart(): lax.ppermute(block, 'ctx', [(i, i ^ distance) for i in range(devices)])  18.3 us
    pallas_call x1, Pallas kernels, attend(): pl.pallas_call(scalars(attend_kernel), out_shape=[jax.ShapeDtypeStruct((T...  15 us
    pallas_call x6, Pallas kernels, whole(): pl.pallas_call(kernel, out_shape=[jax.ShapeDtypeStruct(s, t) for s, t in...  8.8 us
    all_to_all x2, starting transfers between devices, exchanged(): lax.all_to_all(block, 'ctx', 0, 0, axis_index_groups=same_core, tiled=True)  8.57 us
    pallas_call x1, Pallas kernels, finish(): pl.pallas_call(scalars(finish_kernel, local), out_shape=jax.ShapeDtypeStr...  7.42 us
    unnamed x60, local copies, waits for them, and re-layouts  7.13 us
    pallas_call x1, Pallas kernels, intra(): pl.pallas_call(scalars(intra_kernel), out_shape=[jax.ShapeDtypeStruct((TO...  6.75 us
  transfers between devices with their start and end apart: 20, of which 9 were waited for; matrix products, arithmetic and copies ran while one was open for 2% of the time, Pallas kernels for 31%

profile of v2, /device:TPU:3, one launch (start us, length us, event | category | flops | bytes accessed | tf_op | source)
XLA Modules:
  0.0 110.3 jit_solution(9842943936326941951)
XLA Ops:
  0.6 0.1 collective-permute-start
  0.7 1.3 %concatenate.3.ids = s32[14]{0:T(128)} concatenate(s32[1]{0:T(128)} %bitcast, s32[1]{0:T(128)} %bitcast.1, s32[3]{0:T(128)} %bitcast.27, s32[3]{0:T(128)} %bitcast.28, s32[6]{0:T(128)} %param.24), dimensions={0} | concatenate | bytes 112 | tf_op jit(solution)/shard_map/concatenate | solution.py:626
  2.0 2.7 %pack.1 = (bf16[1,512,128]{2,1,0:T(8,128)(2,1)}, bf16[1,512,128]{2,1,0:T(8,128)(2,1)}, bf16[2,128,512]{2,1,0:T(8,128)(2,1)}) custom-call(s32[14]{0:T(128)} %concatenate.3.ids, bf16[3,32,512]{2,1,0:T(8,128)(2,1)} %bitcast.38, bf16[3,32,512]{2,1,0:T(8,128)(2,1)} %bitcast.39, bf16[128,512]{1,0:T(8,128)(2,1)} %bitcast.32, bf16[128,512]{1,0:T(8,128)(2,1)} %bitcast.33), custom_call_target="tpu_custom_call" | custom-call | flops 34359738368 | bytes 1048576 | tf_op jit(solution)/shard_map/pack/pallas_call | solution.py:173
  4.7 4.2 %collective-permute-start.4 = (bf16[2,128,512]{2,1,0:T(8,128)(2,1)}, bf16[2,128,512]{2,1,0:T(8,128)(2,1)}, u32[]{:S(2)}, u32[]{:S(2)}) collective-permute-start(bf16[2,128,512]{2,1,0:T(8,128)(2,1)} %get-tuple-element.18.refs_2_.refs_4_.refs_3_), channel_id=1, source_target_pairs={{0,4},{1,5},{2,6},{3,7},{4,8},{5,9},{6,10},{7,11},{8,12},{9,13},{1... | collective-permute-start | bytes 786440 | tf_op jit(solution)/shard_map/ppermute | solution.py:596
  9.0 1.2 %collective-permute-start.9 = (bf16[2,128,512]{2,1,0:T(8,128)(2,1)}, bf16[2,128,512]{2,1,0:T(8,128)(2,1)S(1)}, u32[]{:S(2)}, u32[]{:S(2)}) collective-permute-start(bf16[2,128,512]{2,1,0:T(8,128)(2,1)} %get-tuple-element.18.refs_2_.refs_4_.refs_3_), channel_id=1, source_target_pairs={{0,1},{1,0},{2,3},{3,2},{4,5},{5,4},{6,7},{7,6},{8,9},{9,8},{10,11... | collective-permute-start | bytes 786440 | tf_op jit(solution)/shard_map/ppermute | solution.py:632
  10.2 1.7 %collective-permute-start.2 = (bf16[1,512,128]{2,1,0:T(8,128)(2,1)}, bf16[1,512,128]{2,1,0:T(8,128)(2,1)S(1)}, u32[]{:S(2)}, u32[]{:S(2)}) collective-permute-start(bf16[1,512,128]{2,1,0:T(8,128)(2,1)} %get-tuple-element.23), channel_id=1, source_target_pairs={{0,8},{1,9},{2,10},{3,11},{4,12},{5,13},{6,14},{7,15},{8,0},{9,1},... | collective-permute-start | bytes 393224 | tf_op jit(solution)/shard_map/ppermute | solution.py:632
  11.9 0.4 reshape_squeeze.3.refs_0_
  12.3 0.9 collective-permute-done.4.refs_5_.refs_1_
  13.2 3.3 %collective-permute-start.6 = (bf16[2,128,512]{2,1,0:T(8,128)(2,1)}, bf16[2,128,512]{2,1,0:T(8,128)(2,1)}, u32[]{:S(2)}, u32[]{:S(2)}) collective-permute-start(bf16[2,128,512]{2,1,0:T(8,128)(2,1)} %collective-permute-done.4.refs_5_.refs_1_), channel_id=1, source_target_pairs={{0,1},{1,0},{2,3},{3,2},{4,5},{5,4},{6,7},{7,6},{8,9},{9,8},{10,11... | collective-permute-start | bytes 786440 | tf_op jit(solution)/shard_map/ppermute | solution.py:632
  16.5 0.0 collective-permute-done
  16.5 0.4 reshape.7.refs_1_
  16.9 0.8 restore.1
  17.8 0.8 copy-done.18
  18.6 0.6 copy-done.21
  19.2 6.0 %collective-permute-start.3 = (bf16[1,256,128]{2,1,0:T(8,128)(2,1)S(1)}, bf16[1,256,128]{2,1,0:T(8,128)(2,1)S(1)}, u32[]{:S(2)}, u32[]{:S(2)}) collective-permute-start(bf16[1,256,128]{2,1,0:T(8,128)(2,1)S(1)} %get-tuple-element.24), channel_id=1, source_target_pairs={{0,8},{1,9},{2,10},{3,11},{4,12},{5,13},{6,14},{7,15},{8,0},{9,1},... | collective-permute-start | bytes 196616 | tf_op jit(solution)/shard_map/ppermute | solution.py:632
  25.2 5.2 %summaries.1 = (bf16[8,272,128]{2,1,0:T(8,128)(2,1)}, bf16[8,272,128]{2,1,0:T(8,128)(2,1)}) custom-call(s32[14]{0:T(128)} %concatenate.3.ids, bf16[128,8192]{1,0:T(8,128)(2,1)} %bitcast.29, bf16[64,128]{1,0:T(8,128)(2,1)} %bitcast.42, bf16[64,128]{1,0:T(8,128)(2,1)} %bitcast.40, bf16[128,512]{1,0:T(8,128)(2,1)} %bitcast.34, bf16[1,256,128]{2,1,0:T(8,128)(2,1)} %copy-done.21), custom_call_target="tpu_custom_call" | custom-call | flops 34359738368 | bytes 1048576 | tf_op jit(solution)/shard_map/summaries/pallas_call | solution.py:139
  30.4 0.3 collective-permute-start.5
  30.7 0.0 collective-permute-done.2.refs_1_
  30.7 0.2 collective-permute-start.1
  31.0 0.0 collective-permute-done.3.refs_3_
  31.0 0.0 copy-start.15
  31.0 1.0 copy-done.15
  32.0 1.5 %join_two.1 = (bf16[2,768,128]{2,1,0:T(8,128)(2,1)S(1)}, bf16[2,128,512]{2,1,0:T(8,128)(2,1)S(1)}) custom-call(s32[14]{0:T(128)S(1)} %copy-done.9, bf16[1,512,128]{2,1,0:T(8,128)(2,1)S(1)} %copy-done.20, bf16[1,512,128]{2,1,0:T(8,128)(2,1)S(1)} %collective-permute-done.2.refs_1_, bf16[1,256,128]{2,1,0:T(8,128)(2,1)S(1)} %copy-done.22, ...), custom_call_target="tpu_custom_call" | custom-call | flops 34359738368 | bytes 1048576 | tf_op jit(solution)/shard_map/join_two/pallas_call | solution.py:173
  33.6 1.3 %collective-permute-start.7 = (bf16[2,128,512]{2,1,0:T(8,128)(2,1)S(1)}, bf16[2,128,512]{2,1,0:T(8,128)(2,1)}, u32[]{:S(2)}, u32[]{:S(2)}) collective-permute-start(bf16[2,128,512]{2,1,0:T(8,128)(2,1)S(1)} %get-tuple-element.29), channel_id=1, source_target_pairs={{0,2},{1,3},{2,0},{3,1},{4,6},{5,7},{6,4},{7,5},{8,10},{9,11},{10,... | collective-permute-start | bytes 786440 | tf_op jit(solution)/shard_map/ppermute | solution.py:632
  34.9 0.0 collective-permute-done.1.refs_1_.refs_6_
  34.9 0.0 collective-permute-start.10
  34.9 1.6 %combine.1.refs_6_ = bf16[8,272,128]{2,1,0:T(8,128)(2,1)} custom-call(s32[14]{0:T(128)S(1)} %copy-done.9, bf16[8,272,128]{2,1,0:T(8,128)(2,1)S(1)} %copy-done.14, bf16[8,272,128]{2,1,0:T(8,128)(2,1)S(1)} %collective-permute-done.1.refs_1_.refs_6_, bf16[2,768,128]{2,1,0:T(8,128)(2,1)S(1)} %get-tuple-element.25.refs_2_.refs_7_.refs_15_.refs_23_.refs_31_), custom_call_target="tpu_custom_call" | custom-call | flops 34359738368 | bytes 1048576 | tf_op jit(solution)/shard_map/combine/pallas_call | solution.py:173
  36.5 3.5 %all-to-all-start = ((bf16[8,272,128]{2,1,0:T(8,128)(2,1)}), bf16[8,272,128]{2,1,0:T(8,128)(2,1)S(1)}, u32[]{:S(2)}, u32[]{:S(2)}) async-start(bf16[8,272,128]{2,1,0:T(8,128)(2,1)} %combine.1.refs_6_), calls=%async_computation | async-start | bytes 1114112 | tf_op jit(solution)/shard_map/all_to_all | solution.py:635
  40.1 0.0 collective-permute-done.9.refs_6_
  40.1 1.4 %collective-permute-start.11 = (bf16[2,768,128]{2,1,0:T(8,128)(2,1)S(1)}, bf16[2,768,128]{2,1,0:T(8,128)(2,1)S(1)}, u32[]{:S(2)}, u32[]{:S(2)}) collective-permute-start(bf16[2,768,128]{2,1,0:T(8,128)(2,1)S(1)} %get-tuple-element.25.refs_2_.refs_7_.refs_15_.refs_23_.refs_31_), channel_id=1, source_target_pairs={{0,2},{1,3},{2,0},{3,1},{4,6},{5,7},{6,4},{7,5},{8,10},{9,11},{10,... | collective-permute-start | bytes 1179656 | tf_op jit(solution)/shard_map/ppermute | solution.py:632
  41.5 0.0 collective-permute-done.7.refs_2_
  41.5 1.1 %collective-permute-start.8 = (bf16[2,128,512]{2,1,0:T(8,128)(2,1)}, bf16[2,128,512]{2,1,0:T(8,128)(2,1)S(1)}, u32[]{:S(2)}, u32[]{:S(2)}) collective-permute-start(bf16[2,128,512]{2,1,0:T(8,128)(2,1)} %collective-permute-done.7.refs_2_), channel_id=1, source_target_pairs={{0,1},{1,0},{2,3},{3,2},{4,5},{5,4},{6,7},{7,6},{8,9},{9,8},{10,11... | collective-permute-start | bytes 786440 | tf_op jit(solution)/shard_map/ppermute | solution.py:632
  42.6 2.4 %collective-permute-done.10.refs_8_.refs_16_.refs_24_.refs_32_ = bf16[2,768,128]{2,1,0:T(8,128)(2,1)S(1)} collective-permute-done((bf16[2,768,128]{2,1,0:T(8,128)(2,1)S(1)}, bf16[2,768,128]{2,1,0:T(8,128)(2,1)S(1)}, u32[]{:S(2)}, u32[]{:S(2)}) %collective-permute-start.10) | collective-permute-done | bytes 393248 | tf_op jit(solution)/shard_map/ppermute | solution.py:632
  45.0 1.0 collective-permute-start.12
  46.0 6.8 %intra.1 = (f32[128,8192]{1,0:T(8,128)}, f32[8,128]{1,0:T(8,128)}) custom-call(s32[14]{0:T(128)} %concatenate.3.ids, f32[64]{0:T(128)} %refs_0_.1, bf16[128,8192]{1,0:T(8,128)(2,1)} %bitcast.30, bf16[64,128]{1,0:T(8,128)(2,1)} %bitcast.43, bf16[64,128]{1,0:T(8,128)(2,1)} %bitcast.41, bf16[128,512]{1,0:T(8,128)(2,1)} %bitcast.35, bf16[128,512]{1,0:T(8,128)(2,1)} %bitcast.36, ...), custom_call_target="tpu_custom_call" | custom-call | flops 34359738368 | bytes 1048576 | tf_op jit(solution)/shard_map/intra/pallas_call | solution.py:323
  52.7 0.0 collective-permute-done.6.refs_4_
  52.7 3.5 %collective-permute-done.11.refs_9_.refs_17_.refs_25_.refs_33_ = bf16[2,768,128]{2,1,0:T(8,128)(2,1)S(1)} collective-permute-done((bf16[2,768,128]{2,1,0:T(8,128)(2,1)S(1)}, bf16[2,768,128]{2,1,0:T(8,128)(2,1)S(1)}, u32[]{:S(2)}, u32[]{:S(2)}) %collective-permute-start.11) | collective-permute-done | bytes 393248 | tf_op jit(solution)/shard_map/ppermute | solution.py:632
  56.3 0.0 collective-permute-done.5.refs_3_.refs_5_
  56.3 0.0 collective-permute-done.8.refs_5_
  56.3 8.4 %collective-permute-done.12.refs_10_.refs_18_.refs_26_.refs_34_ = bf16[2,768,128]{2,1,0:T(8,128)(2,1)S(1)} collective-permute-done((bf16[2,768,128]{2,1,0:T(8,128)(2,1)S(1)}, bf16[2,768,128]{2,1,0:T(8,128)(2,1)S(1)}, u32[]{:S(2)}, u32[]{:S(2)}) %collective-permute-start.12) | collective-permute-done | bytes 393248 | tf_op jit(solution)/shard_map/ppermute | solution.py:632
  64.7 0.0 all-to-all-done.refs_0_
  64.7 1.1 %copy-done.19 = f32[3,256,128]{2,1,0:T(8,128)S(1)} copy-done((f32[3,256,128]{2,1,0:T(8,128)S(1)}, f32[3,256,128]{2,1,0:T(8,128)}, u32[]{:S(2)}) %copy-start.19) | copy-done | bytes 393240
  65.8 0.7 copy-done.23
  66.5 1.5 %recurrence.1 = (bf16[8,256,128]{2,1,0:T(8,128)(2,1)}, f32[8,128]{1,0:T(8,128)S(1)}) custom-call(s32[14]{0:T(128)S(1)} %copy-done.10, bf16[8,272,128]{2,1,0:T(8,128)(2,1)S(1)} %all-to-all-done.refs_0_, f32[3,256,128]{2,1,0:T(8,128)S(1)} %copy-done.19, f32[8,128]{1,0:T(8,128)S(1)} %copy-done.23, ...), custom_call_target="tpu_custom_call" | custom-call | flops 34359738368 | bytes 1048576 | tf_op jit(solution)/shard_map/recurrence/pallas_call | solution.py:173
  68.1 0.6 copy-done.7
  68.6 5.0 %all-to-all-start.1 = ((bf16[8,256,128]{2,1,0:T(8,128)(2,1)}), bf16[8,256,128]{2,1,0:T(8,128)(2,1)S(1)}, u32[]{:S(2)}, u32[]{:S(2)}) async-start(bf16[8,256,128]{2,1,0:T(8,128)(2,1)} %get-tuple-element.30), calls=%async_computation.1 | async-start | bytes 1048576 | tf_op jit(solution)/shard_map/all_to_all | solution.py:635
  73.7 1.0 collective-permute-start.13
  74.7 0.1 collective-permute-start.15
  74.8 0.4 collective-permute-start.14
  75.2 0.1 collective-permute-start.16
  75.3 0.7 collective-permute-done.13.refs_11_.refs_19_.refs_27_.refs_35_
  76.1 0.6 collective-permute-done.15.refs_13_.refs_21_.refs_29_.refs_37_
  76.6 0.6 collective-permute-done.14.refs_12_.refs_20_.refs_28_.refs_36_
  77.2 0.6 collective-permute-done.16.refs_14_.refs_22_.refs_30_.refs_38_
  77.8 0.2 copy-done.26
  78.0 0.5 copy-done.27
  78.5 15.0 %attend.1 = (bf16[128,4096]{1,0:T(8,128)(2,1)}, f32[8,128]{1,0:T(8,128)}) custom-call(s32[14]{0:T(128)} %concatenate.3.ids, bf16[128,4096]{1,0:T(8,128)(2,1)} %bitcast.23, bf16[2,128,512]{2,1,0:T(8,128)(2,1)} %collective-permute-done.4.refs_5_.refs_1_, bf16[2,128,512]{2,1,0:T(8,128)(2,1)} %collective-permute-done.7.refs_2_, ...), custom_call_target="tpu_custom_call" | custom-call | flops 1024 | bytes 1024 | tf_op jit(solution)/shard_map/attend/pallas_call | solution.py:563
  93.5 0.0 all-to-all-done.1.refs_0_
  93.6 0.7 copy-done.17
  94.2 0.6 copy.20.refs_3_
  94.8 5.7 %collective-permute-start.17 = (bf16[8,256,128]{2,1,0:T(8,128)(2,1)S(1)}, bf16[8,256,128]{2,1,0:T(8,128)(2,1)S(1)}, u32[]{:S(2)}, u32[]{:S(2)}) collective-permute-start(bf16[8,256,128]{2,1,0:T(8,128)(2,1)S(1)} %copy.20.refs_3_), channel_id=1, source_target_pairs={{0,1},{1,0},{2,3},{3,2},{4,5},{5,4},{6,7},{7,6},{8,9},{9,8},{10,11... | collective-permute-start | bytes 1572872 | tf_op jit(solution)/shard_map/ppermute | solution.py:632
  100.5 1.5 %collective-permute-done.17.refs_4_ = bf16[8,256,128]{2,1,0:T(8,128)(2,1)S(1)} collective-permute-done((bf16[8,256,128]{2,1,0:T(8,128)(2,1)S(1)}, bf16[8,256,128]{2,1,0:T(8,128)(2,1)S(1)}, u32[]{:S(2)}, u32[]{:S(2)}) %collective-permute-start.17) | collective-permute-done | bytes 524320 | tf_op jit(solution)/shard_map/ppermute | solution.py:632
  102.0 0.8 copy-done.29
  102.8 7.4 %finish.1 = bf16[128,8192]{1,0:T(8,128)(2,1)} custom-call(s32[14]{0:T(128)} %concatenate.3.ids, f32[128,8192]{1,0:T(8,128)} %get-tuple-element.26.refs_0_, bf16[64,128]{1,0:T(8,128)(2,1)} %bitcast.44, bf16[128,512]{1,0:T(8,128)(2,1)} %bitcast.37, bf16[8,256,128]{2,1,0:T(8,128)(2,1)} %copy-done.16, bf16[8,256,128]{2,1,0:T(8,128)(2,1)} %copy-done.29, ...), custom_call_target="tpu_custom_call" | custom-call | flops 34359738368 | bytes 1048576 | tf_op jit(solution)/shard_map/finish/pallas_call | solution.py:411
  (49 shorter events, 0.1 us)
Async XLA Ops:
  0.6 15.9 %collective-permute-start = (f32[3,4,8192]{2,1,0:T(4,128)}, f32[3,4,8192]{2,1,0:T(4,128)S(1)}, u32[]{:S(2)}, u32[]{:S(2)}) collective-permute-start(f32[3,4,8192]{2,1,0:T(4,128)} %bitcast.24), channel_id=1, source_target_pairs={{16,0},{0,16},{17,1},{1,17},{18,2},{2,18},{19,3},{3,19},{20,4},{4,... | collective-permute-start | bytes 1179656 | tf_op jit(solution)/shard_map/ppermute | solution.py:640
  2.0 9.9 %copy-start.28 = (f32[1,3,4,8192]{3,2,1,0:T(4,128)S(1)}, f32[1,3,4,8192]{3,2,1,0:T(4,128)}, u32[]{:S(2)}) copy-start(f32[1,3,4,8192]{3,2,1,0:T(4,128)} %param.23) | copy-start | bytes 1179652
  4.7 12.2 %copy-start.4 = (bf16[2,128,512]{2,1,0:T(8,128)(2,1)S(1)}, bf16[2,128,512]{2,1,0:T(8,128)(2,1)}, u32[]{:S(2)}) copy-start(bf16[2,128,512]{2,1,0:T(8,128)(2,1)} %get-tuple-element.18.refs_2_.refs_4_.refs_3_) | copy-start | bytes 786436
  4.7 12.2 %copy-start.8 = (s32[14]{0:T(128)S(1)}, s32[14]{0:T(128)}, u32[]{:S(2)}) copy-start(s32[14]{0:T(128)} %concatenate.3.ids) | copy-start | bytes 172
  4.7 8.5 %collective-permute-start.4 = (bf16[2,128,512]{2,1,0:T(8,128)(2,1)}, bf16[2,128,512]{2,1,0:T(8,128)(2,1)}, u32[]{:S(2)}, u32[]{:S(2)}) collective-permute-start(bf16[2,128,512]{2,1,0:T(8,128)(2,1)} %get-tuple-element.18.refs_2_.refs_4_.refs_3_), channel_id=1, source_target_pairs={{0,4},{1,5},{2,6},{3,7},{4,8},{5,9},{6,10},{7,11},{8,12},{9,13},{1... | collective-permute-start | bytes 786440 | tf_op jit(solution)/shard_map/ppermute | solution.py:596
  9.0 31.1 %collective-permute-start.9 = (bf16[2,128,512]{2,1,0:T(8,128)(2,1)}, bf16[2,128,512]{2,1,0:T(8,128)(2,1)S(1)}, u32[]{:S(2)}, u32[]{:S(2)}) collective-permute-start(bf16[2,128,512]{2,1,0:T(8,128)(2,1)} %get-tuple-element.18.refs_2_.refs_4_.refs_3_), channel_id=1, source_target_pairs={{0,1},{1,0},{2,3},{3,2},{4,5},{5,4},{6,7},{7,6},{8,9},{9,8},{10,11... | collective-permute-start | bytes 786440 | tf_op jit(solution)/shard_map/ppermute | solution.py:632
  10.2 20.5 %collective-permute-start.2 = (bf16[1,512,128]{2,1,0:T(8,128)(2,1)}, bf16[1,512,128]{2,1,0:T(8,128)(2,1)S(1)}, u32[]{:S(2)}, u32[]{:S(2)}) collective-permute-start(bf16[1,512,128]{2,1,0:T(8,128)(2,1)} %get-tuple-element.23), channel_id=1, source_target_pairs={{0,8},{1,9},{2,10},{3,11},{4,12},{5,13},{6,14},{7,15},{8,0},{9,1},... | collective-permute-start | bytes 393224 | tf_op jit(solution)/shard_map/ppermute | solution.py:632
  13.2 39.5 %collective-permute-start.6 = (bf16[2,128,512]{2,1,0:T(8,128)(2,1)}, bf16[2,128,512]{2,1,0:T(8,128)(2,1)}, u32[]{:S(2)}, u32[]{:S(2)}) collective-permute-start(bf16[2,128,512]{2,1,0:T(8,128)(2,1)} %collective-permute-done.4.refs_5_.refs_1_), channel_id=1, source_target_pairs={{0,1},{1,0},{2,3},{3,2},{4,5},{5,4},{6,7},{7,6},{8,9},{9,8},{10,11... | collective-permute-start | bytes 786440 | tf_op jit(solution)/shard_map/ppermute | solution.py:632
  17.8 0.8 copy-start.18
  18.6 0.6 copy-start.21
  19.2 11.8 %collective-permute-start.3 = (bf16[1,256,128]{2,1,0:T(8,128)(2,1)S(1)}, bf16[1,256,128]{2,1,0:T(8,128)(2,1)S(1)}, u32[]{:S(2)}, u32[]{:S(2)}) collective-permute-start(bf16[1,256,128]{2,1,0:T(8,128)(2,1)S(1)} %get-tuple-element.24), channel_id=1, source_target_pairs={{0,8},{1,9},{2,10},{3,11},{4,12},{5,13},{6,14},{7,15},{8,0},{9,1},... | collective-permute-start | bytes 196616 | tf_op jit(solution)/shard_map/ppermute | solution.py:632
  25.2 5.8 %copy-start.9 = (s32[14]{0:T(128)S(1)}, s32[14]{0:T(128)}, u32[]{:S(2)}) copy-start(s32[14]{0:T(128)} %concatenate.3.ids) | copy-start | bytes 172
  25.2 5.8 %copy-start.20 = (bf16[1,512,128]{2,1,0:T(8,128)(2,1)S(1)}, bf16[1,512,128]{2,1,0:T(8,128)(2,1)}, u32[]{:S(2)}) copy-start(bf16[1,512,128]{2,1,0:T(8,128)(2,1)} %get-tuple-element.22.refs_0_) | copy-start | bytes 393220
  25.2 5.8 %copy-start.22 = (bf16[1,256,128]{2,1,0:T(8,128)(2,1)S(1)}, bf16[1,256,128]{2,1,0:T(8,128)(2,1)}, u32[]{:S(2)}) copy-start(bf16[1,256,128]{2,1,0:T(8,128)(2,1)} %copy-done.21) | copy-start | bytes 196612
  30.4 25.8 %collective-permute-start.5 = (bf16[8,272,128]{2,1,0:T(8,128)(2,1)}, bf16[8,272,128]{2,1,0:T(8,128)(2,1)S(1)}, u32[]{:S(2)}, u32[]{:S(2)}) collective-permute-start(bf16[8,272,128]{2,1,0:T(8,128)(2,1)} %get-tuple-element.20.refs_0_), channel_id=1, source_target_pairs={{0,1},{1,0},{2,3},{3,2},{4,5},{5,4},{6,7},{7,6},{8,9},{9,8},{10,11... | collective-permute-start | bytes 1671176 | tf_op jit(solution)/shard_map/ppermute | solution.py:632
  30.7 4.2 %collective-permute-start.1 = (bf16[8,272,128]{2,1,0:T(8,128)(2,1)}, bf16[8,272,128]{2,1,0:T(8,128)(2,1)S(1)}, u32[]{:S(2)}, u32[]{:S(2)}) collective-permute-start(bf16[8,272,128]{2,1,0:T(8,128)(2,1)} %get-tuple-element.21.refs_6_), channel_id=1, source_target_pairs={{0,1},{1,0},{2,3},{3,2},{4,5},{5,4},{6,7},{7,6},{8,9},{9,8},{10,11... | collective-permute-start | bytes 1671176 | tf_op jit(solution)/shard_map/ppermute | solution.py:632
  31.0 1.1 copy-start.15
  32.0 2.9 %copy-start.14 = (bf16[8,272,128]{2,1,0:T(8,128)(2,1)S(1)}, bf16[8,272,128]{2,1,0:T(8,128)(2,1)}, u32[]{:S(2)}) copy-start(bf16[8,272,128]{2,1,0:T(8,128)(2,1)} %get-tuple-element.20.refs_0_) | copy-start | bytes 1671172
  33.6 40.1 %copy-start = (bf16[2,768,128]{2,1,0:T(8,128)(2,1)}, bf16[2,768,128]{2,1,0:T(8,128)(2,1)S(1)}, u32[]{:S(2)}) copy-start(bf16[2,768,128]{2,1,0:T(8,128)(2,1)S(1)} %get-tuple-element.25.refs_2_.refs_7_.refs_15_.refs_23_.refs_31_) | copy-start | bytes 1179652
  33.6 7.9 %collective-permute-start.7 = (bf16[2,128,512]{2,1,0:T(8,128)(2,1)S(1)}, bf16[2,128,512]{2,1,0:T(8,128)(2,1)}, u32[]{:S(2)}, u32[]{:S(2)}) collective-permute-start(bf16[2,128,512]{2,1,0:T(8,128)(2,1)S(1)} %get-tuple-element.29), channel_id=1, source_target_pairs={{0,2},{1,3},{2,0},{3,1},{4,6},{5,7},{6,4},{7,5},{8,10},{9,11},{10,... | collective-permute-start | bytes 786440 | tf_op jit(solution)/shard_map/ppermute | solution.py:632
  34.9 1.6 %copy-start.13 = (bf16[8,272,128]{2,1,0:T(8,128)(2,1)}, bf16[8,272,128]{2,1,0:T(8,128)(2,1)S(1)}, u32[]{:S(2)}) copy-start(bf16[8,272,128]{2,1,0:T(8,128)(2,1)S(1)} %collective-permute-done.1.refs_1_.refs_6_) | copy-start | bytes 1671172
  34.9 10.1 %collective-permute-start.10 = (bf16[2,768,128]{2,1,0:T(8,128)(2,1)S(1)}, bf16[2,768,128]{2,1,0:T(8,128)(2,1)S(1)}, u32[]{:S(2)}, u32[]{:S(2)}) collective-permute-start(bf16[2,768,128]{2,1,0:T(8,128)(2,1)S(1)} %get-tuple-element.25.refs_2_.refs_7_.refs_15_.refs_23_.refs_31_), channel_id=1, source_target_pairs={{0,4},{1,5},{2,6},{3,7},{4,0},{5,1},{6,2},{7,3},{8,12},{9,13},{10,... | collective-permute-start | bytes 1179656 | tf_op jit(solution)/shard_map/ppermute | solution.py:632
  36.5 28.2 %all-to-all-start = ((bf16[8,272,128]{2,1,0:T(8,128)(2,1)}), bf16[8,272,128]{2,1,0:T(8,128)(2,1)S(1)}, u32[]{:S(2)}, u32[]{:S(2)}) async-start(bf16[8,272,128]{2,1,0:T(8,128)(2,1)} %combine.1.refs_6_), calls=%async_computation | async-start | bytes 1114112 | tf_op jit(solution)/shard_map/all_to_all | solution.py:635
  40.1 24.6 %copy-start.5 = (bf16[2,128,512]{2,1,0:T(8,128)(2,1)}, bf16[2,128,512]{2,1,0:T(8,128)(2,1)S(1)}, u32[]{:S(2)}) copy-start(bf16[2,128,512]{2,1,0:T(8,128)(2,1)S(1)} %collective-permute-done.9.refs_6_) | copy-start | bytes 786436
  40.1 16.2 %collective-permute-start.11 = (bf16[2,768,128]{2,1,0:T(8,128)(2,1)S(1)}, bf16[2,768,128]{2,1,0:T(8,128)(2,1)S(1)}, u32[]{:S(2)}, u32[]{:S(2)}) collective-permute-start(bf16[2,768,128]{2,1,0:T(8,128)(2,1)S(1)} %get-tuple-element.25.refs_2_.refs_7_.refs_15_.refs_23_.refs_31_), channel_id=1, source_target_pairs={{0,2},{1,3},{2,0},{3,1},{4,6},{5,7},{6,4},{7,5},{8,10},{9,11},{10,... | collective-permute-start | bytes 1179656 | tf_op jit(solution)/shard_map/ppermute | solution.py:632
  41.5 14.8 %collective-permute-start.8 = (bf16[2,128,512]{2,1,0:T(8,128)(2,1)}, bf16[2,128,512]{2,1,0:T(8,128)(2,1)S(1)}, u32[]{:S(2)}, u32[]{:S(2)}) collective-permute-start(bf16[2,128,512]{2,1,0:T(8,128)(2,1)} %collective-permute-done.7.refs_2_), channel_id=1, source_target_pairs={{0,1},{1,0},{2,3},{3,2},{4,5},{5,4},{6,7},{7,6},{8,9},{9,8},{10,11... | collective-permute-start | bytes 786440 | tf_op jit(solution)/shard_map/ppermute | solution.py:632
  45.0 29.8 %copy-start.1 = (bf16[2,768,128]{2,1,0:T(8,128)(2,1)}, bf16[2,768,128]{2,1,0:T(8,128)(2,1)S(1)}, u32[]{:S(2)}) copy-start(bf16[2,768,128]{2,1,0:T(8,128)(2,1)S(1)} %collective-permute-done.10.refs_8_.refs_16_.refs_24_.refs_32_) | copy-start | bytes 1179652
  45.0 19.7 %collective-permute-start.12 = (bf16[2,768,128]{2,1,0:T(8,128)(2,1)S(1)}, bf16[2,768,128]{2,1,0:T(8,128)(2,1)S(1)}, u32[]{:S(2)}, u32[]{:S(2)}) collective-permute-start(bf16[2,768,128]{2,1,0:T(8,128)(2,1)S(1)} %collective-permute-done.10.refs_8_.refs_16_.refs_24_.refs_32_), channel_id=1, source_target_pairs={{0,2},{1,3},{2,0},{3,1},{4,6},{5,7},{6,4},{7,5},{8,10},{9,11},{10,... | collective-permute-start | bytes 1179656 | tf_op jit(solution)/shard_map/ppermute | solution.py:632
  46.0 18.7 %copy-start.10 = (s32[14]{0:T(128)S(1)}, s32[14]{0:T(128)}, u32[]{:S(2)}) copy-start(s32[14]{0:T(128)} %concatenate.3.ids) | copy-start | bytes 172
  56.3 18.5 %copy-start.2 = (bf16[2,768,128]{2,1,0:T(8,128)(2,1)}, bf16[2,768,128]{2,1,0:T(8,128)(2,1)S(1)}, u32[]{:S(2)}) copy-start(bf16[2,768,128]{2,1,0:T(8,128)(2,1)S(1)} %collective-permute-done.11.refs_9_.refs_17_.refs_25_.refs_33_) | copy-start | bytes 1179652
  56.3 11.8 %copy-start.12 = (bf16[8,272,128]{2,1,0:T(8,128)(2,1)}, bf16[8,272,128]{2,1,0:T(8,128)(2,1)S(1)}, u32[]{:S(2)}) copy-start(bf16[8,272,128]{2,1,0:T(8,128)(2,1)S(1)} %collective-permute-done.5.refs_3_.refs_5_) | copy-start | bytes 1671172
  56.3 11.8 %copy-start.6 = (bf16[2,128,512]{2,1,0:T(8,128)(2,1)}, bf16[2,128,512]{2,1,0:T(8,128)(2,1)S(1)}, u32[]{:S(2)}) copy-start(bf16[2,128,512]{2,1,0:T(8,128)(2,1)S(1)} %collective-permute-done.8.refs_5_) | copy-start | bytes 786436
  64.7 10.5 %copy-start.3 = (bf16[2,768,128]{2,1,0:T(8,128)(2,1)}, bf16[2,768,128]{2,1,0:T(8,128)(2,1)S(1)}, u32[]{:S(2)}) copy-start(bf16[2,768,128]{2,1,0:T(8,128)(2,1)S(1)} %collective-permute-done.12.refs_10_.refs_18_.refs_26_.refs_34_) | copy-start | bytes 1179652
  64.7 1.1 %copy-start.19 = (f32[3,256,128]{2,1,0:T(8,128)S(1)}, f32[3,256,128]{2,1,0:T(8,128)}, u32[]{:S(2)}) copy-start(f32[3,256,128]{2,1,0:T(8,128)} %copy-done.18) | copy-start | bytes 1179652
  65.8 0.7 copy-start.23
  68.1 0.6 copy-start.7
  68.6 24.9 %all-to-all-start.1 = ((bf16[8,256,128]{2,1,0:T(8,128)(2,1)}), bf16[8,256,128]{2,1,0:T(8,128)(2,1)S(1)}, u32[]{:S(2)}, u32[]{:S(2)}) async-start(bf16[8,256,128]{2,1,0:T(8,128)(2,1)} %get-tuple-element.30), calls=%async_computation.1 | async-start | bytes 1048576 | tf_op jit(solution)/shard_map/all_to_all | solution.py:635
  73.7 2.4 %collective-permute-start.13 = (bf16[2,768,128]{2,1,0:T(8,128)(2,1)S(1)}, bf16[2,768,128]{2,1,0:T(8,128)(2,1)S(1)}, u32[]{:S(2)}, u32[]{:S(2)}) collective-permute-start(bf16[2,768,128]{2,1,0:T(8,128)(2,1)S(1)} %get-tuple-element.25.refs_2_.refs_7_.refs_15_.refs_23_.refs_31_), channel_id=1, source_target_pairs={{0,1},{1,0},{2,3},{3,2},{4,5},{5,4},{6,7},{7,6},{8,9},{9,8},{10,11... | collective-permute-start | bytes 1179656 | tf_op jit(solution)/shard_map/ppermute | solution.py:632
  74.7 1.9 %collective-permute-start.15 = (bf16[2,768,128]{2,1,0:T(8,128)(2,1)S(1)}, bf16[2,768,128]{2,1,0:T(8,128)(2,1)S(1)}, u32[]{:S(2)}, u32[]{:S(2)}) collective-permute-start(bf16[2,768,128]{2,1,0:T(8,128)(2,1)S(1)} %collective-permute-done.11.refs_9_.refs_17_.refs_25_.refs_33_), channel_id=1, source_target_pairs={{0,1},{1,0},{2,3},{3,2},{4,5},{5,4},{6,7},{7,6},{8,9},{9,8},{10,11... | collective-permute-start | bytes 1179656 | tf_op jit(solution)/shard_map/ppermute | solution.py:632
  74.8 2.4 %collective-permute-start.14 = (bf16[2,768,128]{2,1,0:T(8,128)(2,1)S(1)}, bf16[2,768,128]{2,1,0:T(8,128)(2,1)S(1)}, u32[]{:S(2)}, u32[]{:S(2)}) collective-permute-start(bf16[2,768,128]{2,1,0:T(8,128)(2,1)S(1)} %collective-permute-done.10.refs_8_.refs_16_.refs_24_.refs_32_), channel_id=1, source_target_pairs={{0,1},{1,0},{2,3},{3,2},{4,5},{5,4},{6,7},{7,6},{8,9},{9,8},{10,11... | collective-permute-start | bytes 1179656 | tf_op jit(solution)/shard_map/ppermute | solution.py:632
  75.2 2.5 %collective-permute-start.16 = (bf16[2,768,128]{2,1,0:T(8,128)(2,1)S(1)}, bf16[2,768,128]{2,1,0:T(8,128)(2,1)S(1)}, u32[]{:S(2)}, u32[]{:S(2)}) collective-permute-start(bf16[2,768,128]{2,1,0:T(8,128)(2,1)S(1)} %collective-permute-done.12.refs_10_.refs_18_.refs_26_.refs_34_), channel_id=1, source_target_pairs={{0,1},{1,0},{2,3},{3,2},{4,5},{5,4},{6,7},{7,6},{8,9},{9,8},{10,11... | collective-permute-start | bytes 1179656 | tf_op jit(solution)/shard_map/ppermute | solution.py:632
  76.1 1.7 %copy-start.24 = (bf16[2,768,128]{2,1,0:T(8,128)(2,1)}, bf16[2,768,128]{2,1,0:T(8,128)(2,1)S(1)}, u32[]{:S(2)}) copy-start(bf16[2,768,128]{2,1,0:T(8,128)(2,1)S(1)} %collective-permute-done.13.refs_11_.refs_19_.refs_27_.refs_35_) | copy-start | bytes 1179652
  76.6 1.1 %copy-start.25 = (bf16[2,768,128]{2,1,0:T(8,128)(2,1)}, bf16[2,768,128]{2,1,0:T(8,128)(2,1)S(1)}, u32[]{:S(2)}) copy-start(bf16[2,768,128]{2,1,0:T(8,128)(2,1)S(1)} %collective-permute-done.15.refs_13_.refs_21_.refs_29_.refs_37_) | copy-start | bytes 1179652
  77.2 0.8 copy-start.26
  77.7 0.8 copy-start.27
  78.5 15.0 %copy-start.11 = (s32[14]{0:T(128)S(1)}, s32[14]{0:T(128)}, u32[]{:S(2)}) copy-start(s32[14]{0:T(128)} %concatenate.3.ids) | copy-start | bytes 172
  93.6 0.7 copy-start.17
  94.8 7.2 %copy-start.16 = (bf16[8,256,128]{2,1,0:T(8,128)(2,1)}, bf16[8,256,128]{2,1,0:T(8,128)(2,1)S(1)}, u32[]{:S(2)}) copy-start(bf16[8,256,128]{2,1,0:T(8,128)(2,1)S(1)} %copy.20.refs_3_) | copy-start | bytes 1572868
  94.8 7.2 %collective-permute-start.17 = (bf16[8,256,128]{2,1,0:T(8,128)(2,1)S(1)}, bf16[8,256,128]{2,1,0:T(8,128)(2,1)S(1)}, u32[]{:S(2)}, u32[]{:S(2)}) collective-permute-start(bf16[8,256,128]{2,1,0:T(8,128)(2,1)S(1)} %copy.20.refs_3_), channel_id=1, source_target_pairs={{0,1},{1,0},{2,3},{3,2},{4,5},{5,4},{6,7},{7,6},{8,9},{9,8},{10,11... | collective-permute-start | bytes 1572872 | tf_op jit(solution)/shard_map/ppermute | solution.py:632
  102.0 0.8 copy-start.29

commit v3 on v1

--- a/solution.py
+++ b/solution.py
@@ -516,30 +516,33 @@
                     [q_ref[tokens, g * HD : (g + 1) * HD] for g in range(QH // KVH)], axis=0
                 )
                 scores = lax.dot_general(
-                    queries, keys, (((1,), (1,)), ((), ())), preferred_element_type=jnp.float32
+                    keys, queries, (((1,), (1,)), ((), ())), preferred_element_type=jnp.float32
                 )
-                token = lax.broadcasted_iota(jnp.int32, (BLOCK, COLUMNS), 0)
-                column = lax.broadcasted_iota(jnp.int32, (BLOCK, COLUMNS), 1)
+                column = lax.broadcasted_iota(jnp.int32, (COLUMNS, 2 * BLOCK), 0)
+                token = lax.broadcasted_iota(jnp.int32, (COLUMNS, 2 * BLOCK), 1) % BLOCK
                 seen = (column > token) & (column <= token + WINDOW) & (column >= oldest - b * BLOCK)
                 seen = (seen & (column < SPAN)) | ((column >= SPAN) & (column < SPAN + SINKS))
                 bias = jnp.where(seen, 0.0, NEG)
-                weights, sums = [], []
-                for g in range(QH // KVH):
-                    score = scores[g * BLOCK : (g + 1) * BLOCK] * factor + bias
-                    weight = jnp.exp(score - jnp.max(score, axis=1, keepdims=True))
-                    sums.append(jnp.sum(weight, axis=1, keepdims=True))
+                weights, shares = [], []
+                for j in range(QH // KVH // 2):
+                    score = scores[:, j * 2 * BLOCK : (j + 1) * 2 * BLOCK] * factor + bias
+                    weight = jnp.exp(score - jnp.max(score, axis=0, keepdims=True))
+                    shares.append(1.0 / jnp.sum(weight, axis=0, keepdims=True))
                     weights.append(weight.astype(jnp.bfloat16))
-                mixed = jnp.dot(
-                    jnp.concatenate(weights, axis=0), values, preferred_element_type=jnp.float32
+                mixed = lax.dot_general(
+                    values, jnp.concatenate(weights, axis=1), (((0,), (0,)), ((), ())),
+                    preferred_element_type=jnp.float32,
                 )
-                for g in range(QH // KVH):
-                    result = mixed[g * BLOCK : (g + 1) * BLOCK] / sums[g]
-                    lanes = slice(g * HD, (g + 1) * HD)
-                    if resuming:
-                        index = lax.broadcasted_iota(jnp.int32, (BLOCK, HD), 0) + b * BLOCK
-                        before = out_ref[tokens, lanes].astype(jnp.float32)
-                        result = jnp.where(index >= r, result, before)
-                    out_ref[tokens, lanes] = result.astype(jnp.bfloat16)
+                for j in range(QH // KVH // 2):
+                    pair = (mixed[:, j * 2 * BLOCK : (j + 1) * 2 * BLOCK] * shares[j]).T
+                    for g in range(2):
+                        result = pair[g * BLOCK : (g + 1) * BLOCK]
+                        lanes = slice((2 * j + g) * HD, (2 * j + g + 1) * HD)
+                        if resuming:
+                            index = lax.broadcasted_iota(jnp.int32, (BLOCK, HD), 0) + b * BLOCK
+                            before = out_ref[tokens, lanes].astype(jnp.float32)
+                            result = jnp.where(index >= r, result, before)
+                        out_ref[tokens, lanes] = result.astype(jnp.bfloat16)
 
     one_session(opening, history_refs[0:8], history_refs[8:16], False, r > 0)
     one_session(closing, history_refs[16:24], history_refs[24:], True, r >= 0)

time: 107 us -> 105 us (0.981)
  the two profiles are of different devices: /device:TPU:3 before, /device:TPU:0 now
where the time goes in v3:
time: 105 us
  Pallas kernels  42 us (40%)
  starting transfers between devices  27.8 us (26%)
  waiting for transfers between devices  25.6 us (24%)
  local copies, waits for them, and re-layouts  9.15 us (9%)
    ppermute x16, waiting for transfers between devices, apart(): lax.ppermute(block, 'ctx', [(i, i ^ distance) for i in range(devices)])  25.6 us
    pallas_call x1, Pallas kernels, attend(): pl.pallas_call(scalars(attend_kernel), out_shape=[jax.ShapeDtypeStruct((T...  13.8 us
    ppermute x16, starting transfers between devices, apart(): lax.ppermute(block, 'ctx', [(i, i ^ distance) for i in range(devices)])  13.2 us
    pallas_call x6, Pallas kernels, whole(): pl.pallas_call(kernel, out_shape=[jax.ShapeDtypeStruct(s, t) for s, t in...  8.76 us
    all_to_all x2, starting transfers between devices, exchanged(): lax.all_to_all(block, 'ctx', 0, 0, axis_index_groups=same_core, tiled=True)  8.1 us
    pallas_call x1, Pallas kernels, finish(): pl.pallas_call(scalars(finish_kernel, local), out_shape=jax.ShapeDtypeStr...  7.41 us
    pallas_call x1, Pallas kernels, intra(): pl.pallas_call(scalars(intra_kernel), out_shape=[jax.ShapeDtypeStruct((TO...  6.72 us
    unnamed x56, local copies, waits for them, and re-layouts  6 us
  transfers between devices with their start and end apart: 20, of which 9 were waited for; matrix products, arithmetic and copies ran while one was open for 3% of the time, Pallas kernels for 31%

profile of v3, /device:TPU:0, one launch (start us, length us, event | category | flops | bytes accessed | tf_op | source)
XLA Modules:
  0.0 105.4 jit_solution(47391012462673216)
XLA Ops:
  0.6 3.0 %collective-permute-start.2 = (f32[3,4,8192]{2,1,0:T(4,128)}, f32[3,4,8192]{2,1,0:T(4,128)}, u32[]{:S(2)}, u32[]{:S(2)}) collective-permute-start(f32[3,4,8192]{2,1,0:T(4,128)} %bitcast.24), channel_id=1, source_target_pairs={{16,0},{0,16},{17,1},{1,17},{18,2},{2,18},{19,3},{3,19},{20,4},{4,... | collective-permute-start | bytes 1179656 | tf_op jit(solution)/shard_map/ppermute | solution.py:643
  3.6 1.3 %concatenate.3.ids = s32[14]{0:T(128)} concatenate(s32[1]{0:T(128)} %bitcast, s32[1]{0:T(128)} %bitcast.1, s32[3]{0:T(128)} %bitcast.27, s32[3]{0:T(128)} %bitcast.28, s32[6]{0:T(128)} %param.24), dimensions={0} | concatenate | bytes 112 | tf_op jit(solution)/shard_map/concatenate | solution.py:629
  5.0 2.5 %pack.1 = (bf16[1,512,128]{2,1,0:T(8,128)(2,1)}, bf16[1,512,128]{2,1,0:T(8,128)(2,1)}, bf16[2,128,512]{2,1,0:T(8,128)(2,1)}) custom-call(s32[14]{0:T(128)} %concatenate.3.ids, bf16[3,32,512]{2,1,0:T(8,128)(2,1)} %bitcast.38, bf16[3,32,512]{2,1,0:T(8,128)(2,1)} %bitcast.39, bf16[128,512]{1,0:T(8,128)(2,1)} %bitcast.32, bf16[128,512]{1,0:T(8,128)(2,1)} %bitcast.33), custom_call_target="tpu_custom_call" | custom-call | flops 34359738368 | bytes 1048576 | tf_op jit(solution)/shard_map/pack/pallas_call | solution.py:173
  7.5 2.6 %collective-permute-start.1 = (bf16[1,512,128]{2,1,0:T(8,128)(2,1)}, bf16[1,512,128]{2,1,0:T(8,128)(2,1)S(1)}, u32[]{:S(2)}, u32[]{:S(2)}) collective-permute-start(bf16[1,512,128]{2,1,0:T(8,128)(2,1)} %get-tuple-element.18.refs_4_), channel_id=1, source_target_pairs={{0,8},{1,9},{2,10},{3,11},{4,12},{5,13},{6,14},{7,15},{8,0},{9,1},... | collective-permute-start | bytes 393224 | tf_op jit(solution)/shard_map/ppermute | solution.py:635
  10.1 3.5 %collective-permute-start.4 = (bf16[2,128,512]{2,1,0:T(8,128)(2,1)}, bf16[2,128,512]{2,1,0:T(8,128)(2,1)S(1)}, u32[]{:S(2)}, u32[]{:S(2)}) collective-permute-start(bf16[2,128,512]{2,1,0:T(8,128)(2,1)} %get-tuple-element.24.refs_4_.refs_3_), channel_id=1, source_target_pairs={{0,4},{1,5},{2,6},{3,7},{4,8},{5,9},{6,10},{7,11},{8,12},{9,13},{1... | collective-permute-start | bytes 786440 | tf_op jit(solution)/shard_map/ppermute | solution.py:599
  13.6 0.0 copy-start.25
  13.6 5.2 %summaries.1 = (bf16[8,272,128]{2,1,0:T(8,128)(2,1)}, bf16[8,272,128]{2,1,0:T(8,128)(2,1)}) custom-call(s32[14]{0:T(128)} %concatenate.3.ids, bf16[128,8192]{1,0:T(8,128)(2,1)} %bitcast.29, bf16[64,128]{1,0:T(8,128)(2,1)} %bitcast.42, bf16[64,128]{1,0:T(8,128)(2,1)} %bitcast.40, bf16[128,512]{1,0:T(8,128)(2,1)} %bitcast.34, ...), custom_call_target="tpu_custom_call" | custom-call | flops 34359738368 | bytes 1048576 | tf_op jit(solution)/shard_map/summaries/pallas_call | solution.py:139
  18.9 0.0 collective-permute-start
  18.9 0.4 reshape_squeeze.3.refs_0_
  19.3 0.0 collective-permute-done.2
  19.3 1.4 %reshape.7.refs_1_ = f32[3,4,128,64]{3,2,1,0:T(8,128)S(1)} reshape(f32[3,4,8192]{2,1,0:T(4,128)} %collective-permute-done.2) | data formatting | bytes 786432 | tf_op jit(solution)/shard_map/reshape | solution.py:644
  20.7 0.0 copy-start.14
  20.7 1.0 copy-done.14
  21.8 0.8 restore.1
  22.6 0.8 copy-done.17
  23.4 0.3 collective-permute-start.3
  23.7 0.2 collective-permute-start.9
  24.0 0.0 collective-permute-done.1.refs_1_
  24.0 0.3 collective-permute-start.5
  24.2 0.0 collective-permute-done.4.refs_5_.refs_1_
  24.3 0.2 collective-permute-start.6
  24.5 5.2 %collective-permute-done.3.refs_3_ = bf16[1,256,128]{2,1,0:T(8,128)(2,1)S(1)} collective-permute-done((bf16[1,256,128]{2,1,0:T(8,128)(2,1)S(1)}, bf16[1,256,128]{2,1,0:T(8,128)(2,1)S(1)}, u32[]{:S(2)}, u32[]{:S(2)}) %collective-permute-start.3) | collective-permute-done | bytes 65568 | tf_op jit(solution)/shard_map/ppermute | solution.py:635
  29.6 0.0 collective-permute-done.refs_6_.refs_1_
  29.6 0.0 copy-done.19
  29.7 0.6 join_two.1
  30.3 1.6 %collective-permute-start.7 = (bf16[2,128,512]{2,1,0:T(8,128)(2,1)S(1)}, bf16[2,128,512]{2,1,0:T(8,128)(2,1)S(1)}, u32[]{:S(2)}, u32[]{:S(2)}) collective-permute-start(bf16[2,128,512]{2,1,0:T(8,128)(2,1)S(1)} %get-tuple-element.29), channel_id=1, source_target_pairs={{0,2},{1,3},{2,0},{3,1},{4,6},{5,7},{6,4},{7,5},{8,10},{9,11},{10,... | collective-permute-start | bytes 786440 | tf_op jit(solution)/shard_map/ppermute | solution.py:635
  31.9 0.0 collective-permute-start.10
  31.9 2.6 %combine.1.refs_6_ = bf16[8,272,128]{2,1,0:T(8,128)(2,1)} custom-call(s32[14]{0:T(128)S(1)} %copy-done.10, bf16[8,272,128]{2,1,0:T(8,128)(2,1)} %get-tuple-element.19.refs_0_, bf16[8,272,128]{2,1,0:T(8,128)(2,1)S(1)} %collective-permute-done.refs_6_.refs_1_, bf16[2,768,128]{2,1,0:T(8,128)(2,1)S(1)} %get-tuple-element.25.refs_2_.refs_7_.refs_15_.refs_23_.refs_31_), custom_call_target="tpu_custom_call" | custom-call | flops 34359738368 | bytes 1048576 | tf_op jit(solution)/shard_map/combine/pallas_call | solution.py:173
  34.5 3.5 %all-to-all-start = ((bf16[8,272,128]{2,1,0:T(8,128)(2,1)}), bf16[8,272,128]{2,1,0:T(8,128)(2,1)S(1)}, u32[]{:S(2)}, u32[]{:S(2)}) async-start(bf16[8,272,128]{2,1,0:T(8,128)(2,1)} %combine.1.refs_6_), calls=%async_computation | async-start | bytes 1114112 | tf_op jit(solution)/shard_map/all_to_all | solution.py:638
  38.1 0.0 collective-permute-done.9.refs_6_
  38.1 2.0 %collective-permute-start.11 = (bf16[2,768,128]{2,1,0:T(8,128)(2,1)S(1)}, bf16[2,768,128]{2,1,0:T(8,128)(2,1)S(1)}, u32[]{:S(2)}, u32[]{:S(2)}) collective-permute-start(bf16[2,768,128]{2,1,0:T(8,128)(2,1)S(1)} %get-tuple-element.25.refs_2_.refs_7_.refs_15_.refs_23_.refs_31_), channel_id=1, source_target_pairs={{0,2},{1,3},{2,0},{3,1},{4,6},{5,7},{6,4},{7,5},{8,10},{9,11},{10,... | collective-permute-start | bytes 1179656 | tf_op jit(solution)/shard_map/ppermute | solution.py:635
  40.0 0.0 collective-permute-done.7.refs_2_
  40.1 0.0 collective-permute-start.8
  40.1 5.3 %collective-permute-done.10.refs_8_.refs_16_.refs_24_.refs_32_ = bf16[2,768,128]{2,1,0:T(8,128)(2,1)S(1)} collective-permute-done((bf16[2,768,128]{2,1,0:T(8,128)(2,1)S(1)}, bf16[2,768,128]{2,1,0:T(8,128)(2,1)S(1)}, u32[]{:S(2)}, u32[]{:S(2)}) %collective-permute-start.10) | collective-permute-done | bytes 393248 | tf_op jit(solution)/shard_map/ppermute | solution.py:635
  45.4 0.0 collective-permute-start.12
  45.4 6.7 %intra.1 = (f32[128,8192]{1,0:T(8,128)}, f32[8,128]{1,0:T(8,128)}) custom-call(s32[14]{0:T(128)} %concatenate.3.ids, f32[64]{0:T(128)} %refs_0_.1, bf16[128,8192]{1,0:T(8,128)(2,1)} %bitcast.30, bf16[64,128]{1,0:T(8,128)(2,1)} %bitcast.43, bf16[64,128]{1,0:T(8,128)(2,1)} %bitcast.41, bf16[128,512]{1,0:T(8,128)(2,1)} %bitcast.35, bf16[128,512]{1,0:T(8,128)(2,1)} %bitcast.36, ...), custom_call_target="tpu_custom_call" | custom-call | flops 34359738368 | bytes 1048576 | tf_op jit(solution)/shard_map/intra/pallas_call | solution.py:323
  52.1 0.0 copy-done.26
  52.1 0.0 collective-permute-done.6.refs_4_
  52.1 0.0 collective-permute-done.5.refs_3_.refs_5_
  52.1 4.0 %collective-permute-done.11.refs_9_.refs_17_.refs_25_.refs_33_ = bf16[2,768,128]{2,1,0:T(8,128)(2,1)S(1)} collective-permute-done((bf16[2,768,128]{2,1,0:T(8,128)(2,1)S(1)}, bf16[2,768,128]{2,1,0:T(8,128)(2,1)S(1)}, u32[]{:S(2)}, u32[]{:S(2)}) %collective-permute-start.11) | collective-permute-done | bytes 393248 | tf_op jit(solution)/shard_map/ppermute | solution.py:635
  56.1 0.0 collective-permute-done.8.refs_5_
  56.1 7.2 %collective-permute-done.12.refs_10_.refs_18_.refs_26_.refs_34_ = bf16[2,768,128]{2,1,0:T(8,128)(2,1)S(1)} collective-permute-done((bf16[2,768,128]{2,1,0:T(8,128)(2,1)S(1)}, bf16[2,768,128]{2,1,0:T(8,128)(2,1)S(1)}, u32[]{:S(2)}, u32[]{:S(2)}) %collective-permute-start.12) | collective-permute-done | bytes 393248 | tf_op jit(solution)/shard_map/ppermute | solution.py:635
  63.4 0.0 all-to-all-done.refs_0_
  63.4 1.1 %copy-done.18 = f32[3,256,128]{2,1,0:T(8,128)S(1)} copy-done((f32[3,256,128]{2,1,0:T(8,128)S(1)}, f32[3,256,128]{2,1,0:T(8,128)}, u32[]{:S(2)}) %copy-start.18) | copy-done | bytes 393240
  64.5 0.7 copy-done.20
  65.2 1.6 %recurrence.1 = (bf16[8,256,128]{2,1,0:T(8,128)(2,1)}, f32[8,128]{1,0:T(8,128)S(1)}) custom-call(s32[14]{0:T(128)S(1)} %copy-done.11, bf16[8,272,128]{2,1,0:T(8,128)(2,1)S(1)} %all-to-all-done.refs_0_, f32[3,256,128]{2,1,0:T(8,128)S(1)} %copy-done.18, f32[8,128]{1,0:T(8,128)S(1)} %copy-done.20, bf16[8,272,128]{2,1,0:T(8,128)(2,1)} %collective-permute-done.5.refs_3_.refs_5_, ...), custom_call_target="tpu_custom_call" | custom-call | flops 34359738368 | bytes 1048576 | tf_op jit(solution)/shard_map/recurrence/pallas_call | solution.py:173
  66.8 4.6 %all-to-all-start.1 = ((bf16[8,256,128]{2,1,0:T(8,128)(2,1)}), bf16[8,256,128]{2,1,0:T(8,128)(2,1)S(1)}, u32[]{:S(2)}, u32[]{:S(2)}) async-start(bf16[8,256,128]{2,1,0:T(8,128)(2,1)} %get-tuple-element.30), calls=%async_computation.1 | async-start | bytes 1048576 | tf_op jit(solution)/shard_map/all_to_all | solution.py:638
  71.3 0.1 collective-permute-start.13
  71.4 0.5 collective-permute-start.15
  71.9 0.1 collective-permute-start.14
  72.0 0.4 collective-permute-start.16
  72.4 0.7 collective-permute-done.13.refs_11_.refs_19_.refs_27_.refs_35_
  73.1 0.6 collective-permute-done.15.refs_13_.refs_21_.refs_29_.refs_37_
  73.7 0.6 collective-permute-done.14.refs_12_.refs_20_.refs_28_.refs_36_
  74.3 0.6 collective-permute-done.16.refs_14_.refs_22_.refs_30_.refs_38_
  74.8 0.8 copy-done.24
  75.6 13.8 %attend.1 = (bf16[128,4096]{1,0:T(8,128)(2,1)}, f32[8,128]{1,0:T(8,128)}) custom-call(s32[14]{0:T(128)} %concatenate.3.ids, bf16[128,4096]{1,0:T(8,128)(2,1)} %bitcast.23, bf16[2,128,512]{2,1,0:T(8,128)(2,1)} %copy-done.5, bf16[2,128,512]{2,1,0:T(8,128)(2,1)} %copy-done.26, bf16[2,128,512]{2,1,0:T(8,128)(2,1)} %get-tuple-element.24.refs_4_.refs_3_, ...), custom_call_target="tpu_custom_call" | custom-call | flops 1024 | bytes 1024 | tf_op jit(solution)/shard_map/attend/pallas_call | solution.py:566
  89.5 0.0 all-to-all-done.1.refs_0_
  89.5 0.7 copy-done.16
  90.2 0.6 copy.20.refs_3_
  90.8 4.9 %collective-permute-start.17 = (bf16[8,256,128]{2,1,0:T(8,128)(2,1)S(1)}, bf16[8,256,128]{2,1,0:T(8,128)(2,1)S(1)}, u32[]{:S(2)}, u32[]{:S(2)}) collective-permute-start(bf16[8,256,128]{2,1,0:T(8,128)(2,1)S(1)} %copy.20.refs_3_), channel_id=1, source_target_pairs={{0,1},{1,0},{2,3},{3,2},{4,5},{5,4},{6,7},{7,6},{8,9},{9,8},{10,11... | collective-permute-start | bytes 1572872 | tf_op jit(solution)/shard_map/ppermute | solution.py:635
  95.7 1.5 %collective-permute-done.17.refs_4_ = bf16[8,256,128]{2,1,0:T(8,128)(2,1)S(1)} collective-permute-done((bf16[8,256,128]{2,1,0:T(8,128)(2,1)S(1)}, bf16[8,256,128]{2,1,0:T(8,128)(2,1)S(1)}, u32[]{:S(2)}, u32[]{:S(2)}) %collective-permute-start.17) | collective-permute-done | bytes 524320 | tf_op jit(solution)/shard_map/ppermute | solution.py:635
  97.2 0.8 copy-done.27
  98.0 7.4 %finish.1 = bf16[128,8192]{1,0:T(8,128)(2,1)} custom-call(s32[14]{0:T(128)} %concatenate.3.ids, f32[128,8192]{1,0:T(8,128)} %get-tuple-element.26.refs_0_, bf16[64,128]{1,0:T(8,128)(2,1)} %bitcast.44, bf16[128,512]{1,0:T(8,128)(2,1)} %bitcast.37, bf16[8,256,128]{2,1,0:T(8,128)(2,1)} %copy-done.15, bf16[8,256,128]{2,1,0:T(8,128)(2,1)} %copy-done.27, ...), custom_call_target="tpu_custom_call" | custom-call | flops 34359738368 | bytes 1048576 | tf_op jit(solution)/shard_map/finish/pallas_call | solution.py:411
  (45 shorter events, 0.1 us)
Async XLA Ops:
  0.6 18.7 %collective-permute-start.2 = (f32[3,4,8192]{2,1,0:T(4,128)}, f32[3,4,8192]{2,1,0:T(4,128)}, u32[]{:S(2)}, u32[]{:S(2)}) collective-permute-start(f32[3,4,8192]{2,1,0:T(4,128)} %bitcast.24), channel_id=1, source_target_pairs={{16,0},{0,16},{17,1},{1,17},{18,2},{2,18},{19,3},{3,19},{20,4},{4,... | collective-permute-start | bytes 1179656 | tf_op jit(solution)/shard_map/ppermute | solution.py:643
  7.5 16.4 %collective-permute-start.1 = (bf16[1,512,128]{2,1,0:T(8,128)(2,1)}, bf16[1,512,128]{2,1,0:T(8,128)(2,1)S(1)}, u32[]{:S(2)}, u32[]{:S(2)}) collective-permute-start(bf16[1,512,128]{2,1,0:T(8,128)(2,1)} %get-tuple-element.18.refs_4_), channel_id=1, source_target_pairs={{0,8},{1,9},{2,10},{3,11},{4,12},{5,13},{6,14},{7,15},{8,0},{9,1},... | collective-permute-start | bytes 393224 | tf_op jit(solution)/shard_map/ppermute | solution.py:635
  10.1 14.1 %collective-permute-start.4 = (bf16[2,128,512]{2,1,0:T(8,128)(2,1)}, bf16[2,128,512]{2,1,0:T(8,128)(2,1)S(1)}, u32[]{:S(2)}, u32[]{:S(2)}) collective-permute-start(bf16[2,128,512]{2,1,0:T(8,128)(2,1)} %get-tuple-element.24.refs_4_.refs_3_), channel_id=1, source_target_pairs={{0,4},{1,5},{2,6},{3,7},{4,8},{5,9},{6,10},{7,11},{8,12},{9,13},{1... | collective-permute-start | bytes 786440 | tf_op jit(solution)/shard_map/ppermute | solution.py:599
  13.6 5.3 %copy-start.25 = (f32[1,3,4,8192]{3,2,1,0:T(4,128)S(1)}, f32[1,3,4,8192]{3,2,1,0:T(4,128)}, u32[]{:S(2)}) copy-start(f32[1,3,4,8192]{3,2,1,0:T(4,128)} %param.23) | copy-start | bytes 1179652
  18.9 1.8 %copy-start.10 = (s32[14]{0:T(128)S(1)}, s32[14]{0:T(128)}, u32[]{:S(2)}) copy-start(s32[14]{0:T(128)} %concatenate.3.ids) | copy-start | bytes 172
  18.9 10.8 %collective-permute-start = (bf16[8,272,128]{2,1,0:T(8,128)(2,1)}, bf16[8,272,128]{2,1,0:T(8,128)(2,1)S(1)}, u32[]{:S(2)}, u32[]{:S(2)}) collective-permute-start(bf16[8,272,128]{2,1,0:T(8,128)(2,1)} %get-tuple-element.20.refs_2_), channel_id=1, source_target_pairs={{0,1},{1,0},{2,3},{3,2},{4,5},{5,4},{6,7},{7,6},{8,9},{9,8},{10,11... | collective-permute-start | bytes 1671176 | tf_op jit(solution)/shard_map/ppermute | solution.py:635
  20.7 1.1 %copy-start.14 = (bf16[8,272,128]{2,1,0:T(8,128)(2,1)S(1)}, bf16[8,272,128]{2,1,0:T(8,128)(2,1)}, u32[]{:S(2)}) copy-start(bf16[8,272,128]{2,1,0:T(8,128)(2,1)} %get-tuple-element.20.refs_2_) | copy-start | bytes 1671172
  21.8 2.0 %copy-start.4 = (bf16[2,128,512]{2,1,0:T(8,128)(2,1)S(1)}, bf16[2,128,512]{2,1,0:T(8,128)(2,1)}, u32[]{:S(2)}) copy-start(bf16[2,128,512]{2,1,0:T(8,128)(2,1)} %get-tuple-element.24.refs_4_.refs_3_) | copy-start | bytes 786436
  21.8 7.9 %copy-start.19 = (bf16[1,512,128]{2,1,0:T(8,128)(2,1)S(1)}, bf16[1,512,128]{2,1,0:T(8,128)(2,1)}, u32[]{:S(2)}) copy-start(bf16[1,512,128]{2,1,0:T(8,128)(2,1)} %get-tuple-element.21.refs_0_) | copy-start | bytes 393220
  22.6 0.8 copy-start.17
  23.4 6.2 %collective-permute-start.3 = (bf16[1,256,128]{2,1,0:T(8,128)(2,1)S(1)}, bf16[1,256,128]{2,1,0:T(8,128)(2,1)S(1)}, u32[]{:S(2)}, u32[]{:S(2)}) collective-permute-start(bf16[1,256,128]{2,1,0:T(8,128)(2,1)S(1)} %get-tuple-element.23), channel_id=1, source_target_pairs={{0,8},{1,9},{2,10},{3,11},{4,12},{5,13},{6,14},{7,15},{8,0},{9,1},... | collective-permute-start | bytes 196616 | tf_op jit(solution)/shard_map/ppermute | solution.py:635
  23.7 14.3 %collective-permute-start.9 = (bf16[2,128,512]{2,1,0:T(8,128)(2,1)S(1)}, bf16[2,128,512]{2,1,0:T(8,128)(2,1)S(1)}, u32[]{:S(2)}, u32[]{:S(2)}) collective-permute-start(bf16[2,128,512]{2,1,0:T(8,128)(2,1)S(1)} %copy-done.4), channel_id=1, source_target_pairs={{0,1},{1,0},{2,3},{3,2},{4,5},{5,4},{6,7},{7,6},{8,9},{9,8},{10,11... | collective-permute-start | bytes 786440 | tf_op jit(solution)/shard_map/ppermute | solution.py:635
  24.0 28.2 %collective-permute-start.5 = (bf16[8,272,128]{2,1,0:T(8,128)(2,1)}, bf16[8,272,128]{2,1,0:T(8,128)(2,1)}, u32[]{:S(2)}, u32[]{:S(2)}) collective-permute-start(bf16[8,272,128]{2,1,0:T(8,128)(2,1)} %get-tuple-element.19.refs_0_), channel_id=1, source_target_pairs={{0,1},{1,0},{2,3},{3,2},{4,5},{5,4},{6,7},{7,6},{8,9},{9,8},{10,11... | collective-permute-start | bytes 1671176 | tf_op jit(solution)/shard_map/ppermute | solution.py:635
  24.3 6.0 %copy-start.5 = (bf16[2,128,512]{2,1,0:T(8,128)(2,1)}, bf16[2,128,512]{2,1,0:T(8,128)(2,1)S(1)}, u32[]{:S(2)}) copy-start(bf16[2,128,512]{2,1,0:T(8,128)(2,1)S(1)} %collective-permute-done.4.refs_5_.refs_1_) | copy-start | bytes 786436
  24.3 27.9 %collective-permute-start.6 = (bf16[2,128,512]{2,1,0:T(8,128)(2,1)S(1)}, bf16[2,128,512]{2,1,0:T(8,128)(2,1)S(1)}, u32[]{:S(2)}, u32[]{:S(2)}) collective-permute-start(bf16[2,128,512]{2,1,0:T(8,128)(2,1)S(1)} %collective-permute-done.4.refs_5_.refs_1_), channel_id=1, source_target_pairs={{0,1},{1,0},{2,3},{3,2},{4,5},{5,4},{6,7},{7,6},{8,9},{9,8},{10,11... | collective-permute-start | bytes 786440 | tf_op jit(solution)/shard_map/ppermute | solution.py:635
  29.6 2.2 %copy-start.13 = (bf16[8,272,128]{2,1,0:T(8,128)(2,1)}, bf16[8,272,128]{2,1,0:T(8,128)(2,1)S(1)}, u32[]{:S(2)}) copy-start(bf16[8,272,128]{2,1,0:T(8,128)(2,1)S(1)} %collective-permute-done.refs_6_.refs_1_) | copy-start | bytes 1671172
  30.3 41.1 %copy-start = (bf16[2,768,128]{2,1,0:T(8,128)(2,1)}, bf16[2,768,128]{2,1,0:T(8,128)(2,1)S(1)}, u32[]{:S(2)}) copy-start(bf16[2,768,128]{2,1,0:T(8,128)(2,1)S(1)} %get-tuple-element.25.refs_2_.refs_7_.refs_15_.refs_23_.refs_31_) | copy-start | bytes 1179652
  30.3 9.8 %collective-permute-start.7 = (bf16[2,128,512]{2,1,0:T(8,128)(2,1)S(1)}, bf16[2,128,512]{2,1,0:T(8,128)(2,1)S(1)}, u32[]{:S(2)}, u32[]{:S(2)}) collective-permute-start(bf16[2,128,512]{2,1,0:T(8,128)(2,1)S(1)} %get-tuple-element.29), channel_id=1, source_target_pairs={{0,2},{1,3},{2,0},{3,1},{4,6},{5,7},{6,4},{7,5},{8,10},{9,11},{10,... | collective-permute-start | bytes 786440 | tf_op jit(solution)/shard_map/ppermute | solution.py:635
  31.9 13.5 %collective-permute-start.10 = (bf16[2,768,128]{2,1,0:T(8,128)(2,1)S(1)}, bf16[2,768,128]{2,1,0:T(8,128)(2,1)S(1)}, u32[]{:S(2)}, u32[]{:S(2)}) collective-permute-start(bf16[2,768,128]{2,1,0:T(8,128)(2,1)S(1)} %get-tuple-element.25.refs_2_.refs_7_.refs_15_.refs_23_.refs_31_), channel_id=1, source_target_pairs={{0,4},{1,5},{2,6},{3,7},{4,0},{5,1},{6,2},{7,3},{8,12},{9,13},{10,... | collective-permute-start | bytes 1179656 | tf_op jit(solution)/shard_map/ppermute | solution.py:635
  34.5 28.9 %all-to-all-start = ((bf16[8,272,128]{2,1,0:T(8,128)(2,1)}), bf16[8,272,128]{2,1,0:T(8,128)(2,1)S(1)}, u32[]{:S(2)}, u32[]{:S(2)}) async-start(bf16[8,272,128]{2,1,0:T(8,128)(2,1)} %combine.1.refs_6_), calls=%async_computation | async-start | bytes 1114112 | tf_op jit(solution)/shard_map/all_to_all | solution.py:638
  38.1 25.3 %copy-start.6 = (bf16[2,128,512]{2,1,0:T(8,128)(2,1)}, bf16[2,128,512]{2,1,0:T(8,128)(2,1)S(1)}, u32[]{:S(2)}) copy-start(bf16[2,128,512]{2,1,0:T(8,128)(2,1)S(1)} %collective-permute-done.9.refs_6_) | copy-start | bytes 786436
  38.1 18.1 %collective-permute-start.11 = (bf16[2,768,128]{2,1,0:T(8,128)(2,1)S(1)}, bf16[2,768,128]{2,1,0:T(8,128)(2,1)S(1)}, u32[]{:S(2)}, u32[]{:S(2)}) collective-permute-start(bf16[2,768,128]{2,1,0:T(8,128)(2,1)S(1)} %get-tuple-element.25.refs_2_.refs_7_.refs_15_.refs_23_.refs_31_), channel_id=1, source_target_pairs={{0,2},{1,3},{2,0},{3,1},{4,6},{5,7},{6,4},{7,5},{8,10},{9,11},{10,... | collective-permute-start | bytes 1179656 | tf_op jit(solution)/shard_map/ppermute | solution.py:635
  40.1 12.1 %copy-start.26 = (bf16[2,128,512]{2,1,0:T(8,128)(2,1)}, bf16[2,128,512]{2,1,0:T(8,128)(2,1)S(1)}, u32[]{:S(2)}) copy-start(bf16[2,128,512]{2,1,0:T(8,128)(2,1)S(1)} %collective-permute-done.7.refs_2_) | copy-start | bytes 786436
  40.1 16.1 %collective-permute-start.8 = (bf16[2,128,512]{2,1,0:T(8,128)(2,1)S(1)}, bf16[2,128,512]{2,1,0:T(8,128)(2,1)S(1)}, u32[]{:S(2)}, u32[]{:S(2)}) collective-permute-start(bf16[2,128,512]{2,1,0:T(8,128)(2,1)S(1)} %collective-permute-done.7.refs_2_), channel_id=1, source_target_pairs={{0,1},{1,0},{2,3},{3,2},{4,5},{5,4},{6,7},{7,6},{8,9},{9,8},{10,11... | collective-permute-start | bytes 786440 | tf_op jit(solution)/shard_map/ppermute | solution.py:635
  45.4 26.5 %copy-start.1 = (bf16[2,768,128]{2,1,0:T(8,128)(2,1)}, bf16[2,768,128]{2,1,0:T(8,128)(2,1)S(1)}, u32[]{:S(2)}) copy-start(bf16[2,768,128]{2,1,0:T(8,128)(2,1)S(1)} %collective-permute-done.10.refs_8_.refs_16_.refs_24_.refs_32_) | copy-start | bytes 1179652
  45.4 18.0 %collective-permute-start.12 = (bf16[2,768,128]{2,1,0:T(8,128)(2,1)S(1)}, bf16[2,768,128]{2,1,0:T(8,128)(2,1)S(1)}, u32[]{:S(2)}, u32[]{:S(2)}) collective-permute-start(bf16[2,768,128]{2,1,0:T(8,128)(2,1)S(1)} %collective-permute-done.10.refs_8_.refs_16_.refs_24_.refs_32_), channel_id=1, source_target_pairs={{0,2},{1,3},{2,0},{3,1},{4,6},{5,7},{6,4},{7,5},{8,10},{9,11},{10,... | collective-permute-start | bytes 1179656 | tf_op jit(solution)/shard_map/ppermute | solution.py:635
  45.4 18.0 %copy-start.11 = (s32[14]{0:T(128)S(1)}, s32[14]{0:T(128)}, u32[]{:S(2)}) copy-start(s32[14]{0:T(128)} %concatenate.3.ids) | copy-start | bytes 172
  52.1 14.7 %copy-start.7 = (bf16[2,128,512]{2,1,0:T(8,128)(2,1)}, bf16[2,128,512]{2,1,0:T(8,128)(2,1)S(1)}, u32[]{:S(2)}) copy-start(bf16[2,128,512]{2,1,0:T(8,128)(2,1)S(1)} %collective-permute-done.6.refs_4_) | copy-start | bytes 786436
  56.1 15.3 %copy-start.2 = (bf16[2,768,128]{2,1,0:T(8,128)(2,1)}, bf16[2,768,128]{2,1,0:T(8,128)(2,1)S(1)}, u32[]{:S(2)}) copy-start(bf16[2,768,128]{2,1,0:T(8,128)(2,1)S(1)} %collective-permute-done.11.refs_9_.refs_17_.refs_25_.refs_33_) | copy-start | bytes 1179652
  56.1 10.6 %copy-start.8 = (bf16[2,128,512]{2,1,0:T(8,128)(2,1)}, bf16[2,128,512]{2,1,0:T(8,128)(2,1)S(1)}, u32[]{:S(2)}) copy-start(bf16[2,128,512]{2,1,0:T(8,128)(2,1)S(1)} %collective-permute-done.8.refs_5_) | copy-start | bytes 786436
  63.4 8.7 %copy-start.3 = (bf16[2,768,128]{2,1,0:T(8,128)(2,1)}, bf16[2,768,128]{2,1,0:T(8,128)(2,1)S(1)}, u32[]{:S(2)}) copy-start(bf16[2,768,128]{2,1,0:T(8,128)(2,1)S(1)} %collective-permute-done.12.refs_10_.refs_18_.refs_26_.refs_34_) | copy-start | bytes 1179652
  63.4 1.1 %copy-start.18 = (f32[3,256,128]{2,1,0:T(8,128)S(1)}, f32[3,256,128]{2,1,0:T(8,128)}, u32[]{:S(2)}) copy-start(f32[3,256,128]{2,1,0:T(8,128)} %copy-done.17) | copy-start | bytes 1179652
  64.5 0.7 copy-start.20
  66.8 8.8 %copy-start.9 = (f32[8,128]{1,0:T(8,128)}, f32[8,128]{1,0:T(8,128)S(1)}, u32[]{:S(2)}) copy-start(f32[8,128]{1,0:T(8,128)S(1)} %get-tuple-element.31.refs_41_) | copy-start | bytes 12292
  66.8 22.7 %all-to-all-start.1 = ((bf16[8,256,128]{2,1,0:T(8,128)(2,1)}), bf16[8,256,128]{2,1,0:T(8,128)(2,1)S(1)}, u32[]{:S(2)}, u32[]{:S(2)}) async-start(bf16[8,256,128]{2,1,0:T(8,128)(2,1)} %get-tuple-element.30), calls=%async_computation.1 | async-start | bytes 1048576 | tf_op jit(solution)/shard_map/all_to_all | solution.py:638
  71.3 1.8 %collective-permute-start.13 = (bf16[2,768,128]{2,1,0:T(8,128)(2,1)S(1)}, bf16[2,768,128]{2,1,0:T(8,128)(2,1)S(1)}, u32[]{:S(2)}, u32[]{:S(2)}) collective-permute-start(bf16[2,768,128]{2,1,0:T(8,128)(2,1)S(1)} %get-tuple-element.25.refs_2_.refs_7_.refs_15_.refs_23_.refs_31_), channel_id=1, source_target_pairs={{0,1},{1,0},{2,3},{3,2},{4,5},{5,4},{6,7},{7,6},{8,9},{9,8},{10,11... | collective-permute-start | bytes 1179656 | tf_op jit(solution)/shard_map/ppermute | solution.py:635
  71.4 2.3 %collective-permute-start.15 = (bf16[2,768,128]{2,1,0:T(8,128)(2,1)S(1)}, bf16[2,768,128]{2,1,0:T(8,128)(2,1)S(1)}, u32[]{:S(2)}, u32[]{:S(2)}) collective-permute-start(bf16[2,768,128]{2,1,0:T(8,128)(2,1)S(1)} %collective-permute-done.11.refs_9_.refs_17_.refs_25_.refs_33_), channel_id=1, source_target_pairs={{0,1},{1,0},{2,3},{3,2},{4,5},{5,4},{6,7},{7,6},{8,9},{9,8},{10,11... | collective-permute-start | bytes 1179656 | tf_op jit(solution)/shard_map/ppermute | solution.py:635
  71.9 2.3 %collective-permute-start.14 = (bf16[2,768,128]{2,1,0:T(8,128)(2,1)S(1)}, bf16[2,768,128]{2,1,0:T(8,128)(2,1)S(1)}, u32[]{:S(2)}, u32[]{:S(2)}) collective-permute-start(bf16[2,768,128]{2,1,0:T(8,128)(2,1)S(1)} %collective-permute-done.10.refs_8_.refs_16_.refs_24_.refs_32_), channel_id=1, source_target_pairs={{0,1},{1,0},{2,3},{3,2},{4,5},{5,4},{6,7},{7,6},{8,9},{9,8},{10,11... | collective-permute-start | bytes 1179656 | tf_op jit(solution)/shard_map/ppermute | solution.py:635
  72.0 2.8 %collective-permute-start.16 = (bf16[2,768,128]{2,1,0:T(8,128)(2,1)S(1)}, bf16[2,768,128]{2,1,0:T(8,128)(2,1)S(1)}, u32[]{:S(2)}, u32[]{:S(2)}) collective-permute-start(bf16[2,768,128]{2,1,0:T(8,128)(2,1)S(1)} %collective-permute-done.12.refs_10_.refs_18_.refs_26_.refs_34_), channel_id=1, source_target_pairs={{0,1},{1,0},{2,3},{3,2},{4,5},{5,4},{6,7},{7,6},{8,9},{9,8},{10,11... | collective-permute-start | bytes 1179656 | tf_op jit(solution)/shard_map/ppermute | solution.py:635
  73.1 2.5 %copy-start.21 = (bf16[2,768,128]{2,1,0:T(8,128)(2,1)}, bf16[2,768,128]{2,1,0:T(8,128)(2,1)S(1)}, u32[]{:S(2)}) copy-start(bf16[2,768,128]{2,1,0:T(8,128)(2,1)S(1)} %collective-permute-done.13.refs_11_.refs_19_.refs_27_.refs_35_) | copy-start | bytes 1179652
  73.7 1.9 %copy-start.22 = (bf16[2,768,128]{2,1,0:T(8,128)(2,1)}, bf16[2,768,128]{2,1,0:T(8,128)(2,1)S(1)}, u32[]{:S(2)}) copy-start(bf16[2,768,128]{2,1,0:T(8,128)(2,1)S(1)} %collective-permute-done.15.refs_13_.refs_21_.refs_29_.refs_37_) | copy-start | bytes 1179652
  74.3 1.4 %copy-start.23 = (bf16[2,768,128]{2,1,0:T(8,128)(2,1)}, bf16[2,768,128]{2,1,0:T(8,128)(2,1)S(1)}, u32[]{:S(2)}) copy-start(bf16[2,768,128]{2,1,0:T(8,128)(2,1)S(1)} %collective-permute-done.14.refs_12_.refs_20_.refs_28_.refs_36_) | copy-start | bytes 1179652
  74.8 0.8 copy-start.24
  75.6 13.9 %copy-start.12 = (s32[14]{0:T(128)S(1)}, s32[14]{0:T(128)}, u32[]{:S(2)}) copy-start(s32[14]{0:T(128)} %concatenate.3.ids) | copy-start | bytes 172
  89.5 0.7 copy-start.16
  90.8 6.4 %copy-start.15 = (bf16[8,256,128]{2,1,0:T(8,128)(2,1)}, bf16[8,256,128]{2,1,0:T(8,128)(2,1)S(1)}, u32[]{:S(2)}) copy-start(bf16[8,256,128]{2,1,0:T(8,128)(2,1)S(1)} %copy.20.refs_3_) | copy-start | bytes 1572868
  90.8 6.4 %collective-permute-start.17 = (bf16[8,256,128]{2,1,0:T(8,128)(2,1)S(1)}, bf16[8,256,128]{2,1,0:T(8,128)(2,1)S(1)}, u32[]{:S(2)}, u32[]{:S(2)}) collective-permute-start(bf16[8,256,128]{2,1,0:T(8,128)(2,1)S(1)} %copy.20.refs_3_), channel_id=1, source_target_pairs={{0,1},{1,0},{2,3},{3,2},{4,5},{5,4},{6,7},{7,6},{8,9},{9,8},{10,11... | collective-permute-start | bytes 1572872 | tf_op jit(solution)/shard_map/ppermute | solution.py:635
  97.2 0.8 copy-start.27

commit v4 on v3

--- a/solution.py
+++ b/solution.py
@@ -706,7 +706,7 @@
         meta,
         [total, restored],
         [((chips, width, P_SIZE), jnp.bfloat16), (TOKEN.shape, TOKEN.dtype)],
-        idle=[token, low, *across, *pieces],
+        idle=[token, low, *across, *pieces[:3]],
     )
     entering = exchanged(entering)
     pieces += [apart(piece, 1) for piece in pieces]

time: 105 us -> 113 us (1.076)
  waiting for transfers between devices: 25.6 us -> 32.6 us
  Pallas kernels: 42 us -> 47.5 us
  starting transfers between devices: 27.8 us -> 25 us
  local copies, waits for them, and re-layouts: 9.15 us -> 7.93 us
    ppermute x16, waiting for transfers between devices: 25.6 us -> 32.6 us  [apart(): lax.ppermute(block, 'ctx', [(i, i ^ distance) for i in range(devices)])]
    pallas_call x1, Pallas kernels: 13.8 us -> 18.5 us  [attend(): pl.pallas_call(scalars(attend_kernel), out_shape=[jax.ShapeDtypeStruct((T...]
    ppermute x16, starting transfers between devices: 13.2 us -> 10.3 us  [apart(): lax.ppermute(block, 'ctx', [(i, i ^ distance) for i in range(devices)])]
    unnamed x56 -> x54, local copies, waits for them, and re-layouts: 6 us -> 4.81 us
  transfers between devices with their start and end apart: 20 -> 20, of which waited for: 9 -> 6; matrix products, arithmetic and copies ran while one was open for 3% -> 3% of each run, Pallas kernels for 31% -> 33%
where the time goes in v4:
time: 113 us; the launch traced here: 114 us
  Pallas kernels  47.5 us (42%)
  waiting for transfers between devices  32.6 us (29%)
  starting transfers between devices  25 us (22%)
  local copies, waits for them, and re-layouts  7.93 us (7%)
    ppermute x16, waiting for transfers between devices, apart(): lax.ppermute(block, 'ctx', [(i, i ^ distance) for i in range(devices)])  32.6 us
    pallas_call x1, Pallas kernels, attend(): pl.pallas_call(scalars(attend_kernel), out_shape=[jax.ShapeDtypeStruct((T...  18.5 us
    ppermute x16, starting transfers between devices, apart(): lax.ppermute(block, 'ctx', [(i, i ^ distance) for i in range(devices)])  10.3 us
    pallas_call x6, Pallas kernels, whole(): pl.pallas_call(kernel, out_shape=[jax.ShapeDtypeStruct(s, t) for s, t in...  9.49 us
    all_to_all x2, starting transfers between devices, exchanged(): lax.all_to_all(block, 'ctx', 0, 0, axis_index_groups=same_core, tiled=True)  8.2 us
    pallas_call x1, Pallas kernels, finish(): pl.pallas_call(scalars(finish_kernel, local), out_shape=jax.ShapeDtypeStr...  7.42 us
    pallas_call x1, Pallas kernels, intra(): pl.pallas_call(scalars(intra_kernel), out_shape=[jax.ShapeDtypeStruct((TO...  6.78 us
    pallas_call x1, Pallas kernels, summaries(): pl.pallas_call(scalars(summary_kernel, local), out_shape=[shape, shape],...  5.24 us
  transfers between devices with their start and end apart: 20, of which 6 were waited for; matrix products, arithmetic and copies ran while one was open for 3% of the time, Pallas kernels for 33%

profile of v4, /device:TPU:0, one launch (start us, length us, event | category | flops | bytes accessed | tf_op | source)
XLA Modules:
  0.0 113.9 jit_solution(12477966464840466020)
XLA Ops:
  0.6 3.0 %collective-permute-start.2 = (f32[3,4,8192]{2,1,0:T(4,128)}, f32[3,4,8192]{2,1,0:T(4,128)}, u32[]{:S(2)}, u32[]{:S(2)}) collective-permute-start(f32[3,4,8192]{2,1,0:T(4,128)} %bitcast.24), channel_id=1, source_target_pairs={{16,0},{0,16},{17,1},{1,17},{18,2},{2,18},{19,3},{3,19},{20,4},{4,... | collective-permute-start | bytes 1179656 | tf_op jit(solution)/shard_map/ppermute | solution.py:643
  3.6 1.3 %concatenate.3.ids = s32[14]{0:T(128)} concatenate(s32[1]{0:T(128)} %bitcast, s32[1]{0:T(128)} %bitcast.1, s32[3]{0:T(128)} %bitcast.27, s32[3]{0:T(128)} %bitcast.28, s32[6]{0:T(128)} %param.24), dimensions={0} | concatenate | bytes 112 | tf_op jit(solution)/shard_map/concatenate | solution.py:629
  4.9 2.6 %pack.1 = (bf16[1,512,128]{2,1,0:T(8,128)(2,1)}, bf16[1,512,128]{2,1,0:T(8,128)(2,1)}, bf16[2,128,512]{2,1,0:T(8,128)(2,1)}) custom-call(s32[14]{0:T(128)} %concatenate.3.ids, bf16[3,32,512]{2,1,0:T(8,128)(2,1)} %bitcast.38, bf16[3,32,512]{2,1,0:T(8,128)(2,1)} %bitcast.39, bf16[128,512]{1,0:T(8,128)(2,1)} %bitcast.32, bf16[128,512]{1,0:T(8,128)(2,1)} %bitcast.33), custom_call_target="tpu_custom_call" | custom-call | flops 34359738368 | bytes 1048576 | tf_op jit(solution)/shard_map/pack/pallas_call | solution.py:173
  7.5 2.6 %collective-permute-start.1 = (bf16[1,512,128]{2,1,0:T(8,128)(2,1)}, bf16[1,512,128]{2,1,0:T(8,128)(2,1)S(1)}, u32[]{:S(2)}, u32[]{:S(2)}) collective-permute-start(bf16[1,512,128]{2,1,0:T(8,128)(2,1)} %get-tuple-element.18.refs_4_), channel_id=1, source_target_pairs={{0,8},{1,9},{2,10},{3,11},{4,12},{5,13},{6,14},{7,15},{8,0},{9,1},... | collective-permute-start | bytes 393224 | tf_op jit(solution)/shard_map/ppermute | solution.py:635
  10.1 3.5 %collective-permute-start.4 = (bf16[2,128,512]{2,1,0:T(8,128)(2,1)}, bf16[2,128,512]{2,1,0:T(8,128)(2,1)S(1)}, u32[]{:S(2)}, u32[]{:S(2)}) collective-permute-start(bf16[2,128,512]{2,1,0:T(8,128)(2,1)} %get-tuple-element.24.refs_4_.refs_3_), channel_id=1, source_target_pairs={{0,4},{1,5},{2,6},{3,7},{4,8},{5,9},{6,10},{7,11},{8,12},{9,13},{1... | collective-permute-start | bytes 786440 | tf_op jit(solution)/shard_map/ppermute | solution.py:599
  13.6 0.0 copy-start.25
  13.6 5.2 %summaries.1 = (bf16[8,272,128]{2,1,0:T(8,128)(2,1)}, bf16[8,272,128]{2,1,0:T(8,128)(2,1)}) custom-call(s32[14]{0:T(128)} %concatenate.3.ids, bf16[128,8192]{1,0:T(8,128)(2,1)} %bitcast.29, bf16[64,128]{1,0:T(8,128)(2,1)} %bitcast.42, bf16[64,128]{1,0:T(8,128)(2,1)} %bitcast.40, bf16[128,512]{1,0:T(8,128)(2,1)} %bitcast.34, ...), custom_call_target="tpu_custom_call" | custom-call | flops 34359738368 | bytes 1048576 | tf_op jit(solution)/shard_map/summaries/pallas_call | solution.py:139
  18.8 0.0 collective-permute-start
  18.8 0.4 reshape_squeeze.3.refs_0_
  19.3 0.0 collective-permute-done.2
  19.3 1.4 %reshape.7.refs_1_ = f32[3,4,128,64]{3,2,1,0:T(8,128)S(1)} reshape(f32[3,4,8192]{2,1,0:T(4,128)} %collective-permute-done.2) | data formatting | bytes 786432 | tf_op jit(solution)/shard_map/reshape | solution.py:644
  20.7 0.0 copy-start.13
  20.7 1.0 copy-done.13
  21.7 0.8 restore.1
  22.6 0.8 copy-done.16
  23.3 0.3 collective-permute-start.3
  23.7 0.2 collective-permute-start.9
  23.9 0.0 collective-permute-done.1.refs_1_
  23.9 0.3 collective-permute-start.5
  24.2 0.0 collective-permute-done.4.refs_5_.refs_1_
  24.2 0.2 collective-permute-start.6
  24.4 5.2 %collective-permute-done.3.refs_3_ = bf16[1,256,128]{2,1,0:T(8,128)(2,1)S(1)} collective-permute-done((bf16[1,256,128]{2,1,0:T(8,128)(2,1)S(1)}, bf16[1,256,128]{2,1,0:T(8,128)(2,1)S(1)}, u32[]{:S(2)}, u32[]{:S(2)}) %collective-permute-start.3) | collective-permute-done | bytes 65568 | tf_op jit(solution)/shard_map/ppermute | solution.py:635
  29.6 0.0 collective-permute-done.refs_6_.refs_1_
  29.6 1.3 %join_two.1 = (bf16[2,768,128]{2,1,0:T(8,128)(2,1)S(1)}, bf16[2,128,512]{2,1,0:T(8,128)(2,1)}) custom-call(s32[14]{0:T(128)S(1)} %copy-done.9, bf16[1,512,128]{2,1,0:T(8,128)(2,1)S(1)} %copy-done.18, bf16[1,512,128]{2,1,0:T(8,128)(2,1)S(1)} %collective-permute-done.1.refs_1_, bf16[1,256,128]{2,1,0:T(8,128)(2,1)S(1)} %get-tuple-element.22.refs_2_, ...), custom_call_target="tpu_custom_call" | custom-call | flops 34359738368 | bytes 1048576 | tf_op jit(solution)/shard_map/join_two/pallas_call | solution.py:173
  30.9 0.0 copy-done.4
  30.9 1.5 %collective-permute-start.7 = (bf16[2,128,512]{2,1,0:T(8,128)(2,1)}, bf16[2,128,512]{2,1,0:T(8,128)(2,1)}, u32[]{:S(2)}, u32[]{:S(2)}) collective-permute-start(bf16[2,128,512]{2,1,0:T(8,128)(2,1)} %get-tuple-element.29), channel_id=1, source_target_pairs={{0,2},{1,3},{2,0},{3,1},{4,6},{5,7},{6,4},{7,5},{8,10},{9,11},{10,... | collective-permute-start | bytes 786440 | tf_op jit(solution)/shard_map/ppermute | solution.py:635
  32.4 0.5 collective-permute-start.11
  32.9 0.0 copy-done.12
  32.9 2.7 %combine.1.refs_6_ = bf16[8,272,128]{2,1,0:T(8,128)(2,1)} custom-call(s32[14]{0:T(128)S(1)} %copy-done.9, bf16[8,272,128]{2,1,0:T(8,128)(2,1)} %get-tuple-element.19.refs_0_, bf16[8,272,128]{2,1,0:T(8,128)(2,1)S(1)} %collective-permute-done.refs_6_.refs_1_, bf16[2,768,128]{2,1,0:T(8,128)(2,1)S(1)} %get-tuple-element.25.refs_2_.refs_7_.refs_15_.refs_23_.refs_31_), custom_call_target="tpu_custom_call" | custom-call | flops 34359738368 | bytes 1048576 | tf_op jit(solution)/shard_map/combine/pallas_call | solution.py:173
  35.6 3.5 %all-to-all-start = ((bf16[8,272,128]{2,1,0:T(8,128)(2,1)}), bf16[8,272,128]{2,1,0:T(8,128)(2,1)S(1)}, u32[]{:S(2)}, u32[]{:S(2)}) async-start(bf16[8,272,128]{2,1,0:T(8,128)(2,1)} %combine.1.refs_6_), calls=%async_computation | async-start | bytes 1114112 | tf_op jit(solution)/shard_map/all_to_all | solution.py:638
  39.1 0.0 collective-permute-done.9.refs_6_
  39.2 2.0 %collective-permute-start.10 = (bf16[2,768,128]{2,1,0:T(8,128)(2,1)S(1)}, bf16[2,768,128]{2,1,0:T(8,128)(2,1)S(1)}, u32[]{:S(2)}, u32[]{:S(2)}) collective-permute-start(bf16[2,768,128]{2,1,0:T(8,128)(2,1)S(1)} %get-tuple-element.25.refs_2_.refs_7_.refs_15_.refs_23_.refs_31_), channel_id=1, source_target_pairs={{0,4},{1,5},{2,6},{3,7},{4,0},{5,1},{6,2},{7,3},{8,12},{9,13},{10,... | collective-permute-start | bytes 1179656 | tf_op jit(solution)/shard_map/ppermute | solution.py:635
  41.1 0.0 collective-permute-done.7.refs_2_
  41.1 0.0 collective-permute-start.8
  41.2 6.8 %intra.1 = (f32[128,8192]{1,0:T(8,128)}, f32[8,128]{1,0:T(8,128)}) custom-call(s32[14]{0:T(128)} %concatenate.3.ids, f32[64]{0:T(128)} %refs_0_.1, bf16[128,8192]{1,0:T(8,128)(2,1)} %bitcast.30, bf16[64,128]{1,0:T(8,128)(2,1)} %bitcast.43, bf16[64,128]{1,0:T(8,128)(2,1)} %bitcast.41, bf16[128,512]{1,0:T(8,128)(2,1)} %bitcast.35, bf16[128,512]{1,0:T(8,128)(2,1)} %bitcast.36, ...), custom_call_target="tpu_custom_call" | custom-call | flops 34359738368 | bytes 1048576 | tf_op jit(solution)/shard_map/intra/pallas_call | solution.py:323
  47.9 0.0 collective-permute-done.6.refs_4_
  48.0 0.0 collective-permute-done.5.refs_3_.refs_5_
  48.0 5.0 %collective-permute-done.11.refs_9_.refs_17_.refs_25_.refs_33_ = bf16[2,768,128]{2,1,0:T(8,128)(2,1)S(1)} collective-permute-done((bf16[2,768,128]{2,1,0:T(8,128)(2,1)S(1)}, bf16[2,768,128]{2,1,0:T(8,128)(2,1)S(1)}, u32[]{:S(2)}, u32[]{:S(2)}) %collective-permute-start.11) | collective-permute-done | bytes 393248 | tf_op jit(solution)/shard_map/ppermute | solution.py:635
  52.9 5.8 %collective-permute-done.10.refs_8_.refs_16_.refs_24_.refs_32_ = bf16[2,768,128]{2,1,0:T(8,128)(2,1)S(1)} collective-permute-done((bf16[2,768,128]{2,1,0:T(8,128)(2,1)S(1)}, bf16[2,768,128]{2,1,0:T(8,128)(2,1)S(1)}, u32[]{:S(2)}, u32[]{:S(2)}) %collective-permute-start.10) | collective-permute-done | bytes 393248 | tf_op jit(solution)/shard_map/ppermute | solution.py:635
  58.7 0.0 collective-permute-done.8.refs_5_
  58.7 0.0 all-to-all-done.refs_0_
  58.8 0.7 copy-done.19
  59.5 1.6 %recurrence.1 = (bf16[8,256,128]{2,1,0:T(8,128)(2,1)}, f32[8,128]{1,0:T(8,128)S(1)}) custom-call(s32[14]{0:T(128)S(1)} %copy-done.10, bf16[8,272,128]{2,1,0:T(8,128)(2,1)S(1)} %all-to-all-done.refs_0_, f32[3,256,128]{2,1,0:T(8,128)S(1)} %copy-done.17, f32[8,128]{1,0:T(8,128)S(1)} %copy-done.19, bf16[8,272,128]{2,1,0:T(8,128)(2,1)} %collective-permute-done.5.refs_3_.refs_5_, ...), custom_call_target="tpu_custom_call" | custom-call | flops 34359738368 | bytes 1048576 | tf_op jit(solution)/shard_map/recurrence/pallas_call | solution.py:173
  61.0 0.0 copy-done.6
  61.0 4.7 %all-to-all-start.1 = ((bf16[8,256,128]{2,1,0:T(8,128)(2,1)}), bf16[8,256,128]{2,1,0:T(8,128)(2,1)S(1)}, u32[]{:S(2)}, u32[]{:S(2)}) async-start(bf16[8,256,128]{2,1,0:T(8,128)(2,1)} %get-tuple-element.30), calls=%async_computation.1 | async-start | bytes 1048576 | tf_op jit(solution)/shard_map/all_to_all | solution.py:638
  65.7 2.0 %collective-permute-start.12 = (bf16[2,768,128]{2,1,0:T(8,128)(2,1)S(1)}, bf16[2,768,128]{2,1,0:T(8,128)(2,1)S(1)}, u32[]{:S(2)}, u32[]{:S(2)}) collective-permute-start(bf16[2,768,128]{2,1,0:T(8,128)(2,1)S(1)} %collective-permute-done.10.refs_8_.refs_16_.refs_24_.refs_32_), channel_id=1, source_target_pairs={{0,2},{1,3},{2,0},{3,1},{4,6},{5,7},{6,4},{7,5},{8,10},{9,11},{10,... | collective-permute-start | bytes 1179656 | tf_op jit(solution)/shard_map/ppermute | solution.py:635
  67.7 0.0 collective-permute-start.13
  67.7 0.5 collective-permute-start.15
  68.2 0.1 collective-permute-start.14
  68.3 13.1 %collective-permute-done.12.refs_10_.refs_18_.refs_26_.refs_34_ = bf16[2,768,128]{2,1,0:T(8,128)(2,1)S(1)} collective-permute-done((bf16[2,768,128]{2,1,0:T(8,128)(2,1)S(1)}, bf16[2,768,128]{2,1,0:T(8,128)(2,1)S(1)}, u32[]{:S(2)}, u32[]{:S(2)}) %collective-permute-start.12) | collective-permute-done | bytes 393248 | tf_op jit(solution)/shard_map/ppermute | solution.py:635
  81.4 0.0 collective-permute-start.16
  81.4 0.0 collective-permute-done.13.refs_11_.refs_19_.refs_27_.refs_35_
  81.4 0.0 collective-permute-done.15.refs_13_.refs_21_.refs_29_.refs_37_
  81.4 0.0 collective-permute-done.14.refs_12_.refs_20_.refs_28_.refs_36_
  81.5 1.7 %collective-permute-done.16.refs_14_.refs_22_.refs_30_.refs_38_ = bf16[2,768,128]{2,1,0:T(8,128)(2,1)S(1)} collective-permute-done((bf16[2,768,128]{2,1,0:T(8,128)(2,1)S(1)}, bf16[2,768,128]{2,1,0:T(8,128)(2,1)S(1)}, u32[]{:S(2)}, u32[]{:S(2)}) %collective-permute-start.16) | collective-permute-done | bytes 393248 | tf_op jit(solution)/shard_map/ppermute | solution.py:635
  83.1 0.7 copy-done.24
  83.9 18.5 %attend.1 = (bf16[128,4096]{1,0:T(8,128)(2,1)}, f32[8,128]{1,0:T(8,128)}) custom-call(s32[14]{0:T(128)} %concatenate.3.ids, bf16[128,4096]{1,0:T(8,128)(2,1)} %bitcast.23, bf16[2,128,512]{2,1,0:T(8,128)(2,1)} %copy-done.4, bf16[2,128,512]{2,1,0:T(8,128)(2,1)} %collective-permute-done.7.refs_2_, bf16[2,128,512]{2,1,0:T(8,128)(2,1)} %get-tuple-element.24.refs_4_.refs_3_, ...), custom_call_target="tpu_custom_call" | custom-call | flops 1024 | bytes 1024 | tf_op jit(solution)/shard_map/attend/pallas_call | solution.py:566
  102.4 0.0 all-to-all-done.1.refs_0_
  102.5 0.7 copy-done.15
  103.1 0.6 copy.20.refs_3_
  103.7 0.1 collective-permute-start.17
  103.8 1.9 %collective-permute-done.17.refs_4_ = bf16[8,256,128]{2,1,0:T(8,128)(2,1)S(1)} collective-permute-done((bf16[8,256,128]{2,1,0:T(8,128)(2,1)S(1)}, bf16[8,256,128]{2,1,0:T(8,128)(2,1)S(1)}, u32[]{:S(2)}, u32[]{:S(2)}) %collective-permute-start.17) | collective-permute-done | bytes 524320 | tf_op jit(solution)/shard_map/ppermute | solution.py:635
  105.7 0.8 copy-done.26
  106.5 7.4 %finish.1 = bf16[128,8192]{1,0:T(8,128)(2,1)} custom-call(s32[14]{0:T(128)} %concatenate.3.ids, f32[128,8192]{1,0:T(8,128)} %get-tuple-element.26.refs_0_, bf16[64,128]{1,0:T(8,128)(2,1)} %bitcast.44, bf16[128,512]{1,0:T(8,128)(2,1)} %bitcast.37, bf16[8,256,128]{2,1,0:T(8,128)(2,1)} %copy-done.14, bf16[8,256,128]{2,1,0:T(8,128)(2,1)} %copy-done.26, ...), custom_call_target="tpu_custom_call" | custom-call | flops 34359738368 | bytes 1048576 | tf_op jit(solution)/shard_map/finish/pallas_call | solution.py:411
  (43 shorter events, 0.1 us)
Async XLA Ops:
  0.6 18.6 %collective-permute-start.2 = (f32[3,4,8192]{2,1,0:T(4,128)}, f32[3,4,8192]{2,1,0:T(4,128)}, u32[]{:S(2)}, u32[]{:S(2)}) collective-permute-start(f32[3,4,8192]{2,1,0:T(4,128)} %bitcast.24), channel_id=1, source_target_pairs={{16,0},{0,16},{17,1},{1,17},{18,2},{2,18},{19,3},{3,19},{20,4},{4,... | collective-permute-start | bytes 1179656 | tf_op jit(solution)/shard_map/ppermute | solution.py:643
  7.5 16.4 %collective-permute-start.1 = (bf16[1,512,128]{2,1,0:T(8,128)(2,1)}, bf16[1,512,128]{2,1,0:T(8,128)(2,1)S(1)}, u32[]{:S(2)}, u32[]{:S(2)}) collective-permute-start(bf16[1,512,128]{2,1,0:T(8,128)(2,1)} %get-tuple-element.18.refs_4_), channel_id=1, source_target_pairs={{0,8},{1,9},{2,10},{3,11},{4,12},{5,13},{6,14},{7,15},{8,0},{9,1},... | collective-permute-start | bytes 393224 | tf_op jit(solution)/shard_map/ppermute | solution.py:635
  10.1 14.1 %collective-permute-start.4 = (bf16[2,128,512]{2,1,0:T(8,128)(2,1)}, bf16[2,128,512]{2,1,0:T(8,128)(2,1)S(1)}, u32[]{:S(2)}, u32[]{:S(2)}) collective-permute-start(bf16[2,128,512]{2,1,0:T(8,128)(2,1)} %get-tuple-element.24.refs_4_.refs_3_), channel_id=1, source_target_pairs={{0,4},{1,5},{2,6},{3,7},{4,8},{5,9},{6,10},{7,11},{8,12},{9,13},{1... | collective-permute-start | bytes 786440 | tf_op jit(solution)/shard_map/ppermute | solution.py:599
  13.6 5.3 %copy-start.25 = (f32[1,3,4,8192]{3,2,1,0:T(4,128)S(1)}, f32[1,3,4,8192]{3,2,1,0:T(4,128)}, u32[]{:S(2)}) copy-start(f32[1,3,4,8192]{3,2,1,0:T(4,128)} %param.23) | copy-start | bytes 1179652
  18.8 1.8 %copy-start.9 = (s32[14]{0:T(128)S(1)}, s32[14]{0:T(128)}, u32[]{:S(2)}) copy-start(s32[14]{0:T(128)} %concatenate.3.ids) | copy-start | bytes 172
  18.8 10.7 %collective-permute-start = (bf16[8,272,128]{2,1,0:T(8,128)(2,1)}, bf16[8,272,128]{2,1,0:T(8,128)(2,1)S(1)}, u32[]{:S(2)}, u32[]{:S(2)}) collective-permute-start(bf16[8,272,128]{2,1,0:T(8,128)(2,1)} %get-tuple-element.20.refs_2_), channel_id=1, source_target_pairs={{0,1},{1,0},{2,3},{3,2},{4,5},{5,4},{6,7},{7,6},{8,9},{9,8},{10,11... | collective-permute-start | bytes 1671176 | tf_op jit(solution)/shard_map/ppermute | solution.py:635
  20.7 1.1 copy-start.13
  21.7 1.9 %copy-start.3 = (bf16[2,128,512]{2,1,0:T(8,128)(2,1)S(1)}, bf16[2,128,512]{2,1,0:T(8,128)(2,1)}, u32[]{:S(2)}) copy-start(bf16[2,128,512]{2,1,0:T(8,128)(2,1)} %get-tuple-element.24.refs_4_.refs_3_) | copy-start | bytes 786436
  21.7 7.9 %copy-start.18 = (bf16[1,512,128]{2,1,0:T(8,128)(2,1)S(1)}, bf16[1,512,128]{2,1,0:T(8,128)(2,1)}, u32[]{:S(2)}) copy-start(bf16[1,512,128]{2,1,0:T(8,128)(2,1)} %get-tuple-element.21.refs_0_) | copy-start | bytes 393220
  22.6 0.8 copy-start.16
  23.3 6.2 %collective-permute-start.3 = (bf16[1,256,128]{2,1,0:T(8,128)(2,1)S(1)}, bf16[1,256,128]{2,1,0:T(8,128)(2,1)S(1)}, u32[]{:S(2)}, u32[]{:S(2)}) collective-permute-start(bf16[1,256,128]{2,1,0:T(8,128)(2,1)S(1)} %get-tuple-element.23), channel_id=1, source_target_pairs={{0,8},{1,9},{2,10},{3,11},{4,12},{5,13},{6,14},{7,15},{8,0},{9,1},... | collective-permute-start | bytes 196616 | tf_op jit(solution)/shard_map/ppermute | solution.py:635
  23.7 15.5 %collective-permute-start.9 = (bf16[2,128,512]{2,1,0:T(8,128)(2,1)S(1)}, bf16[2,128,512]{2,1,0:T(8,128)(2,1)S(1)}, u32[]{:S(2)}, u32[]{:S(2)}) collective-permute-start(bf16[2,128,512]{2,1,0:T(8,128)(2,1)S(1)} %copy-done.3), channel_id=1, source_target_pairs={{0,1},{1,0},{2,3},{3,2},{4,5},{5,4},{6,7},{7,6},{8,9},{9,8},{10,11... | collective-permute-start | bytes 786440 | tf_op jit(solution)/shard_map/ppermute | solution.py:635
  23.9 24.1 %collective-permute-start.5 = (bf16[8,272,128]{2,1,0:T(8,128)(2,1)}, bf16[8,272,128]{2,1,0:T(8,128)(2,1)}, u32[]{:S(2)}, u32[]{:S(2)}) collective-permute-start(bf16[8,272,128]{2,1,0:T(8,128)(2,1)} %get-tuple-element.19.refs_0_), channel_id=1, source_target_pairs={{0,1},{1,0},{2,3},{3,2},{4,5},{5,4},{6,7},{7,6},{8,9},{9,8},{10,11... | collective-permute-start | bytes 1671176 | tf_op jit(solution)/shard_map/ppermute | solution.py:635
  24.2 6.7 %copy-start.4 = (bf16[2,128,512]{2,1,0:T(8,128)(2,1)}, bf16[2,128,512]{2,1,0:T(8,128)(2,1)S(1)}, u32[]{:S(2)}) copy-start(bf16[2,128,512]{2,1,0:T(8,128)(2,1)S(1)} %collective-permute-done.4.refs_5_.refs_1_) | copy-start | bytes 786436
  24.2 23.8 %collective-permute-start.6 = (bf16[2,128,512]{2,1,0:T(8,128)(2,1)S(1)}, bf16[2,128,512]{2,1,0:T(8,128)(2,1)S(1)}, u32[]{:S(2)}, u32[]{:S(2)}) collective-permute-start(bf16[2,128,512]{2,1,0:T(8,128)(2,1)S(1)} %collective-permute-done.4.refs_5_.refs_1_), channel_id=1, source_target_pairs={{0,1},{1,0},{2,3},{3,2},{4,5},{5,4},{6,7},{7,6},{8,9},{9,8},{10,11... | collective-permute-start | bytes 786440 | tf_op jit(solution)/shard_map/ppermute | solution.py:635
  29.6 3.4 %copy-start.12 = (bf16[8,272,128]{2,1,0:T(8,128)(2,1)}, bf16[8,272,128]{2,1,0:T(8,128)(2,1)S(1)}, u32[]{:S(2)}) copy-start(bf16[8,272,128]{2,1,0:T(8,128)(2,1)S(1)} %collective-permute-done.refs_6_.refs_1_) | copy-start | bytes 1671172
  30.9 36.8 %copy-start = (bf16[2,768,128]{2,1,0:T(8,128)(2,1)}, bf16[2,768,128]{2,1,0:T(8,128)(2,1)S(1)}, u32[]{:S(2)}) copy-start(bf16[2,768,128]{2,1,0:T(8,128)(2,1)S(1)} %get-tuple-element.25.refs_2_.refs_7_.refs_15_.refs_23_.refs_31_) | copy-start | bytes 1179652
  30.9 10.2 %collective-permute-start.7 = (bf16[2,128,512]{2,1,0:T(8,128)(2,1)}, bf16[2,128,512]{2,1,0:T(8,128)(2,1)}, u32[]{:S(2)}, u32[]{:S(2)}) collective-permute-start(bf16[2,128,512]{2,1,0:T(8,128)(2,1)} %get-tuple-element.29), channel_id=1, source_target_pairs={{0,2},{1,3},{2,0},{3,1},{4,6},{5,7},{6,4},{7,5},{8,10},{9,11},{10,... | collective-permute-start | bytes 786440 | tf_op jit(solution)/shard_map/ppermute | solution.py:635
  32.4 20.5 %collective-permute-start.11 = (bf16[2,768,128]{2,1,0:T(8,128)(2,1)S(1)}, bf16[2,768,128]{2,1,0:T(8,128)(2,1)S(1)}, u32[]{:S(2)}, u32[]{:S(2)}) collective-permute-start(bf16[2,768,128]{2,1,0:T(8,128)(2,1)S(1)} %get-tuple-element.25.refs_2_.refs_7_.refs_15_.refs_23_.refs_31_), channel_id=1, source_target_pairs={{0,2},{1,3},{2,0},{3,1},{4,6},{5,7},{6,4},{7,5},{8,10},{9,11},{10,... | collective-permute-start | bytes 1179656 | tf_op jit(solution)/shard_map/ppermute | solution.py:635
  35.6 23.1 %all-to-all-start = ((bf16[8,272,128]{2,1,0:T(8,128)(2,1)}), bf16[8,272,128]{2,1,0:T(8,128)(2,1)S(1)}, u32[]{:S(2)}, u32[]{:S(2)}) async-start(bf16[8,272,128]{2,1,0:T(8,128)(2,1)} %combine.1.refs_6_), calls=%async_computation | async-start | bytes 1114112 | tf_op jit(solution)/shard_map/all_to_all | solution.py:638
  39.2 19.6 %copy-start.5 = (bf16[2,128,512]{2,1,0:T(8,128)(2,1)}, bf16[2,128,512]{2,1,0:T(8,128)(2,1)S(1)}, u32[]{:S(2)}) copy-start(bf16[2,128,512]{2,1,0:T(8,128)(2,1)S(1)} %collective-permute-done.9.refs_6_) | copy-start | bytes 786436
  39.2 19.6 %collective-permute-start.10 = (bf16[2,768,128]{2,1,0:T(8,128)(2,1)S(1)}, bf16[2,768,128]{2,1,0:T(8,128)(2,1)S(1)}, u32[]{:S(2)}, u32[]{:S(2)}) collective-permute-start(bf16[2,768,128]{2,1,0:T(8,128)(2,1)S(1)} %get-tuple-element.25.refs_2_.refs_7_.refs_15_.refs_23_.refs_31_), channel_id=1, source_target_pairs={{0,4},{1,5},{2,6},{3,7},{4,0},{5,1},{6,2},{7,3},{8,12},{9,13},{10,... | collective-permute-start | bytes 1179656 | tf_op jit(solution)/shard_map/ppermute | solution.py:635
  41.1 17.6 %collective-permute-start.8 = (bf16[2,128,512]{2,1,0:T(8,128)(2,1)}, bf16[2,128,512]{2,1,0:T(8,128)(2,1)S(1)}, u32[]{:S(2)}, u32[]{:S(2)}) collective-permute-start(bf16[2,128,512]{2,1,0:T(8,128)(2,1)} %collective-permute-done.7.refs_2_), channel_id=1, source_target_pairs={{0,1},{1,0},{2,3},{3,2},{4,5},{5,4},{6,7},{7,6},{8,9},{9,8},{10,11... | collective-permute-start | bytes 786440 | tf_op jit(solution)/shard_map/ppermute | solution.py:635
  41.1 17.6 %copy-start.10 = (s32[14]{0:T(128)S(1)}, s32[14]{0:T(128)}, u32[]{:S(2)}) copy-start(s32[14]{0:T(128)} %concatenate.3.ids) | copy-start | bytes 172
  41.2 17.6 %copy-start.17 = (f32[3,256,128]{2,1,0:T(8,128)S(1)}, f32[3,256,128]{2,1,0:T(8,128)}, u32[]{:S(2)}) copy-start(f32[3,256,128]{2,1,0:T(8,128)} %copy-done.16) | copy-start | bytes 1179652
  47.9 13.1 %copy-start.6 = (bf16[2,128,512]{2,1,0:T(8,128)(2,1)}, bf16[2,128,512]{2,1,0:T(8,128)(2,1)S(1)}, u32[]{:S(2)}) copy-start(bf16[2,128,512]{2,1,0:T(8,128)(2,1)S(1)} %collective-permute-done.6.refs_4_) | copy-start | bytes 786436
  52.9 14.8 %copy-start.1 = (bf16[2,768,128]{2,1,0:T(8,128)(2,1)}, bf16[2,768,128]{2,1,0:T(8,128)(2,1)S(1)}, u32[]{:S(2)}) copy-start(bf16[2,768,128]{2,1,0:T(8,128)(2,1)S(1)} %collective-permute-done.11.refs_9_.refs_17_.refs_25_.refs_33_) | copy-start | bytes 1179652
  58.7 9.5 %copy-start.2 = (bf16[2,768,128]{2,1,0:T(8,128)(2,1)}, bf16[2,768,128]{2,1,0:T(8,128)(2,1)S(1)}, u32[]{:S(2)}) copy-start(bf16[2,768,128]{2,1,0:T(8,128)(2,1)S(1)} %collective-permute-done.10.refs_8_.refs_16_.refs_24_.refs_32_) | copy-start | bytes 1179652
  58.7 2.3 %copy-start.7 = (bf16[2,128,512]{2,1,0:T(8,128)(2,1)}, bf16[2,128,512]{2,1,0:T(8,128)(2,1)S(1)}, u32[]{:S(2)}) copy-start(bf16[2,128,512]{2,1,0:T(8,128)(2,1)S(1)} %collective-permute-done.8.refs_5_) | copy-start | bytes 786436
  58.8 0.7 copy-start.19
  61.0 22.8 %copy-start.8 = (f32[8,128]{1,0:T(8,128)}, f32[8,128]{1,0:T(8,128)S(1)}, u32[]{:S(2)}) copy-start(f32[8,128]{1,0:T(8,128)S(1)} %get-tuple-element.31.refs_41_) | copy-start | bytes 12292
  61.0 41.4 %all-to-all-start.1 = ((bf16[8,256,128]{2,1,0:T(8,128)(2,1)}), bf16[8,256,128]{2,1,0:T(8,128)(2,1)S(1)}, u32[]{:S(2)}, u32[]{:S(2)}) async-start(bf16[8,256,128]{2,1,0:T(8,128)(2,1)} %get-tuple-element.30), calls=%async_computation.1 | async-start | bytes 1048576 | tf_op jit(solution)/shard_map/all_to_all | solution.py:638
  65.7 15.7 %collective-permute-start.12 = (bf16[2,768,128]{2,1,0:T(8,128)(2,1)S(1)}, bf16[2,768,128]{2,1,0:T(8,128)(2,1)S(1)}, u32[]{:S(2)}, u32[]{:S(2)}) collective-permute-start(bf16[2,768,128]{2,1,0:T(8,128)(2,1)S(1)} %collective-permute-done.10.refs_8_.refs_16_.refs_24_.refs_32_), channel_id=1, source_target_pairs={{0,2},{1,3},{2,0},{3,1},{4,6},{5,7},{6,4},{7,5},{8,10},{9,11},{10,... | collective-permute-start | bytes 1179656 | tf_op jit(solution)/shard_map/ppermute | solution.py:635
  67.7 13.7 %collective-permute-start.13 = (bf16[2,768,128]{2,1,0:T(8,128)(2,1)S(1)}, bf16[2,768,128]{2,1,0:T(8,128)(2,1)S(1)}, u32[]{:S(2)}, u32[]{:S(2)}) collective-permute-start(bf16[2,768,128]{2,1,0:T(8,128)(2,1)S(1)} %get-tuple-element.25.refs_2_.refs_7_.refs_15_.refs_23_.refs_31_), channel_id=1, source_target_pairs={{0,1},{1,0},{2,3},{3,2},{4,5},{5,4},{6,7},{7,6},{8,9},{9,8},{10,11... | collective-permute-start | bytes 1179656 | tf_op jit(solution)/shard_map/ppermute | solution.py:635
  67.7 13.7 %collective-permute-start.15 = (bf16[2,768,128]{2,1,0:T(8,128)(2,1)S(1)}, bf16[2,768,128]{2,1,0:T(8,128)(2,1)S(1)}, u32[]{:S(2)}, u32[]{:S(2)}) collective-permute-start(bf16[2,768,128]{2,1,0:T(8,128)(2,1)S(1)} %collective-permute-done.11.refs_9_.refs_17_.refs_25_.refs_33_), channel_id=1, source_target_pairs={{0,1},{1,0},{2,3},{3,2},{4,5},{5,4},{6,7},{7,6},{8,9},{9,8},{10,11... | collective-permute-start | bytes 1179656 | tf_op jit(solution)/shard_map/ppermute | solution.py:635
  68.2 13.2 %collective-permute-start.14 = (bf16[2,768,128]{2,1,0:T(8,128)(2,1)S(1)}, bf16[2,768,128]{2,1,0:T(8,128)(2,1)S(1)}, u32[]{:S(2)}, u32[]{:S(2)}) collective-permute-start(bf16[2,768,128]{2,1,0:T(8,128)(2,1)S(1)} %collective-permute-done.10.refs_8_.refs_16_.refs_24_.refs_32_), channel_id=1, source_target_pairs={{0,1},{1,0},{2,3},{3,2},{4,5},{5,4},{6,7},{7,6},{8,9},{9,8},{10,11... | collective-permute-start | bytes 1179656 | tf_op jit(solution)/shard_map/ppermute | solution.py:635
  81.4 2.5 %copy-start.20 = (bf16[2,768,128]{2,1,0:T(8,128)(2,1)}, bf16[2,768,128]{2,1,0:T(8,128)(2,1)S(1)}, u32[]{:S(2)}) copy-start(bf16[2,768,128]{2,1,0:T(8,128)(2,1)S(1)} %collective-permute-done.12.refs_10_.refs_18_.refs_26_.refs_34_) | copy-start | bytes 1179652
  81.4 1.7 %collective-permute-start.16 = (bf16[2,768,128]{2,1,0:T(8,128)(2,1)S(1)}, bf16[2,768,128]{2,1,0:T(8,128)(2,1)S(1)}, u32[]{:S(2)}, u32[]{:S(2)}) collective-permute-start(bf16[2,768,128]{2,1,0:T(8,128)(2,1)S(1)} %collective-permute-done.12.refs_10_.refs_18_.refs_26_.refs_34_), channel_id=1, source_target_pairs={{0,1},{1,0},{2,3},{3,2},{4,5},{5,4},{6,7},{7,6},{8,9},{9,8},{10,11... | collective-permute-start | bytes 1179656 | tf_op jit(solution)/shard_map/ppermute | solution.py:635
  81.4 2.5 %copy-start.21 = (bf16[2,768,128]{2,1,0:T(8,128)(2,1)}, bf16[2,768,128]{2,1,0:T(8,128)(2,1)S(1)}, u32[]{:S(2)}) copy-start(bf16[2,768,128]{2,1,0:T(8,128)(2,1)S(1)} %collective-permute-done.13.refs_11_.refs_19_.refs_27_.refs_35_) | copy-start | bytes 1179652
  81.4 2.5 %copy-start.22 = (bf16[2,768,128]{2,1,0:T(8,128)(2,1)}, bf16[2,768,128]{2,1,0:T(8,128)(2,1)S(1)}, u32[]{:S(2)}) copy-start(bf16[2,768,128]{2,1,0:T(8,128)(2,1)S(1)} %collective-permute-done.15.refs_13_.refs_21_.refs_29_.refs_37_) | copy-start | bytes 1179652
  81.4 2.4 %copy-start.23 = (bf16[2,768,128]{2,1,0:T(8,128)(2,1)}, bf16[2,768,128]{2,1,0:T(8,128)(2,1)S(1)}, u32[]{:S(2)}) copy-start(bf16[2,768,128]{2,1,0:T(8,128)(2,1)S(1)} %collective-permute-done.14.refs_12_.refs_20_.refs_28_.refs_36_) | copy-start | bytes 1179652
  83.1 0.8 copy-start.24
  83.9 18.5 %copy-start.11 = (s32[14]{0:T(128)S(1)}, s32[14]{0:T(128)}, u32[]{:S(2)}) copy-start(s32[14]{0:T(128)} %concatenate.3.ids) | copy-start | bytes 172
  102.4 0.7 copy-start.15
  103.7 2.0 %copy-start.14 = (bf16[8,256,128]{2,1,0:T(8,128)(2,1)}, bf16[8,256,128]{2,1,0:T(8,128)(2,1)S(1)}, u32[]{:S(2)}) copy-start(bf16[8,256,128]{2,1,0:T(8,128)(2,1)S(1)} %copy.20.refs_3_) | copy-start | bytes 1572868
  103.7 2.0 %collective-permute-start.17 = (bf16[8,256,128]{2,1,0:T(8,128)(2,1)S(1)}, bf16[8,256,128]{2,1,0:T(8,128)(2,1)S(1)}, u32[]{:S(2)}, u32[]{:S(2)}) collective-permute-start(bf16[8,256,128]{2,1,0:T(8,128)(2,1)S(1)} %copy.20.refs_3_), channel_id=1, source_target_pairs={{0,1},{1,0},{2,3},{3,2},{4,5},{5,4},{6,7},{7,6},{8,9},{9,8},{10,11... | collective-permute-start | bytes 1572872 | tf_op jit(solution)/shard_map/ppermute | solution.py:635
  105.7 0.8 copy-start.26

commit v5 on v3

--- a/solution.py
+++ b/solution.py
@@ -26,7 +26,7 @@
 EXTRA = 16
 BLOCK = 64
 SPAN = WINDOW + BLOCK
-COLUMNS = SPAN + 64
+COLUMNS = SPAN + 16
 NEG = -1e30
 TOKEN = jax.ShapeDtypeStruct((8, 128), jnp.float32)
 SHORT = pl.CostEstimate(flops=1024, bytes_accessed=1024, transcendentals=0)

time: 105 us -> 104 us (level)
  the two profiles are of different devices: /device:TPU:0 before, /device:TPU:29 now
where the time goes in v5:
time: 104 us; the launch traced here: 103 us
  Pallas kernels  45.3 us (44%)
  starting transfers between devices  27.3 us (26%)
  waiting for transfers between devices  20.6 us (20%)
  local copies, waits for them, and re-layouts  9.15 us (9%)
    ppermute x16, waiting for transfers between devices, apart(): lax.ppermute(block, 'ctx', [(i, i ^ distance) for i in range(devices)])  20.6 us
    pallas_call x1, Pallas kernels, attend(): pl.pallas_call(scalars(attend_kernel), out_shape=[jax.ShapeDtypeStruct((T...  17.1 us
    all_to_all x2, starting transfers between devices, exchanged(): lax.all_to_all(block, 'ctx', 0, 0, axis_index_groups=same_core, tiled=True)  12.7 us
    ppermute x16, starting transfers between devices, apart(): lax.ppermute(block, 'ctx', [(i, i ^ distance) for i in range(devices)])  12.1 us
    pallas_call x6, Pallas kernels, whole(): pl.pallas_call(kernel, out_shape=[jax.ShapeDtypeStruct(s, t) for s, t in...  8.76 us
    pallas_call x1, Pallas kernels, finish(): pl.pallas_call(scalars(finish_kernel, local), out_shape=jax.ShapeDtypeStr...  7.42 us
    pallas_call x1, Pallas kernels, intra(): pl.pallas_call(scalars(intra_kernel), out_shape=[jax.ShapeDtypeStruct((TO...  6.73 us
    unnamed x56, local copies, waits for them, and re-layouts  6 us
  transfers between devices with their start and end apart: 20, of which 8 were waited for; matrix products, arithmetic and copies ran while one was open for 3% of the time, Pallas kernels for 35%

profile of v5, /device:TPU:29, one launch (start us, length us, event | category | flops | bytes accessed | tf_op | source)
XLA Modules:
  0.0 103.2 jit_solution(3580878358398981400)
XLA Ops:
  0.6 1.3 %collective-permute-start.2 = (f32[3,4,8192]{2,1,0:T(4,128)}, f32[3,4,8192]{2,1,0:T(4,128)}, u32[]{:S(2)}, u32[]{:S(2)}) collective-permute-start(f32[3,4,8192]{2,1,0:T(4,128)} %bitcast.24), channel_id=1, source_target_pairs={{16,0},{0,16},{17,1},{1,17},{18,2},{2,18},{19,3},{3,19},{20,4},{4,... | collective-permute-start | bytes 1179656 | tf_op jit(solution)/shard_map/ppermute | solution.py:643
  1.9 1.3 %concatenate.3.ids = s32[14]{0:T(128)} concatenate(s32[1]{0:T(128)} %bitcast, s32[1]{0:T(128)} %bitcast.1, s32[3]{0:T(128)} %bitcast.27, s32[3]{0:T(128)} %bitcast.28, s32[6]{0:T(128)} %param.24), dimensions={0} | concatenate | bytes 112 | tf_op jit(solution)/shard_map/concatenate | solution.py:629
  3.2 2.5 %pack.1 = (bf16[1,512,128]{2,1,0:T(8,128)(2,1)}, bf16[1,512,128]{2,1,0:T(8,128)(2,1)}, bf16[2,128,512]{2,1,0:T(8,128)(2,1)}) custom-call(s32[14]{0:T(128)} %concatenate.3.ids, bf16[3,32,512]{2,1,0:T(8,128)(2,1)} %bitcast.38, bf16[3,32,512]{2,1,0:T(8,128)(2,1)} %bitcast.39, bf16[128,512]{1,0:T(8,128)(2,1)} %bitcast.32, bf16[128,512]{1,0:T(8,128)(2,1)} %bitcast.33), custom_call_target="tpu_custom_call" | custom-call | flops 34359738368 | bytes 1048576 | tf_op jit(solution)/shard_map/pack/pallas_call | solution.py:173
  5.8 0.1 collective-permute-start.1
  5.8 1.3 %collective-permute-start.4 = (bf16[2,128,512]{2,1,0:T(8,128)(2,1)}, bf16[2,128,512]{2,1,0:T(8,128)(2,1)S(1)}, u32[]{:S(2)}, u32[]{:S(2)}) collective-permute-start(bf16[2,128,512]{2,1,0:T(8,128)(2,1)} %get-tuple-element.24.refs_4_.refs_3_), channel_id=1, source_target_pairs={{0,4},{1,5},{2,6},{3,7},{4,8},{5,9},{6,10},{7,11},{8,12},{9,13},{1... | collective-permute-start | bytes 786440 | tf_op jit(solution)/shard_map/ppermute | solution.py:599
  7.1 0.0 copy-start.25
  7.1 5.2 %summaries.1 = (bf16[8,272,128]{2,1,0:T(8,128)(2,1)}, bf16[8,272,128]{2,1,0:T(8,128)(2,1)}) custom-call(s32[14]{0:T(128)} %concatenate.3.ids, bf16[128,8192]{1,0:T(8,128)(2,1)} %bitcast.29, bf16[64,128]{1,0:T(8,128)(2,1)} %bitcast.42, bf16[64,128]{1,0:T(8,128)(2,1)} %bitcast.40, bf16[128,512]{1,0:T(8,128)(2,1)} %bitcast.34, ...), custom_call_target="tpu_custom_call" | custom-call | flops 34359738368 | bytes 1048576 | tf_op jit(solution)/shard_map/summaries/pallas_call | solution.py:139
  12.4 1.2 %collective-permute-start = (bf16[8,272,128]{2,1,0:T(8,128)(2,1)}, bf16[8,272,128]{2,1,0:T(8,128)(2,1)S(1)}, u32[]{:S(2)}, u32[]{:S(2)}) collective-permute-start(bf16[8,272,128]{2,1,0:T(8,128)(2,1)} %get-tuple-element.20.refs_2_), channel_id=1, source_target_pairs={{0,1},{1,0},{2,3},{3,2},{4,5},{5,4},{6,7},{7,6},{8,9},{9,8},{10,11... | collective-permute-start | bytes 1671176 | tf_op jit(solution)/shard_map/ppermute | solution.py:635
  13.6 0.4 reshape_squeeze.3.refs_0_
  14.0 0.0 collective-permute-done.2
  14.1 1.4 %reshape.7.refs_1_ = f32[3,4,128,64]{3,2,1,0:T(8,128)S(1)} reshape(f32[3,4,8192]{2,1,0:T(4,128)} %collective-permute-done.2) | data formatting | bytes 786432 | tf_op jit(solution)/shard_map/reshape | solution.py:644
  15.5 0.0 copy-start.14
  15.5 1.0 %copy-done.14 = bf16[8,272,128]{2,1,0:T(8,128)(2,1)S(1)} copy-done((bf16[8,272,128]{2,1,0:T(8,128)(2,1)S(1)}, bf16[8,272,128]{2,1,0:T(8,128)(2,1)}, u32[]{:S(2)}) %copy-start.14) | copy-done | bytes 557080
  16.5 0.8 restore.1
  17.4 0.8 copy-done.17
  18.2 2.9 %collective-permute-start.3 = (bf16[1,256,128]{2,1,0:T(8,128)(2,1)S(1)}, bf16[1,256,128]{2,1,0:T(8,128)(2,1)S(1)}, u32[]{:S(2)}, u32[]{:S(2)}) collective-permute-start(bf16[1,256,128]{2,1,0:T(8,128)(2,1)S(1)} %get-tuple-element.23), channel_id=1, source_target_pairs={{0,8},{1,9},{2,10},{3,11},{4,12},{5,13},{6,14},{7,15},{8,0},{9,1},... | collective-permute-start | bytes 196616 | tf_op jit(solution)/shard_map/ppermute | solution.py:635
  21.1 0.3 collective-permute-start.9
  21.4 0.0 collective-permute-done.1.refs_1_
  21.4 0.2 collective-permute-start.5
  21.6 0.0 collective-permute-done.4.refs_5_.refs_1_
  21.6 0.3 collective-permute-start.6
  21.9 1.6 %collective-permute-done.3.refs_3_ = bf16[1,256,128]{2,1,0:T(8,128)(2,1)S(1)} collective-permute-done((bf16[1,256,128]{2,1,0:T(8,128)(2,1)S(1)}, bf16[1,256,128]{2,1,0:T(8,128)(2,1)S(1)}, u32[]{:S(2)}, u32[]{:S(2)}) %collective-permute-start.3) | collective-permute-done | bytes 65568 | tf_op jit(solution)/shard_map/ppermute | solution.py:635
  23.6 0.0 collective-permute-done.refs_6_.refs_1_
  23.6 0.6 join_two.1
  24.2 0.3 collective-permute-start.7
  24.5 2.0 %collective-permute-start.10 = (bf16[2,768,128]{2,1,0:T(8,128)(2,1)S(1)}, bf16[2,768,128]{2,1,0:T(8,128)(2,1)S(1)}, u32[]{:S(2)}, u32[]{:S(2)}) collective-permute-start(bf16[2,768,128]{2,1,0:T(8,128)(2,1)S(1)} %get-tuple-element.25.refs_2_.refs_7_.refs_15_.refs_23_.refs_31_), channel_id=1, source_target_pairs={{0,4},{1,5},{2,6},{3,7},{4,0},{5,1},{6,2},{7,3},{8,12},{9,13},{10,... | collective-permute-start | bytes 1179656 | tf_op jit(solution)/shard_map/ppermute | solution.py:635
  26.5 2.6 %combine.1.refs_6_ = bf16[8,272,128]{2,1,0:T(8,128)(2,1)} custom-call(s32[14]{0:T(128)S(1)} %copy-done.10, bf16[8,272,128]{2,1,0:T(8,128)(2,1)} %get-tuple-element.19.refs_0_, bf16[8,272,128]{2,1,0:T(8,128)(2,1)S(1)} %collective-permute-done.refs_6_.refs_1_, bf16[2,768,128]{2,1,0:T(8,128)(2,1)S(1)} %get-tuple-element.25.refs_2_.refs_7_.refs_15_.refs_23_.refs_31_), custom_call_target="tpu_custom_call" | custom-call | flops 34359738368 | bytes 1048576 | tf_op jit(solution)/shard_map/combine/pallas_call | solution.py:173
  29.1 7.3 %all-to-all-start = ((bf16[8,272,128]{2,1,0:T(8,128)(2,1)}), bf16[8,272,128]{2,1,0:T(8,128)(2,1)S(1)}, u32[]{:S(2)}, u32[]{:S(2)}) async-start(bf16[8,272,128]{2,1,0:T(8,128)(2,1)} %combine.1.refs_6_), calls=%async_computation | async-start | bytes 1114112 | tf_op jit(solution)/shard_map/all_to_all | solution.py:638
  36.4 0.0 collective-permute-done.9.refs_6_
  36.4 0.3 collective-permute-start.11
  36.7 0.0 collective-permute-done.7.refs_2_
  36.7 1.3 %collective-permute-start.8 = (bf16[2,128,512]{2,1,0:T(8,128)(2,1)S(1)}, bf16[2,128,512]{2,1,0:T(8,128)(2,1)S(1)}, u32[]{:S(2)}, u32[]{:S(2)}) collective-permute-start(bf16[2,128,512]{2,1,0:T(8,128)(2,1)S(1)} %collective-permute-done.7.refs_2_), channel_id=1, source_target_pairs={{0,1},{1,0},{2,3},{3,2},{4,5},{5,4},{6,7},{7,6},{8,9},{9,8},{10,11... | collective-permute-start | bytes 786440 | tf_op jit(solution)/shard_map/ppermute | solution.py:635
  38.0 0.0 collective-permute-done.10.refs_8_.refs_16_.refs_24_.refs_32_
  38.0 1.2 %collective-permute-start.12 = (bf16[2,768,128]{2,1,0:T(8,128)(2,1)S(1)}, bf16[2,768,128]{2,1,0:T(8,128)(2,1)S(1)}, u32[]{:S(2)}, u32[]{:S(2)}) collective-permute-start(bf16[2,768,128]{2,1,0:T(8,128)(2,1)S(1)} %collective-permute-done.10.refs_8_.refs_16_.refs_24_.refs_32_), channel_id=1, source_target_pairs={{0,2},{1,3},{2,0},{3,1},{4,6},{5,7},{6,4},{7,5},{8,10},{9,11},{10,... | collective-permute-start | bytes 1179656 | tf_op jit(solution)/shard_map/ppermute | solution.py:635
  39.2 6.7 %intra.1 = (f32[128,8192]{1,0:T(8,128)}, f32[8,128]{1,0:T(8,128)}) custom-call(s32[14]{0:T(128)} %concatenate.3.ids, f32[64]{0:T(128)} %refs_0_.1, bf16[128,8192]{1,0:T(8,128)(2,1)} %bitcast.30, bf16[64,128]{1,0:T(8,128)(2,1)} %bitcast.43, bf16[64,128]{1,0:T(8,128)(2,1)} %bitcast.41, bf16[128,512]{1,0:T(8,128)(2,1)} %bitcast.35, bf16[128,512]{1,0:T(8,128)(2,1)} %bitcast.36, ...), custom_call_target="tpu_custom_call" | custom-call | flops 34359738368 | bytes 1048576 | tf_op jit(solution)/shard_map/intra/pallas_call | solution.py:323
  46.0 0.0 copy-done.26
  46.0 0.0 collective-permute-done.6.refs_4_
  46.0 0.0 copy-start.7
  46.0 0.0 collective-permute-done.5.refs_3_.refs_5_
  46.0 6.2 %collective-permute-done.11.refs_9_.refs_17_.refs_25_.refs_33_ = bf16[2,768,128]{2,1,0:T(8,128)(2,1)S(1)} collective-permute-done((bf16[2,768,128]{2,1,0:T(8,128)(2,1)S(1)}, bf16[2,768,128]{2,1,0:T(8,128)(2,1)S(1)}, u32[]{:S(2)}, u32[]{:S(2)}) %collective-permute-start.11) | collective-permute-done | bytes 393248 | tf_op jit(solution)/shard_map/ppermute | solution.py:635
  52.2 0.0 collective-permute-done.8.refs_5_
  52.2 8.4 %collective-permute-done.12.refs_10_.refs_18_.refs_26_.refs_34_ = bf16[2,768,128]{2,1,0:T(8,128)(2,1)S(1)} collective-permute-done((bf16[2,768,128]{2,1,0:T(8,128)(2,1)S(1)}, bf16[2,768,128]{2,1,0:T(8,128)(2,1)S(1)}, u32[]{:S(2)}, u32[]{:S(2)}) %collective-permute-start.12) | collective-permute-done | bytes 393248 | tf_op jit(solution)/shard_map/ppermute | solution.py:635
  60.6 0.0 all-to-all-done.refs_0_
  60.6 1.1 %copy-done.18 = f32[3,256,128]{2,1,0:T(8,128)S(1)} copy-done((f32[3,256,128]{2,1,0:T(8,128)S(1)}, f32[3,256,128]{2,1,0:T(8,128)}, u32[]{:S(2)}) %copy-start.18) | copy-done | bytes 393240
  61.8 0.7 copy-done.20
  62.4 1.6 %recurrence.1 = (bf16[8,256,128]{2,1,0:T(8,128)(2,1)}, f32[8,128]{1,0:T(8,128)S(1)}) custom-call(s32[14]{0:T(128)S(1)} %copy-done.11, bf16[8,272,128]{2,1,0:T(8,128)(2,1)S(1)} %all-to-all-done.refs_0_, f32[3,256,128]{2,1,0:T(8,128)S(1)} %copy-done.18, f32[8,128]{1,0:T(8,128)S(1)} %copy-done.20, bf16[8,272,128]{2,1,0:T(8,128)(2,1)} %collective-permute-done.5.refs_3_.refs_5_, ...), custom_call_target="tpu_custom_call" | custom-call | flops 34359738368 | bytes 1048576 | tf_op jit(solution)/shard_map/recurrence/pallas_call | solution.py:173
  64.0 5.4 %all-to-all-start.1 = ((bf16[8,256,128]{2,1,0:T(8,128)(2,1)}), bf16[8,256,128]{2,1,0:T(8,128)(2,1)S(1)}, u32[]{:S(2)}, u32[]{:S(2)}) async-start(bf16[8,256,128]{2,1,0:T(8,128)(2,1)} %get-tuple-element.30), calls=%async_computation.1 | async-start | bytes 1048576 | tf_op jit(solution)/shard_map/all_to_all | solution.py:638
  69.5 1.3 %collective-permute-start.13 = (bf16[2,768,128]{2,1,0:T(8,128)(2,1)S(1)}, bf16[2,768,128]{2,1,0:T(8,128)(2,1)S(1)}, u32[]{:S(2)}, u32[]{:S(2)}) collective-permute-start(bf16[2,768,128]{2,1,0:T(8,128)(2,1)S(1)} %get-tuple-element.25.refs_2_.refs_7_.refs_15_.refs_23_.refs_31_), channel_id=1, source_target_pairs={{0,1},{1,0},{2,3},{3,2},{4,5},{5,4},{6,7},{7,6},{8,9},{9,8},{10,11... | collective-permute-start | bytes 1179656 | tf_op jit(solution)/shard_map/ppermute | solution.py:635
  70.7 0.1 collective-permute-start.15
  70.8 0.4 collective-permute-start.14
  71.3 0.1 collective-permute-start.16
  71.3 0.8 collective-permute-done.13.refs_11_.refs_19_.refs_27_.refs_35_
  72.1 0.6 collective-permute-done.15.refs_13_.refs_21_.refs_29_.refs_37_
  72.7 0.6 collective-permute-done.14.refs_12_.refs_20_.refs_28_.refs_36_
  73.2 0.6 collective-permute-done.16.refs_14_.refs_22_.refs_30_.refs_38_
  73.8 0.8 copy-done.24
  74.6 17.1 %attend.1 = (bf16[128,4096]{1,0:T(8,128)(2,1)}, f32[8,128]{1,0:T(8,128)}) custom-call(s32[14]{0:T(128)} %concatenate.3.ids, bf16[128,4096]{1,0:T(8,128)(2,1)} %bitcast.23, bf16[2,128,512]{2,1,0:T(8,128)(2,1)} %copy-done.5, bf16[2,128,512]{2,1,0:T(8,128)(2,1)} %copy-done.26, bf16[2,128,512]{2,1,0:T(8,128)(2,1)} %get-tuple-element.24.refs_4_.refs_3_, ...), custom_call_target="tpu_custom_call" | custom-call | flops 1024 | bytes 1024 | tf_op jit(solution)/shard_map/attend/pallas_call | solution.py:566
  91.7 0.0 all-to-all-done.1.refs_0_
  91.8 0.7 copy-done.16
  92.4 0.6 copy.20.refs_3_
  93.0 0.1 collective-permute-start.17
  93.1 1.9 %collective-permute-done.17.refs_4_ = bf16[8,256,128]{2,1,0:T(8,128)(2,1)S(1)} collective-permute-done((bf16[8,256,128]{2,1,0:T(8,128)(2,1)S(1)}, bf16[8,256,128]{2,1,0:T(8,128)(2,1)S(1)}, u32[]{:S(2)}, u32[]{:S(2)}) %collective-permute-start.17) | collective-permute-done | bytes 524320 | tf_op jit(solution)/shard_map/ppermute | solution.py:635
  95.0 0.8 copy-done.27
  95.8 7.4 %finish.1 = bf16[128,8192]{1,0:T(8,128)(2,1)} custom-call(s32[14]{0:T(128)} %concatenate.3.ids, f32[128,8192]{1,0:T(8,128)} %get-tuple-element.26.refs_0_, bf16[64,128]{1,0:T(8,128)(2,1)} %bitcast.44, bf16[128,512]{1,0:T(8,128)(2,1)} %bitcast.37, bf16[8,256,128]{2,1,0:T(8,128)(2,1)} %copy-done.15, bf16[8,256,128]{2,1,0:T(8,128)(2,1)} %copy-done.27, ...), custom_call_target="tpu_custom_call" | custom-call | flops 34359738368 | bytes 1048576 | tf_op jit(solution)/shard_map/finish/pallas_call | solution.py:411
  (45 shorter events, 0.1 us)
Async XLA Ops:
  0.6 13.4 %collective-permute-start.2 = (f32[3,4,8192]{2,1,0:T(4,128)}, f32[3,4,8192]{2,1,0:T(4,128)}, u32[]{:S(2)}, u32[]{:S(2)}) collective-permute-start(f32[3,4,8192]{2,1,0:T(4,128)} %bitcast.24), channel_id=1, source_target_pairs={{16,0},{0,16},{17,1},{1,17},{18,2},{2,18},{19,3},{3,19},{20,4},{4,... | collective-permute-start | bytes 1179656 | tf_op jit(solution)/shard_map/ppermute | solution.py:643
  5.8 15.6 %collective-permute-start.1 = (bf16[1,512,128]{2,1,0:T(8,128)(2,1)}, bf16[1,512,128]{2,1,0:T(8,128)(2,1)S(1)}, u32[]{:S(2)}, u32[]{:S(2)}) collective-permute-start(bf16[1,512,128]{2,1,0:T(8,128)(2,1)} %get-tuple-element.18.refs_4_), channel_id=1, source_target_pairs={{0,8},{1,9},{2,10},{3,11},{4,12},{5,13},{6,14},{7,15},{8,0},{9,1},... | collective-permute-start | bytes 393224 | tf_op jit(solution)/shard_map/ppermute | solution.py:635
  5.8 15.8 %collective-permute-start.4 = (bf16[2,128,512]{2,1,0:T(8,128)(2,1)}, bf16[2,128,512]{2,1,0:T(8,128)(2,1)S(1)}, u32[]{:S(2)}, u32[]{:S(2)}) collective-permute-start(bf16[2,128,512]{2,1,0:T(8,128)(2,1)} %get-tuple-element.24.refs_4_.refs_3_), channel_id=1, source_target_pairs={{0,4},{1,5},{2,6},{3,7},{4,8},{5,9},{6,10},{7,11},{8,12},{9,13},{1... | collective-permute-start | bytes 786440 | tf_op jit(solution)/shard_map/ppermute | solution.py:599
  7.1 6.5 %copy-start.25 = (f32[1,3,4,8192]{3,2,1,0:T(4,128)S(1)}, f32[1,3,4,8192]{3,2,1,0:T(4,128)}, u32[]{:S(2)}) copy-start(f32[1,3,4,8192]{3,2,1,0:T(4,128)} %param.23) | copy-start | bytes 1179652
  12.4 3.1 %copy-start.10 = (s32[14]{0:T(128)S(1)}, s32[14]{0:T(128)}, u32[]{:S(2)}) copy-start(s32[14]{0:T(128)} %concatenate.3.ids) | copy-start | bytes 172
  12.4 11.2 %collective-permute-start = (bf16[8,272,128]{2,1,0:T(8,128)(2,1)}, bf16[8,272,128]{2,1,0:T(8,128)(2,1)S(1)}, u32[]{:S(2)}, u32[]{:S(2)}) collective-permute-start(bf16[8,272,128]{2,1,0:T(8,128)(2,1)} %get-tuple-element.20.refs_2_), channel_id=1, source_target_pairs={{0,1},{1,0},{2,3},{3,2},{4,5},{5,4},{6,7},{7,6},{8,9},{9,8},{10,11... | collective-permute-start | bytes 1671176 | tf_op jit(solution)/shard_map/ppermute | solution.py:635
  15.5 1.1 %copy-start.14 = (bf16[8,272,128]{2,1,0:T(8,128)(2,1)S(1)}, bf16[8,272,128]{2,1,0:T(8,128)(2,1)}, u32[]{:S(2)}) copy-start(bf16[8,272,128]{2,1,0:T(8,128)(2,1)} %get-tuple-element.20.refs_2_) | copy-start | bytes 1671172
  16.5 4.6 %copy-start.4 = (bf16[2,128,512]{2,1,0:T(8,128)(2,1)S(1)}, bf16[2,128,512]{2,1,0:T(8,128)(2,1)}, u32[]{:S(2)}) copy-start(bf16[2,128,512]{2,1,0:T(8,128)(2,1)} %get-tuple-element.24.refs_4_.refs_3_) | copy-start | bytes 786436
  16.5 7.0 %copy-start.19 = (bf16[1,512,128]{2,1,0:T(8,128)(2,1)S(1)}, bf16[1,512,128]{2,1,0:T(8,128)(2,1)}, u32[]{:S(2)}) copy-start(bf16[1,512,128]{2,1,0:T(8,128)(2,1)} %get-tuple-element.21.refs_0_) | copy-start | bytes 393220
  17.4 0.8 copy-start.17
  18.2 5.4 %collective-permute-start.3 = (bf16[1,256,128]{2,1,0:T(8,128)(2,1)S(1)}, bf16[1,256,128]{2,1,0:T(8,128)(2,1)S(1)}, u32[]{:S(2)}, u32[]{:S(2)}) collective-permute-start(bf16[1,256,128]{2,1,0:T(8,128)(2,1)S(1)} %get-tuple-element.23), channel_id=1, source_target_pairs={{0,8},{1,9},{2,10},{3,11},{4,12},{5,13},{6,14},{7,15},{8,0},{9,1},... | collective-permute-start | bytes 196616 | tf_op jit(solution)/shard_map/ppermute | solution.py:635
  21.1 15.3 %collective-permute-start.9 = (bf16[2,128,512]{2,1,0:T(8,128)(2,1)S(1)}, bf16[2,128,512]{2,1,0:T(8,128)(2,1)S(1)}, u32[]{:S(2)}, u32[]{:S(2)}) collective-permute-start(bf16[2,128,512]{2,1,0:T(8,128)(2,1)S(1)} %copy-done.4), channel_id=1, source_target_pairs={{0,1},{1,0},{2,3},{3,2},{4,5},{5,4},{6,7},{7,6},{8,9},{9,8},{10,11... | collective-permute-start | bytes 786440 | tf_op jit(solution)/shard_map/ppermute | solution.py:635
  21.4 24.6 %collective-permute-start.5 = (bf16[8,272,128]{2,1,0:T(8,128)(2,1)}, bf16[8,272,128]{2,1,0:T(8,128)(2,1)}, u32[]{:S(2)}, u32[]{:S(2)}) collective-permute-start(bf16[8,272,128]{2,1,0:T(8,128)(2,1)} %get-tuple-element.19.refs_0_), channel_id=1, source_target_pairs={{0,1},{1,0},{2,3},{3,2},{4,5},{5,4},{6,7},{7,6},{8,9},{9,8},{10,11... | collective-permute-start | bytes 1671176 | tf_op jit(solution)/shard_map/ppermute | solution.py:635
  21.6 2.5 %copy-start.5 = (bf16[2,128,512]{2,1,0:T(8,128)(2,1)}, bf16[2,128,512]{2,1,0:T(8,128)(2,1)S(1)}, u32[]{:S(2)}) copy-start(bf16[2,128,512]{2,1,0:T(8,128)(2,1)S(1)} %collective-permute-done.4.refs_5_.refs_1_) | copy-start | bytes 786436
  21.6 24.4 %collective-permute-start.6 = (bf16[2,128,512]{2,1,0:T(8,128)(2,1)S(1)}, bf16[2,128,512]{2,1,0:T(8,128)(2,1)S(1)}, u32[]{:S(2)}, u32[]{:S(2)}) collective-permute-start(bf16[2,128,512]{2,1,0:T(8,128)(2,1)S(1)} %collective-permute-done.4.refs_5_.refs_1_), channel_id=1, source_target_pairs={{0,1},{1,0},{2,3},{3,2},{4,5},{5,4},{6,7},{7,6},{8,9},{9,8},{10,11... | collective-permute-start | bytes 786440 | tf_op jit(solution)/shard_map/ppermute | solution.py:635
  23.6 2.9 %copy-start.13 = (bf16[8,272,128]{2,1,0:T(8,128)(2,1)}, bf16[8,272,128]{2,1,0:T(8,128)(2,1)S(1)}, u32[]{:S(2)}) copy-start(bf16[8,272,128]{2,1,0:T(8,128)(2,1)S(1)} %collective-permute-done.refs_6_.refs_1_) | copy-start | bytes 1671172
  24.2 45.3 %copy-start = (bf16[2,768,128]{2,1,0:T(8,128)(2,1)}, bf16[2,768,128]{2,1,0:T(8,128)(2,1)S(1)}, u32[]{:S(2)}) copy-start(bf16[2,768,128]{2,1,0:T(8,128)(2,1)S(1)} %get-tuple-element.25.refs_2_.refs_7_.refs_15_.refs_23_.refs_31_) | copy-start | bytes 1179652
  24.2 12.6 %collective-permute-start.7 = (bf16[2,128,512]{2,1,0:T(8,128)(2,1)S(1)}, bf16[2,128,512]{2,1,0:T(8,128)(2,1)S(1)}, u32[]{:S(2)}, u32[]{:S(2)}) collective-permute-start(bf16[2,128,512]{2,1,0:T(8,128)(2,1)S(1)} %get-tuple-element.29), channel_id=1, source_target_pairs={{0,2},{1,3},{2,0},{3,1},{4,6},{5,7},{6,4},{7,5},{8,10},{9,11},{10,... | collective-permute-start | bytes 786440 | tf_op jit(solution)/shard_map/ppermute | solution.py:635
  24.5 13.5 %collective-permute-start.10 = (bf16[2,768,128]{2,1,0:T(8,128)(2,1)S(1)}, bf16[2,768,128]{2,1,0:T(8,128)(2,1)S(1)}, u32[]{:S(2)}, u32[]{:S(2)}) collective-permute-start(bf16[2,768,128]{2,1,0:T(8,128)(2,1)S(1)} %get-tuple-element.25.refs_2_.refs_7_.refs_15_.refs_23_.refs_31_), channel_id=1, source_target_pairs={{0,4},{1,5},{2,6},{3,7},{4,0},{5,1},{6,2},{7,3},{8,12},{9,13},{10,... | collective-permute-start | bytes 1179656 | tf_op jit(solution)/shard_map/ppermute | solution.py:635
  29.1 31.5 %all-to-all-start = ((bf16[8,272,128]{2,1,0:T(8,128)(2,1)}), bf16[8,272,128]{2,1,0:T(8,128)(2,1)S(1)}, u32[]{:S(2)}, u32[]{:S(2)}) async-start(bf16[8,272,128]{2,1,0:T(8,128)(2,1)} %combine.1.refs_6_), calls=%async_computation | async-start | bytes 1114112 | tf_op jit(solution)/shard_map/all_to_all | solution.py:638
  36.4 24.2 %copy-start.6 = (bf16[2,128,512]{2,1,0:T(8,128)(2,1)}, bf16[2,128,512]{2,1,0:T(8,128)(2,1)S(1)}, u32[]{:S(2)}) copy-start(bf16[2,128,512]{2,1,0:T(8,128)(2,1)S(1)} %collective-permute-done.9.refs_6_) | copy-start | bytes 786436
  36.4 15.8 %collective-permute-start.11 = (bf16[2,768,128]{2,1,0:T(8,128)(2,1)S(1)}, bf16[2,768,128]{2,1,0:T(8,128)(2,1)S(1)}, u32[]{:S(2)}, u32[]{:S(2)}) collective-permute-start(bf16[2,768,128]{2,1,0:T(8,128)(2,1)S(1)} %get-tuple-element.25.refs_2_.refs_7_.refs_15_.refs_23_.refs_31_), channel_id=1, source_target_pairs={{0,2},{1,3},{2,0},{3,1},{4,6},{5,7},{6,4},{7,5},{8,10},{9,11},{10,... | collective-permute-start | bytes 1179656 | tf_op jit(solution)/shard_map/ppermute | solution.py:635
  36.7 9.2 %copy-start.26 = (bf16[2,128,512]{2,1,0:T(8,128)(2,1)}, bf16[2,128,512]{2,1,0:T(8,128)(2,1)S(1)}, u32[]{:S(2)}) copy-start(bf16[2,128,512]{2,1,0:T(8,128)(2,1)S(1)} %collective-permute-done.7.refs_2_) | copy-start | bytes 786436
  36.7 15.4 %collective-permute-start.8 = (bf16[2,128,512]{2,1,0:T(8,128)(2,1)S(1)}, bf16[2,128,512]{2,1,0:T(8,128)(2,1)S(1)}, u32[]{:S(2)}, u32[]{:S(2)}) collective-permute-start(bf16[2,128,512]{2,1,0:T(8,128)(2,1)S(1)} %collective-permute-done.7.refs_2_), channel_id=1, source_target_pairs={{0,1},{1,0},{2,3},{3,2},{4,5},{5,4},{6,7},{7,6},{8,9},{9,8},{10,11... | collective-permute-start | bytes 786440 | tf_op jit(solution)/shard_map/ppermute | solution.py:635
  38.0 32.8 %copy-start.1 = (bf16[2,768,128]{2,1,0:T(8,128)(2,1)}, bf16[2,768,128]{2,1,0:T(8,128)(2,1)S(1)}, u32[]{:S(2)}) copy-start(bf16[2,768,128]{2,1,0:T(8,128)(2,1)S(1)} %collective-permute-done.10.refs_8_.refs_16_.refs_24_.refs_32_) | copy-start | bytes 1179652
  38.0 22.6 %collective-permute-start.12 = (bf16[2,768,128]{2,1,0:T(8,128)(2,1)S(1)}, bf16[2,768,128]{2,1,0:T(8,128)(2,1)S(1)}, u32[]{:S(2)}, u32[]{:S(2)}) collective-permute-start(bf16[2,768,128]{2,1,0:T(8,128)(2,1)S(1)} %collective-permute-done.10.refs_8_.refs_16_.refs_24_.refs_32_), channel_id=1, source_target_pairs={{0,2},{1,3},{2,0},{3,1},{4,6},{5,7},{6,4},{7,5},{8,10},{9,11},{10,... | collective-permute-start | bytes 1179656 | tf_op jit(solution)/shard_map/ppermute | solution.py:635
  39.2 21.4 %copy-start.11 = (s32[14]{0:T(128)S(1)}, s32[14]{0:T(128)}, u32[]{:S(2)}) copy-start(s32[14]{0:T(128)} %concatenate.3.ids) | copy-start | bytes 172
  46.0 18.0 %copy-start.7 = (bf16[2,128,512]{2,1,0:T(8,128)(2,1)}, bf16[2,128,512]{2,1,0:T(8,128)(2,1)S(1)}, u32[]{:S(2)}) copy-start(bf16[2,128,512]{2,1,0:T(8,128)(2,1)S(1)} %collective-permute-done.6.refs_4_) | copy-start | bytes 786436
  52.2 18.6 %copy-start.2 = (bf16[2,768,128]{2,1,0:T(8,128)(2,1)}, bf16[2,768,128]{2,1,0:T(8,128)(2,1)S(1)}, u32[]{:S(2)}) copy-start(bf16[2,768,128]{2,1,0:T(8,128)(2,1)S(1)} %collective-permute-done.11.refs_9_.refs_17_.refs_25_.refs_33_) | copy-start | bytes 1179652
  52.2 11.8 %copy-start.8 = (bf16[2,128,512]{2,1,0:T(8,128)(2,1)}, bf16[2,128,512]{2,1,0:T(8,128)(2,1)S(1)}, u32[]{:S(2)}) copy-start(bf16[2,128,512]{2,1,0:T(8,128)(2,1)S(1)} %collective-permute-done.8.refs_5_) | copy-start | bytes 786436
  60.6 10.7 %copy-start.3 = (bf16[2,768,128]{2,1,0:T(8,128)(2,1)}, bf16[2,768,128]{2,1,0:T(8,128)(2,1)S(1)}, u32[]{:S(2)}) copy-start(bf16[2,768,128]{2,1,0:T(8,128)(2,1)S(1)} %collective-permute-done.12.refs_10_.refs_18_.refs_26_.refs_34_) | copy-start | bytes 1179652
  60.6 1.1 %copy-start.18 = (f32[3,256,128]{2,1,0:T(8,128)S(1)}, f32[3,256,128]{2,1,0:T(8,128)}, u32[]{:S(2)}) copy-start(f32[3,256,128]{2,1,0:T(8,128)} %copy-done.17) | copy-start | bytes 1179652
  61.8 0.7 copy-start.20
  64.0 10.6 %copy-start.9 = (f32[8,128]{1,0:T(8,128)}, f32[8,128]{1,0:T(8,128)S(1)}, u32[]{:S(2)}) copy-start(f32[8,128]{1,0:T(8,128)S(1)} %get-tuple-element.31.refs_41_) | copy-start | bytes 12292
  64.0 27.7 %all-to-all-start.1 = ((bf16[8,256,128]{2,1,0:T(8,128)(2,1)}), bf16[8,256,128]{2,1,0:T(8,128)(2,1)S(1)}, u32[]{:S(2)}, u32[]{:S(2)}) async-start(bf16[8,256,128]{2,1,0:T(8,128)(2,1)} %get-tuple-element.30), calls=%async_computation.1 | async-start | bytes 1048576 | tf_op jit(solution)/shard_map/all_to_all | solution.py:638
  69.5 2.6 %collective-permute-start.13 = (bf16[2,768,128]{2,1,0:T(8,128)(2,1)S(1)}, bf16[2,768,128]{2,1,0:T(8,128)(2,1)S(1)}, u32[]{:S(2)}, u32[]{:S(2)}) collective-permute-start(bf16[2,768,128]{2,1,0:T(8,128)(2,1)S(1)} %get-tuple-element.25.refs_2_.refs_7_.refs_15_.refs_23_.refs_31_), channel_id=1, source_target_pairs={{0,1},{1,0},{2,3},{3,2},{4,5},{5,4},{6,7},{7,6},{8,9},{9,8},{10,11... | collective-permute-start | bytes 1179656 | tf_op jit(solution)/shard_map/ppermute | solution.py:635
  70.7 1.9 %collective-permute-start.15 = (bf16[2,768,128]{2,1,0:T(8,128)(2,1)S(1)}, bf16[2,768,128]{2,1,0:T(8,128)(2,1)S(1)}, u32[]{:S(2)}, u32[]{:S(2)}) collective-permute-start(bf16[2,768,128]{2,1,0:T(8,128)(2,1)S(1)} %collective-permute-done.11.refs_9_.refs_17_.refs_25_.refs_33_), channel_id=1, source_target_pairs={{0,1},{1,0},{2,3},{3,2},{4,5},{5,4},{6,7},{7,6},{8,9},{9,8},{10,11... | collective-permute-start | bytes 1179656 | tf_op jit(solution)/shard_map/ppermute | solution.py:635
  70.8 2.4 %collective-permute-start.14 = (bf16[2,768,128]{2,1,0:T(8,128)(2,1)S(1)}, bf16[2,768,128]{2,1,0:T(8,128)(2,1)S(1)}, u32[]{:S(2)}, u32[]{:S(2)}) collective-permute-start(bf16[2,768,128]{2,1,0:T(8,128)(2,1)S(1)} %collective-permute-done.10.refs_8_.refs_16_.refs_24_.refs_32_), channel_id=1, source_target_pairs={{0,1},{1,0},{2,3},{3,2},{4,5},{5,4},{6,7},{7,6},{8,9},{9,8},{10,11... | collective-permute-start | bytes 1179656 | tf_op jit(solution)/shard_map/ppermute | solution.py:635
  71.3 2.5 %collective-permute-start.16 = (bf16[2,768,128]{2,1,0:T(8,128)(2,1)S(1)}, bf16[2,768,128]{2,1,0:T(8,128)(2,1)S(1)}, u32[]{:S(2)}, u32[]{:S(2)}) collective-permute-start(bf16[2,768,128]{2,1,0:T(8,128)(2,1)S(1)} %collective-permute-done.12.refs_10_.refs_18_.refs_26_.refs_34_), channel_id=1, source_target_pairs={{0,1},{1,0},{2,3},{3,2},{4,5},{5,4},{6,7},{7,6},{8,9},{9,8},{10,11... | collective-permute-start | bytes 1179656 | tf_op jit(solution)/shard_map/ppermute | solution.py:635
  72.1 2.5 %copy-start.21 = (bf16[2,768,128]{2,1,0:T(8,128)(2,1)}, bf16[2,768,128]{2,1,0:T(8,128)(2,1)S(1)}, u32[]{:S(2)}) copy-start(bf16[2,768,128]{2,1,0:T(8,128)(2,1)S(1)} %collective-permute-done.13.refs_11_.refs_19_.refs_27_.refs_35_) | copy-start | bytes 1179652
  72.7 1.9 %copy-start.22 = (bf16[2,768,128]{2,1,0:T(8,128)(2,1)}, bf16[2,768,128]{2,1,0:T(8,128)(2,1)S(1)}, u32[]{:S(2)}) copy-start(bf16[2,768,128]{2,1,0:T(8,128)(2,1)S(1)} %collective-permute-done.15.refs_13_.refs_21_.refs_29_.refs_37_) | copy-start | bytes 1179652
  73.2 1.4 %copy-start.23 = (bf16[2,768,128]{2,1,0:T(8,128)(2,1)}, bf16[2,768,128]{2,1,0:T(8,128)(2,1)S(1)}, u32[]{:S(2)}) copy-start(bf16[2,768,128]{2,1,0:T(8,128)(2,1)S(1)} %collective-permute-done.14.refs_12_.refs_20_.refs_28_.refs_36_) | copy-start | bytes 1179652
  73.8 0.8 copy-start.24
  74.6 17.2 %copy-start.12 = (s32[14]{0:T(128)S(1)}, s32[14]{0:T(128)}, u32[]{:S(2)}) copy-start(s32[14]{0:T(128)} %concatenate.3.ids) | copy-start | bytes 172
  91.8 0.7 copy-start.16
  93.0 2.0 %copy-start.15 = (bf16[8,256,128]{2,1,0:T(8,128)(2,1)}, bf16[8,256,128]{2,1,0:T(8,128)(2,1)S(1)}, u32[]{:S(2)}) copy-start(bf16[8,256,128]{2,1,0:T(8,128)(2,1)S(1)} %copy.20.refs_3_) | copy-start | bytes 1572868
  93.0 2.0 %collective-permute-start.17 = (bf16[8,256,128]{2,1,0:T(8,128)(2,1)S(1)}, bf16[8,256,128]{2,1,0:T(8,128)(2,1)S(1)}, u32[]{:S(2)}, u32[]{:S(2)}) collective-permute-start(bf16[8,256,128]{2,1,0:T(8,128)(2,1)S(1)} %copy.20.refs_3_), channel_id=1, source_target_pairs={{0,1},{1,0},{2,3},{3,2},{4,5},{5,4},{6,7},{7,6},{8,9},{9,8},{10,11... | collective-permute-start | bytes 1572872 | tf_op jit(solution)/shard_map/ppermute | solution.py:635
  95.0 0.8 copy-start.27
